TPU v7x, 32 devices: a whole 2x2x4 slice. The times are simulated.
32 devices in a mesh: dp: 8 (over z, core), tensor: 4 (over y, x).
Axes of the slice: x: 2, y: 2, z: 4, core: 2. Of those that a mesh axis runs over, the one named last changes fastest.
Arguments:
- history: bfloat16 [9, 8192, 2048], P(None, 'dp', 'tensor'), may hold values from -6 to 6
- mix_in: float32 [36, 8192], P(None, 'dp'), may hold values from -2.5 to 2.5
- group_ids: int32 [8], P('dp'), may hold values from 0 to 3
- group_weight: float32 [4], replicated, may hold values from 0.3 to 3
- block_cotangent: bfloat16 [8192, 2048], P('dp', 'tensor'), may hold values from -6 to 6
- mix_cotangent: float32 [40, 8192], P(None, 'dp'), may hold values from -6 to 6
- qkv_weight: bfloat16 [3, 2048, 2048], P(None, 'dp', 'tensor'), may hold values from -0.125 to 0.125
- out_weight: bfloat16 [2048, 2048], P('tensor', 'dp'), may hold values from -2 to 2
- up_weight: bfloat16 [2048, 8192], P('dp', 'tensor'), may hold values from -0.125 to 0.125
- down_weight: bfloat16 [8192, 2048], P('tensor', 'dp'), may hold values from -0.0625 to 0.0625
- norm_gain: bfloat16 [4, 2048], P(None, 'dp'), may hold values from 0.5 to 1.5
- norm_bias: bfloat16 [4, 2048], P(None, 'dp'), may hold values from -2.5 to 2.5
- mix_weight: bfloat16 [2048, 40], P('dp'), may hold values from -0.125 to 0.125
- next_weight: bfloat16 [40, 40], replicated, may hold values from -1 to 1
Outputs:
- block_out: bfloat16 [8192, 2048], P('dp', 'tensor')
- next_mix: float32 [40, 8192], P(None, 'dp')
- history_grad: float32 [9, 8192, 2048], P(None, 'dp', 'tensor')
- mix_grad: float32 [36, 8192], P(None, 'dp')
- qkv_grad: float32 [3, 2048, 2048], P(None, 'dp', 'tensor')
- out_grad: float32 [2048, 2048], P('tensor', 'dp')
- up_grad: float32 [2048, 8192], P('dp', 'tensor')
- down_grad: float32 [8192, 2048], P('tensor', 'dp')
- gain_grad: float32 [4, 2048], P(None, 'dp')
- bias_grad: float32 [4, 2048], P(None, 'dp')
- mix_proj_grad: float32 [2048, 40], P('dp')
- next_proj_grad: float32 [40, 40], replicated
All inputs are finite; a program needn't handle non-finite values.
Results may differ from a plain program's by a relative error of at most 0.024.
Values may be sent and summed in bfloat16 or wider, within the bound.
No kernel may reach another device: no remote copies, remote signals or barrier semaphores. Data moves between devices by JAX's collectives and lax.ppermute only.
A program may use at most 256 MiB of HBM per device.

v0:
```python
import jax
import jax.numpy as jnp
from jax import lax
from jax.sharding import PartitionSpec as P

HEAD_DIM = 128
ROT = 32
STREAMS = 4
ENTRIES = 9
LENGTH = 1024


ln_eps = 1e-05
rms_eps = 1e-06
big_negative = -1e30
root_half = 0.7071067811865476
inv_root_tau = 0.3989422804014327


def gelu_exact(values):
    return jax.nn.gelu(values, approximate=False)


def gelu_slope(values):
    return (
        0.5 * (1.0 + lax.erf(values * root_half))
        + values * jnp.exp(-0.5 * values * values) * inv_root_tau
    )


def rotary_tables(count):
    places = (jnp.arange(count, dtype=jnp.int32) % LENGTH).astype(jnp.float32)
    freqs = jnp.power(10000.0, -jnp.arange(0, ROT, 2).astype(jnp.float32) / ROT)
    angles = places[:, None] * freqs[None, :]
    return (jnp.cos(angles), jnp.sin(angles))


def rotate(values, cosine, sine):
    halfway = ROT // 2
    first_half = values[..., :halfway]
    second_half = values[..., halfway:ROT]
    cos_wide = cosine[:, None, :]
    sin_wide = sine[:, None, :]
    return jnp.concatenate(
        [
            first_half * cos_wide - second_half * sin_wide,
            second_half * cos_wide + first_half * sin_wide,
            values[..., ROT:],
        ],
        axis=-1,
    )


def local_dot(left, right):
    return jnp.dot(left, right, preferred_element_type=jnp.float32)


def contract_rows(left, right):
    return lax.dot_general(
        left, right, (((0,), (0,)), ((), ())), preferred_element_type=jnp.float32
    )


def contract_cols(left, right):
    return lax.dot_general(
        left, right, (((1,), (1,)), ((), ())), preferred_element_type=jnp.float32
    )


def blocked_project(pieces, weight):
    count = pieces.shape[0]
    split = weight.reshape(count, pieces.shape[2], weight.shape[1])
    return jnp.einsum("ntw,nwk->tk", pieces, split, preferred_element_type=jnp.float32)


def blocked_rows(pieces, grad):
    whole = jnp.einsum("ntw,tk->nwk", pieces, grad, preferred_element_type=jnp.float32)
    return whole.reshape(pieces.shape[0] * pieces.shape[2], grad.shape[1])


def blocked_back(grad, weight, count):
    split = weight.reshape(count, weight.shape[0] // count, weight.shape[1])
    return jnp.einsum("tk,nwk->ntw", grad, split, preferred_element_type=jnp.float32)


def masked_scores(queries, key_heads, block_start, block_stop):
    score_scale = queries.shape[2] ** (-0.5)
    scores = (
        jnp.einsum(
            "qhd,khd->hqk",
            queries[block_start:block_stop],
            key_heads[:block_stop],
            preferred_element_type=jnp.float32,
        )
        * score_scale
    )
    allowed = (
        jnp.arange(block_stop)[None, :]
        <= (block_start + jnp.arange(block_stop - block_start))[:, None]
    )
    return jnp.where(allowed[None], scores, big_negative)


def attention_forward(queries, key_heads, value_heads):
    length = queries.shape[0]
    block_rows = min(512, length)
    outputs = []
    totals = []
    for number in range(length // block_rows):
        block_start = number * block_rows
        block_stop = block_start + block_rows
        scores = masked_scores(queries, key_heads, block_start, block_stop)
        summit = jnp.max(scores, axis=-1, keepdims=True)
        exponent = jnp.exp(scores - summit)
        partition = jnp.sum(exponent, axis=-1, keepdims=True)
        weights_low = (exponent / partition).astype(jnp.bfloat16)
        outputs.append(
            jnp.einsum(
                "hqk,khd->qhd",
                weights_low,
                value_heads[:block_stop],
                preferred_element_type=jnp.float32,
            )
        )
        totals.append(summit + jnp.log(partition))
    return (jnp.concatenate(outputs, 0).astype(jnp.bfloat16), totals)


def attention_backward(queries, key_heads, value_heads, grad_out, totals):
    length = queries.shape[0]
    block_rows = min(512, length)
    score_scale = queries.shape[2] ** (-0.5)
    key_grad = jnp.zeros(key_heads.shape, jnp.float32)
    value_grad = jnp.zeros(value_heads.shape, jnp.float32)
    query_grads = []
    for number in range(length // block_rows):
        block_start = number * block_rows
        block_stop = block_start + block_rows
        scores = masked_scores(queries, key_heads, block_start, block_stop)
        probs = jnp.exp(scores - totals[number])
        probs_low = probs.astype(jnp.bfloat16)
        grad_rows = grad_out[block_start:block_stop]
        prob_grad = jnp.einsum(
            "qhd,khd->hqk", grad_rows, value_heads[:block_stop], preferred_element_type=jnp.float32
        )
        value_grad = value_grad.at[:block_stop].add(
            jnp.einsum("hqk,qhd->khd", probs_low, grad_rows, preferred_element_type=jnp.float32)
        )
        center = jnp.sum(probs * prob_grad, axis=-1, keepdims=True)
        score_grad = (probs * (prob_grad - center)).astype(jnp.bfloat16)
        query_grads.append(
            jnp.einsum(
                "hqk,khd->qhd",
                score_grad,
                key_heads[:block_stop],
                preferred_element_type=jnp.float32,
            )
            * score_scale
        )
        key_grad = key_grad.at[:block_stop].add(
            jnp.einsum(
                "hqk,qhd->khd",
                score_grad,
                queries[block_start:block_stop],
                preferred_element_type=jnp.float32,
            )
            * score_scale
        )
    return (jnp.concatenate(query_grads, 0), key_grad, value_grad)


def per_device(
    history,
    mix_in,
    group_ids,
    group_weight,
    block_cotangent,
    mix_cotangent,
    qkv_weight,
    out_weight,
    up_weight,
    down_weight,
    norm_gain,
    norm_bias,
    mix_weight,
    next_weight,
):
    tensor_count = lax.axis_size("tensor")
    tensor_place = lax.axis_index("tensor")
    tokens = history.shape[1]
    width_own = history.shape[2]
    width_all = width_own * tensor_count
    column_start = tensor_place * width_own
    gathered = (
        lax.all_gather(qkv_weight, "dp", axis=1, tiled=True),
        lax.all_gather(out_weight, "dp", axis=1, tiled=True),
        lax.all_gather(up_weight, "dp", axis=0, tiled=True),
        lax.all_gather(down_weight, "dp", axis=1, tiled=True),
        lax.all_gather(norm_gain, "dp", axis=1, tiled=True),
        lax.all_gather(norm_bias, "dp", axis=1, tiled=True),
        lax.all_gather(mix_weight, "dp", axis=0, tiled=True),
    )
    qkv_full, out_full, up_full, down_full, gain_full, bias_full, mix_full = gathered
    heads_own = qkv_full.shape[2] // HEAD_DIM
    coeffs = mix_in.reshape(STREAMS, ENTRIES, tokens)
    streams_own = jnp.zeros((STREAMS, tokens, width_own), jnp.float32)
    for entry in range(ENTRIES):
        streams_own = (
            streams_own + coeffs[:, entry, :, None] * history[entry].astype(jnp.float32)[None]
        )
    gain_flat = gain_full.astype(jnp.float32)
    bias_flat = bias_full.astype(jnp.float32)
    gain_own = lax.dynamic_slice_in_dim(gain_flat, column_start, width_own, 1)[:, None, :]
    bias_own = lax.dynamic_slice_in_dim(bias_flat, column_start, width_own, 1)[:, None, :]
    residual_own = streams_own[3]
    total_sum, total_square = lax.psum(
        (
            jnp.sum(streams_own, axis=-1, keepdims=True),
            jnp.sum(streams_own * streams_own, axis=-1, keepdims=True),
        ),
        "tensor",
    )
    center = total_sum / width_all
    inv_spread = lax.rsqrt(total_square / width_all - center * center + ln_eps)
    unit_own = (streams_own - center) * inv_spread
    normed_own = (unit_own * gain_own + bias_own).astype(jnp.bfloat16)
    normed = lax.all_gather(normed_own[None], "tensor", axis=0, tiled=True)
    cosine, sine = rotary_tables(tokens)
    q_lin = blocked_project(normed[:, 0], qkv_full[0]).reshape(tokens, heads_own, HEAD_DIM)
    k_lin = blocked_project(normed[:, 1], qkv_full[1]).reshape(tokens, heads_own, HEAD_DIM)
    q_rot, query_pull = jax.vjp(lambda values: rotate(values, cosine, sine), q_lin)
    k_rot, key_pull = jax.vjp(lambda values: rotate(values, cosine, sine), k_lin)
    queries = q_rot.astype(jnp.bfloat16)
    key_heads = k_rot.astype(jnp.bfloat16)
    value_heads = (
        blocked_project(normed[:, 2], qkv_full[2])
        .astype(jnp.bfloat16)
        .reshape(tokens, heads_own, HEAD_DIM)
    )
    result, totals = attention_forward(queries, key_heads, value_heads)
    attended = result.reshape(tokens, heads_own * HEAD_DIM)
    hidden_pre = blocked_project(normed[:, 3], up_full)
    hidden = gelu_exact(hidden_pre).astype(jnp.bfloat16)
    partial_branch = local_dot(attended, out_full) + local_dot(hidden, down_full)
    branch_total = lax.psum(partial_branch.astype(jnp.bfloat16), "tensor").astype(jnp.float32)
    branch_own = lax.dynamic_slice_in_dim(branch_total, column_start, width_own, 1)
    block_own = (residual_own + branch_own).astype(jnp.bfloat16)
    block_full = lax.all_gather(block_own, "tensor", axis=1, tiled=True)
    block_wide = block_full.astype(jnp.float32)
    root_inv = lax.rsqrt(jnp.mean(block_wide * block_wide, axis=-1, keepdims=True) + rms_eps)
    scaled = (block_wide * root_inv).astype(jnp.bfloat16)
    pre_mix = local_dot(scaled, mix_full)
    mix_hidden = gelu_exact(pre_mix).astype(jnp.bfloat16)
    next_mix = local_dot(mix_hidden, next_weight).T
    member = (group_ids[:, None] == jnp.arange(group_weight.shape[0])[None, :]).astype(jnp.float32)
    seq_scale = jnp.sum(member * group_weight[None, :], axis=1)
    token_scale = jnp.repeat(seq_scale, LENGTH)
    mix_seed = (mix_cotangent * token_scale[None, :]).T.astype(jnp.bfloat16)
    next_part = contract_rows(mix_hidden, mix_seed)
    mix_hidden_grad = contract_cols(mix_seed, next_weight)
    pre_mix_grad = (mix_hidden_grad * gelu_slope(pre_mix)).astype(jnp.bfloat16)
    mix_part = contract_rows(scaled, pre_mix_grad)
    scaled_grad = contract_cols(pre_mix_grad, mix_full)
    block_mix_grad = (
        root_inv * scaled_grad
        - block_wide
        * root_inv
        * root_inv
        * root_inv
        * jnp.mean(scaled_grad * block_wide, axis=-1, keepdims=True)
    )
    block_grad_own = (
        lax.dynamic_slice_in_dim(block_mix_grad, column_start, width_own, 1)
        + block_cotangent.astype(jnp.float32) * token_scale[:, None]
    )
    branch_grad = lax.all_gather(block_grad_own.astype(jnp.bfloat16), "tensor", axis=1, tiled=True)
    down_part = contract_rows(hidden, branch_grad)
    hidden_grad = contract_cols(branch_grad, down_full)
    hidden_pre_grad = (hidden_grad * gelu_slope(hidden_pre)).astype(jnp.bfloat16)
    up_part = blocked_rows(normed[:, 3], hidden_pre_grad)
    normed_grad_mlp = blocked_back(hidden_pre_grad, up_full, tensor_count)
    out_part = contract_rows(attended, branch_grad)
    attended_grad = (
        contract_cols(branch_grad, out_full)
        .astype(jnp.bfloat16)
        .reshape(tokens, heads_own, HEAD_DIM)
    )
    q_grad, k_grad, v_grad = attention_backward(
        queries, key_heads, value_heads, attended_grad, totals
    )
    q_lin_grad = query_pull(q_grad)[0].astype(jnp.bfloat16).reshape(tokens, heads_own * HEAD_DIM)
    k_lin_grad = key_pull(k_grad)[0].astype(jnp.bfloat16).reshape(tokens, heads_own * HEAD_DIM)
    v_lin_grad = v_grad.astype(jnp.bfloat16).reshape(tokens, heads_own * HEAD_DIM)
    qkv_part = jnp.stack(
        [
            blocked_rows(normed[:, 0], q_lin_grad),
            blocked_rows(normed[:, 1], k_lin_grad),
            blocked_rows(normed[:, 2], v_lin_grad),
        ],
        0,
    )
    normed_grad = jnp.stack(
        [
            blocked_back(q_lin_grad, qkv_full[0], tensor_count),
            blocked_back(k_lin_grad, qkv_full[1], tensor_count),
            blocked_back(v_lin_grad, qkv_full[2], tensor_count),
            normed_grad_mlp,
        ],
        1,
    )
    normed_grad_own = lax.psum_scatter(
        normed_grad.astype(jnp.bfloat16), "tensor", scatter_dimension=0, tiled=True
    ).astype(jnp.float32)[0]
    gain_scaled = normed_grad_own * gain_own
    sum_plain, sum_unit = (
        lax.psum(
            jnp.sum(gain_scaled, axis=-1, keepdims=True).astype(jnp.bfloat16), "tensor"
        ).astype(jnp.float32),
        lax.psum(
            jnp.sum(gain_scaled * unit_own, axis=-1, keepdims=True).astype(jnp.bfloat16), "tensor"
        ).astype(jnp.float32),
    )
    stream_grad = inv_spread * (
        gain_scaled - sum_plain / width_all - unit_own * (sum_unit / width_all)
    )
    empty = jnp.zeros((STREAMS, width_all), jnp.float32)
    gain_part = lax.dynamic_update_slice_in_dim(
        empty, jnp.sum(normed_grad_own * unit_own, axis=1), column_start, 1
    )
    bias_part = lax.dynamic_update_slice_in_dim(
        empty, jnp.sum(normed_grad_own, axis=1), column_start, 1
    )
    stream_grad = stream_grad.at[3].add(block_grad_own)
    entry_grads = []
    entry_mixes = []
    for entry in range(ENTRIES):
        entry_grads.append(jnp.sum(coeffs[:, entry, :, None] * stream_grad, axis=0))
        entry_mixes.append(jnp.sum(stream_grad * history[entry].astype(jnp.float32)[None], axis=-1))
    history_grad = jnp.stack(entry_grads, 0)
    mix_partial = jnp.stack(entry_mixes, 1).reshape(STREAMS * ENTRIES, tokens)
    reduced = (
        lax.psum_scatter(
            qkv_part.astype(jnp.bfloat16), "dp", scatter_dimension=1, tiled=True
        ).astype(jnp.float32),
        lax.psum_scatter(
            out_part.astype(jnp.bfloat16), "dp", scatter_dimension=1, tiled=True
        ).astype(jnp.float32),
        lax.psum_scatter(
            up_part.astype(jnp.bfloat16), "dp", scatter_dimension=0, tiled=True
        ).astype(jnp.float32),
        lax.psum_scatter(
            down_part.astype(jnp.bfloat16), "dp", scatter_dimension=1, tiled=True
        ).astype(jnp.float32),
        lax.psum_scatter(
            gain_part.astype(jnp.bfloat16), "dp", scatter_dimension=1, tiled=True
        ).astype(jnp.float32),
        lax.psum_scatter(
            bias_part.astype(jnp.bfloat16), "dp", scatter_dimension=1, tiled=True
        ).astype(jnp.float32),
        lax.psum_scatter(
            mix_part.astype(jnp.bfloat16), "dp", scatter_dimension=0, tiled=True
        ).astype(jnp.float32),
    )
    qkv_grad, out_grad, up_grad, down_grad, gain_shard, bias_shard, mix_proj_grad = reduced
    mix_grad, gain_grad, bias_grad = (
        lax.psum(mix_partial.astype(jnp.bfloat16), "tensor").astype(jnp.float32),
        lax.psum(gain_shard.astype(jnp.bfloat16), "tensor").astype(jnp.float32),
        lax.psum(bias_shard.astype(jnp.bfloat16), "tensor").astype(jnp.float32),
    )
    next_proj_grad = lax.psum(next_part, "dp")
    return (
        block_own,
        next_mix,
        history_grad,
        mix_grad,
        qkv_grad,
        out_grad,
        up_grad,
        down_grad,
        gain_grad,
        bias_grad,
        mix_proj_grad,
        next_proj_grad,
    )


def solution(mesh):
    placed = (
        P(None, "dp", "tensor"),
        P(None, "dp"),
        P("dp"),
        P(),
        P("dp", "tensor"),
        P(None, "dp"),
        P(None, "dp", "tensor"),
        P("tensor", "dp"),
        P("dp", "tensor"),
        P("tensor", "dp"),
        P(None, "dp"),
        P(None, "dp"),
        P("dp", None),
        P(),
    )
    return jax.shard_map(
        per_device,
        mesh=mesh,
        in_specs=placed,
        out_specs=(
            P("dp", "tensor"),
            P(None, "dp"),
            P(None, "dp", "tensor"),
            P(None, "dp"),
            P(None, "dp", "tensor"),
            P("tensor", "dp"),
            P("dp", "tensor"),
            P("tensor", "dp"),
            P(None, "dp"),
            P(None, "dp"),
            P("dp", None),
            P(),
        ),
        check_vma=False,
    )
```

profile of v0, /device:TPU:0, one launch (start us, length us, event | category | flops | bytes accessed | tf_op | source)
XLA Modules:
  0.0 1370.8 jit_solution(10313408589853638833)
XLA Ops:
  9.1 14.5 %all_gather.30 = bf16[4,2048]{1,0:T(4,128)(2,1)S(1)} all-gather(bf16[4,256]{1,0:T(4,128)(2,1)} %param.38), channel_id=1, replica_groups=mesh['dp'=8,'tensor'=4] {'dp'}, dimensions={1}, use_global_device_ids=true | all-gather | bytes 18432 | tf_op jit(solution)/shard_map/all_gather | solution.py:199
  23.6 13.0 all_gather.31
  36.7 5.1 bitcast_convert_fusion.9
  41.9 10.4 fusion.125
  52.3 16.4 %all-reduce.9 = (f32[4,1024,1]{1,0,2:T(4,128)S(1)}, f32[4,1024,1]{1,0,2:T(4,128)S(1)}) all-reduce(f32[4,1024,1]{1,0,2:T(4,128)S(1)} %bitcast.391, f32[4,1024,1]{1,0,2:T(4,128)S(1)} %bitcast.390), channel_id=1, replica_groups=mesh['dp'=8,'tensor'=4] {'tensor'}, use_global_device_ids=true, to_apply=%region_3.0 | all-reduce | flops 8192 | bytes 65536 | tf_op jit(solution)/shard_map/psum | solution.py:216
  69.4 10.4 add_convert_fusion.1
  84.9 6.9 fusion.128
  94.5 4.2 copy.79
  98.7 137.1 %all-gather.8.cloned.1.call-done = bf16[4,4,1024,512]{3,2,0,1:T(8,128)(2,1)} async-done(((bf16[1,4,1024,512]{3,2,0,1:T(8,128)(2,1)}), bf16[4,4,1024,512]{3,2,0,1:T(8,128)(2,1)}) %all-gather.8.cloned.1.call-update) | async-done | bytes 16777232 | tf_op jit(solution)/shard_map/all_gather | solution.py:227
  235.7 5.4 fusion.81
  253.6 65.9 %all-gather.14.cloned.1.call-done = bf16[2048,2048]{1,0:T(8,128)(2,1)} async-done(((bf16[256,2048]{1,0:T(8,128)(2,1)}), bf16[2048,2048]{1,0:T(8,128)(2,1)}) %all-gather.14.cloned.1.call-update) | async-done | bytes 8388624 | tf_op jit(solution)/shard_map/all_gather | solution.py:197
  319.4 30.9 %fusion.11 = (bf16[1024,2048]{1,0:T(8,128)(2,1)}, f32[1024,2048,1]{1,0,2:T(8,128)}) fusion(bf16[4,512,2048]{2,1,0:T(8,128)(2,1)} %bitcast.396, bf16[4,4,1024,512]{3,2,0,1:T(8,128)(2,1)} %all-gather.8.cloned.1.call-done), kind=kOutput, calls=%fused_computation.19 | convolution fusion | flops 8726249472 | bytes 25165824 | tf_op jit(solution)/shard_map/ntw,nwk->tk/dot_general | solution.py:73
  358.6 43.4 %all-gather.16.cloned.1.call-done = bf16[2048,2048]{1,0:T(8,128)(2,1)} async-done(((bf16[2048,256]{1,0:T(8,128)(2,1)}), bf16[2048,2048]{1,0:T(8,128)(2,1)}) %all-gather.16.cloned.1.call-update) | async-done | bytes 8388624 | tf_op jit(solution)/shard_map/all_gather | solution.py:198
  401.9 15.0 %fusion.133 = f32[1024,2048]{1,0:T(8,128)} fusion(bf16[1024,2048]{1,0:T(8,128)(2,1)} %get-tuple-element.164, bf16[2048,2048]{1,0:T(8,128)(2,1)} %all-gather.16.cloned.1.call-done), kind=kOutput, calls=%fused_computation.290 | convolution fusion | flops 8589934592 | bytes 20971520 | tf_op jit(solution)/shard_map/dot_general | solution.py:55
  417.0 15.5 %all-gather.12.cloned.1.call-done = bf16[512,2048]{1,0:T(8,128)(2,1)} async-done(((bf16[512,256]{1,0:T(8,128)(2,1)}), bf16[512,2048]{1,0:T(8,128)(2,1)}) %all-gather.12.cloned.1.call-update) | async-done | bytes 2097168 | tf_op jit(solution)/shard_map/all_gather | solution.py:196
  432.4 8.6 add_convert_fusion
  441.1 103.0 %all-reduce.14.cloned.1.call-done = bf16[1024,2048]{1,0:T(8,128)(2,1)} async-done(((bf16[1024,2048]{1,0:T(8,128)(2,1)}), bf16[1024,2048]{1,0:T(8,128)(2,1)}) %all-reduce.14.cloned.1.call-update) | async-done | bytes 4194320 | tf_op jit(solution)/shard_map/psum | solution.py:245
  548.0 14.1 %all_gather.38 = bf16[2048,40]{0,1:T(8,128)(2,1)S(1)} all-gather(bf16[256,40]{0,1:T(8,128)(2,1)S(1)} %copy-done.97), channel_id=1, replica_groups=mesh['dp'=8,'tensor'=4] {'dp'}, dimensions={0}, use_global_device_ids=true | all-gather | bytes 184320 | tf_op jit(solution)/shard_map/all_gather | solution.py:201
  562.7 37.3 %all-gather.18.cloned.1.call-done = bf16[1024,2048]{1,0:T(8,128)(2,1)} async-done(((bf16[1024,512]{1,0:T(8,128)(2,1)}), bf16[1024,2048]{1,0:T(8,128)(2,1)}) %all-gather.18.cloned.1.call-update) | async-done | bytes 4194320 | tf_op jit(solution)/shard_map/all_gather | solution.py:248
  603.3 4.6 fusion.103
  614.6 51.9 %all-gather.20.cloned.1.call-done = bf16[1024,2048]{1,0:T(8,128)(2,1)} async-done(((bf16[1024,512]{1,0:T(8,128)(2,1)}), bf16[1024,2048]{1,0:T(8,128)(2,1)}) %all-gather.20.cloned.1.call-update) | async-done | bytes 4194320 | tf_op jit(solution)/shard_map/all_gather | solution.py:276
  666.5 5.4 convolution_convert_fusion.7
  686.1 17.2 %fusion.19 = bf16[1024,2048]{1,0:T(8,128)(2,1)} fusion(f32[1024,2048,1]{1,0,2:T(8,128)} %get-tuple-element.165, bf16[1024,2048]{1,0:T(8,128)(2,1)} %all-gather.20.cloned.1.call-done, bf16[2048,2048]{1,0:T(8,128)(2,1)} %all-gather.16.cloned.1.call-done), kind=kOutput, calls=%fused_computation.27 | convolution fusion | flops 8610906112 | bytes 25165824 | tf_op jit(solution)/shard_map/dot_general | solution.py:65
  703.2 12.7 convert_bitcast_fusion.1
  730.7 6.5 copy.96
  742.1 6.2 convolution_convert_fusion.2
  748.3 13.0 slice_bitcast_fusion
  761.4 6.5 copy.100
  767.9 6.4 copy.99
  774.3 6.5 copy.98
  780.7 4.9 fusion.58
  793.8 6.6 copy.101
  800.4 14.2 %convolution_convert_fusion.1 = bf16[2048,2048]{1,0:T(8,128)(2,1)} fusion(bf16[2048,1024]{1,0:T(8,128)(2,1)} %bitcast.370, bf16[1024,2048]{1,0:T(8,128)(2,1)} %fusion.19), kind=kOutput, calls=%fused_computation.81 | convolution fusion | flops 8594128896 | bytes 16777216 | tf_op jit(solution)/shard_map/ntw,tk->nwk/dot_general | solution.py:77
  814.7 14.2 %convolution_convert_fusion = bf16[2048,2048]{1,0:T(8,128)(2,1)} fusion(bf16[1024,2048]{1,0:T(8,128)(2,1)} %get-tuple-element.164, bf16[1024,2048]{1,0:T(8,128)(2,1)} %all-gather.20.cloned.1.call-done), kind=kOutput, calls=%fused_computation.80 | convolution fusion | flops 8594128896 | bytes 16777216 | tf_op jit(solution)/shard_map/dot_general | solution.py:59
  830.7 60.7 %reduce-scatter.29.cloned.1.call-done = bf16[1,4,1024,512]{3,2,1,0:T(8,128)(2,1)} async-done(((bf16[4,4,1024,512]{3,2,1,0:T(8,128)(2,1)}), bf16[1,4,1024,512]{3,2,1,0:T(8,128)(2,1)}) %reduce-scatter.29.cloned.1.call-update) | async-done | bytes 4194320
  891.3 7.7 fusion.8
  905.3 29.1 %psum.71 = f32[40,40]{1,0:T(8,128)} all-reduce(f32[40,40]{1,0:T(8,128)S(1)} %fusion.115), channel_id=1, replica_groups=mesh['dp'=8,'tensor'=4] {'dp'}, use_global_device_ids=true, to_apply=%region_49.50 | all-reduce | flops 1600 | bytes 12800 | tf_op jit(solution)/shard_map/psum | solution.py:370
  935.8 25.5 %reduce-scatter.17.cloned.1.call-done = bf16[512,256]{1,0:T(8,128)(2,1)} async-done(((bf16[512,2048]{1,0:T(8,128)(2,1)}), bf16[512,256]{1,0:T(8,128)(2,1)}) %reduce-scatter.17.cloned.1.call-update) | async-done | bytes 262160 | tf_op jit(solution)/shard_map/reduce_scatter | solution.py:345
  963.0 68.7 %reduce-scatter.15.cloned.1.call-done = bf16[3,256,512]{2,1,0:T(8,128)(2,1)} async-done(((bf16[3,2048,512]{2,1,0:T(8,128)(2,1)}), bf16[3,256,512]{2,1,0:T(8,128)(2,1)}) %reduce-scatter.15.cloned.1.call-update) | async-done | bytes 786448 | tf_op jit(solution)/shard_map/reduce_scatter | solution.py:342
  1034.2 87.8 %reduce-scatter.19.cloned.1.call-done = bf16[256,2048]{1,0:T(8,128)(2,1)} async-done(((bf16[2048,2048]{1,0:T(8,128)(2,1)}), bf16[256,2048]{1,0:T(8,128)(2,1)}) %reduce-scatter.19.cloned.1.call-update) | async-done | bytes 1048592 | tf_op jit(solution)/shard_map/reduce_scatter | solution.py:348
  1124.8 87.3 %reduce-scatter.21.cloned.1.call-done = bf16[2048,256]{1,0:T(8,128)(2,1)} async-done(((bf16[2048,2048]{1,0:T(8,128)(2,1)}), bf16[2048,256]{1,0:T(8,128)(2,1)}) %reduce-scatter.21.cloned.1.call-update) | async-done | bytes 1048592 | tf_op jit(solution)/shard_map/reduce_scatter | solution.py:351
  1214.9 29.3 %reduce-scatter.25.cloned.1.call-done = bf16[256,4]{1,0:T(8,128)(2,1)} async-done(((bf16[2048,4]{1,0:T(8,128)(2,1)}), bf16[256,4]{1,0:T(8,128)(2,1)}) %reduce-scatter.25.cloned.1.call-update) | async-done | bytes 2064
  1245.1 30.4 %reduce-scatter.27.cloned.1.call-done = bf16[256,4]{1,0:T(8,128)(2,1)} async-done(((bf16[2048,4]{1,0:T(8,128)(2,1)}), bf16[256,4]{1,0:T(8,128)(2,1)}) %reduce-scatter.27.cloned.1.call-update) | async-done | bytes 2064
  1276.4 16.3 %all-reduce.10 = (bf16[4,1024,1]{1,0,2:T(4,128)(2,1)S(1)}, bf16[4,1024,1]{1,0,2:T(4,128)(2,1)S(1)}, bf16[4,256]{1,0:T(4,128)(2,1)S(1)}, bf16[4,256]{1,0:T(4,128)(2,1)S(1)}) all-reduce(bf16[4,1024,1]{1,0,2:T(4,128)(2,1)S(1)} %bitcast.394, bf16[4,1024,1]{1,0,2:T(4,128)(2,1)S(1)} %bitcast.395, ...), channel_id=1, replica_groups=mesh['dp'=8,'tensor'=4] {'tensor'}, use_global_device_ids=true, to_apply=%region_18.19 | all-reduce | flops 10240 | bytes 40960 | tf_op jit(solution)/shard_map/psum | solution.py:319
  1292.9 8.6 fusion.6
  1302.2 21.7 %multiply_reduce_fusion = (bf16[4,1024]{1,0:T(4,128)(2,1)S(1)}, bf16[4,1024]{1,0:T(4,128)(2,1)S(1)}, bf16[4,1024]{1,0:T(4,128)(2,1)S(1)}, bf16[4,1024]{1,0:T(4,1...) fusion(f32[4,1024,512]{2,1,0:T(8,128)S(1)} %fusion.63, ...), kind=kLoop, calls=%fused_computation.35 | loop fusion | flops 70742016 | bytes 46358528 | tf_op jit(solution)/shard_map/reduce_sum | solution.py:338
  1331.8 6.8 copy-done.85
  1339.8 22.6 %all-reduce.16.cloned.1.call-done = bf16[36,1024]{1,0:T(8,128)(2,1)} async-done(((bf16[36,1024]{1,0:T(8,128)(2,1)}), bf16[36,1024]{1,0:T(8,128)(2,1)}) %all-reduce.16.cloned.1.call-update) | async-done | bytes 73744 | tf_op jit(solution)/shard_map/psum | solution.py:366
  (351 shorter events, 117.9 us)
Async XLA Ops:
  7.2 600.7 %copy-start = (bf16[40,40]{1,0:T(8,128)(2,1)S(1)}, bf16[40,40]{1,0:T(8,128)(2,1)}, u32[]{:S(2)}) copy-start(bf16[40,40]{1,0:T(8,128)(2,1)} %param.41) | copy-start | bytes 9604
  7.2 77.7 %all-gather.10.cloned.1.call-start = ((), (), s32[]{:S(2)}) async-start(), calls=%async_computation.9 | async-start | bytes 7077888 | tf_op jit(solution)/shard_map/all_gather | solution.py:195
  7.9 227.8 %all-gather.8.cloned.1.call-start = ((), (), s32[]{:S(2)}) async-start(), calls=%async_computation.8 | async-start | bytes 20971520 | tf_op jit(solution)/shard_map/all_gather | solution.py:227
  9.0 59.8 %copy-start.63 = (f32[4,1,1024]{2,0,1:T(4,128)}, f32[4,1,1024]{2,0,1:T(4,128)S(1)}, u32[]{:S(2)}) copy-start(f32[4,1,1024]{2,0,1:T(4,128)S(1)} %copy.145) | copy-start | bytes 49156
  36.6 32.3 %copy-start.65 = (f32[4,1024]{1,0:T(4,128)}, f32[4,1024]{1,0:T(4,128)S(1)}, u32[]{:S(2)}) copy-start(f32[4,1024]{1,0:T(4,128)S(1)} %get-tuple-element.177) | copy-start | bytes 49156
  36.6 32.3 %copy-start.67 = (f32[4,1024]{1,0:T(4,128)}, f32[4,1024]{1,0:T(4,128)S(1)}, u32[]{:S(2)}) copy-start(f32[4,1024]{1,0:T(4,128)S(1)} %get-tuple-element.178) | copy-start | bytes 49156
  36.6 32.3 %copy-start.69 = (f32[4,1024]{1,0:T(4,128)}, f32[4,1024]{1,0:T(4,128)S(1)}, u32[]{:S(2)}) copy-start(f32[4,1024]{1,0:T(4,128)S(1)} %get-tuple-element.179) | copy-start | bytes 49156
  36.6 32.3 %copy-start.71 = (f32[4,1024]{1,0:T(4,128)}, f32[4,1024]{1,0:T(4,128)S(1)}, u32[]{:S(2)}) copy-start(f32[4,1024]{1,0:T(4,128)S(1)} %get-tuple-element.180) | copy-start | bytes 49156
  36.6 32.3 %copy-start.73 = (f32[4,1024]{1,0:T(4,128)}, f32[4,1024]{1,0:T(4,128)S(1)}, u32[]{:S(2)}) copy-start(f32[4,1024]{1,0:T(4,128)S(1)} %get-tuple-element.181) | copy-start | bytes 49156
  36.7 32.3 %copy-start.75 = (f32[4,1024]{1,0:T(4,128)}, f32[4,1024]{1,0:T(4,128)S(1)}, u32[]{:S(2)}) copy-start(f32[4,1024]{1,0:T(4,128)S(1)} %get-tuple-element.182) | copy-start | bytes 49156
  36.7 32.2 %copy-start.77 = (f32[4,1024]{1,0:T(4,128)}, f32[4,1024]{1,0:T(4,128)S(1)}, u32[]{:S(2)}) copy-start(f32[4,1024]{1,0:T(4,128)S(1)} %get-tuple-element.183) | copy-start | bytes 49156
  36.7 32.2 %copy-start.79 = (f32[4,1024]{1,0:T(4,128)}, f32[4,1024]{1,0:T(4,128)S(1)}, u32[]{:S(2)}) copy-start(f32[4,1024]{1,0:T(4,128)S(1)} %get-tuple-element.184) | copy-start | bytes 49156
  41.8 10.5 copy-start.6
  41.8 10.5 copy-start.8
  41.8 10.5 copy-start.10
  41.8 10.5 copy-start.12
  41.9 27.1 %copy-start.4 = (f32[1024,512]{1,0:T(8,128)}, f32[1024,512]{1,0:T(8,128)S(1)}, u32[]{:S(2)}) copy-start(f32[1024,512]{1,0:T(8,128)S(1)} %get-tuple-element.126) | copy-start | bytes 6291460
  79.8 239.6 %all-gather.14.cloned.1.call-start = ((), (), s32[]{:S(2)}) async-start(), calls=%async_computation.11 | async-start | bytes 9437184 | tf_op jit(solution)/shard_map/all_gather | solution.py:197
  80.6 321.4 %all-gather.16.cloned.1.call-start = ((), (), s32[]{:S(2)}) async-start(), calls=%async_computation.12 | async-start | bytes 9437184 | tf_op jit(solution)/shard_map/all_gather | solution.py:198
  81.1 351.3 %all-gather.12.cloned.1.call-start = ((), (), s32[]{:S(2)}) async-start(), calls=%async_computation.10 | async-start | bytes 2359296 | tf_op jit(solution)/shard_map/all_gather | solution.py:196
  81.7 462.4 %all-reduce.14.cloned.1.call-start = ((), (), s32[]{:S(2)}) async-start(), calls=%async_computation.13 | async-start | bytes 8388608 | tf_op jit(solution)/shard_map/psum | solution.py:245
  91.8 149.3 %copy-start.28 = (bf16[1,2048,512]{2,1,0:T(8,128)(2,1)}, bf16[1,2048,512]{2,1,0:T(8,128)(2,1)S(1)}, u32[]{:S(2)}) copy-start(bf16[1,2048,512]{2,1,0:T(8,128)(2,1)S(1)} %get-tuple-element.136) | copy-start | bytes 6291460
  249.5 100.8 %copy-start.57 = (bf16[1024,4,16]{0,2,1:T(8,128)(2,1)}, bf16[1024,4,16]{0,2,1:T(8,128)(2,1)S(1)}, u32[]{:S(2)}) copy-start(bf16[1024,4,16]{0,2,1:T(8,128)(2,1)S(1)} %get-tuple-element.142) | copy-start | bytes 393220
  249.5 100.8 %copy-start.59 = (bf16[1024,4,16]{0,2,1:T(8,128)(2,1)}, bf16[1024,4,16]{0,2,1:T(8,128)(2,1)S(1)}, u32[]{:S(2)}) copy-start(bf16[1024,4,16]{0,2,1:T(8,128)(2,1)S(1)} %get-tuple-element.143) | copy-start | bytes 393220
  253.6 178.9 %copy-start.99 = (bf16[4,128,512]{2,1,0:T(8,128)(2,1)}, bf16[4,128,512]{2,1,0:T(8,128)(2,1)S(1)}, u32[]{:S(2)}) copy-start(bf16[4,128,512]{2,1,0:T(8,128)(2,1)S(1)} %fusion.94) | copy-start | bytes 1572868
  319.4 30.9 %copy-start.36 = (bf16[1024,4,96]{0,2,1:T(8,128)(2,1)S(1)}, bf16[1024,4,96]{0,2,1:T(8,128)(2,1)}, u32[]{:S(2)}) copy-start(bf16[1024,4,96]{0,2,1:T(8,128)(2,1)} %copy-done.35) | copy-start | bytes 2359300
  319.4 31.0 %copy-start.56 = (pred[512,1024]{1,0:T(8,128)(4,1)S(1)}, pred[512,1024]{1,0:T(8,128)(4,1)}, u32[]{:S(2)}) copy-start(pred[512,1024]{1,0:T(8,128)(4,1)} %iota_compare_fusion) | copy-start | bytes 1572868
  441.0 107.0 %copy-start.97 = (bf16[256,40]{0,1:T(8,128)(2,1)S(1)}, bf16[256,40]{0,1:T(8,128)(2,1)}, u32[]{:S(2)}) copy-start(bf16[256,40]{0,1:T(8,128)(2,1)} %param.40) | copy-start | bytes 61444
  441.0 121.1 %copy-start.98 = (f32[4]{0:T(128)S(1)}, f32[4]{0:T(128)}, u32[]{:S(2)}) copy-start(f32[4]{0:T(128)} %param.31) | copy-start | bytes 52
  441.0 159.0 %all-gather.18.cloned.1.call-start = ((), (), s32[]{:S(2)}) async-start(), calls=%async_computation.14 | async-start | bytes 5242880 | tf_op jit(solution)/shard_map/all_gather | solution.py:248
  547.3 119.2 %all-gather.20.cloned.1.call-start = ((), (), s32[]{:S(2)}) async-start(), calls=%async_computation.15 | async-start | bytes 5242880 | tf_op jit(solution)/shard_map/all_gather | solution.py:276
  562.7 45.1 %copy-start.86 = (f32[40,1024]{1,0:T(8,128)S(1)}, f32[40,1024]{1,0:T(8,128)}, u32[]{:S(2)}) copy-start(f32[40,1024]{1,0:T(8,128)} %param.33) | copy-start | bytes 491524
  613.8 277.5 %reduce-scatter.29.cloned.1.call-start = ((), (), s32[]{:S(2)}) async-start(), calls=%async_computation.24 | async-start | bytes 20971520
  614.0 59.8 %copy-start.90 = (f32[4,512]{1,0:T(4,128)}, f32[4,512]{1,0:T(4,128)S(1)}, u32[]{:S(2)}) copy-start(f32[4,512]{1,0:T(4,128)S(1)} %log_add_fusion.1) | copy-start | bytes 24580
  703.2 12.7 copy-start.33
  703.2 12.8 copy-start.89
  737.3 197.1 %reduce-scatter.23.cloned.1.call-start = ((), (), s32[]{:S(2)}) async-start(), calls=%async_computation.21 | async-start | bytes 184320 | tf_op jit(solution)/shard_map/reduce_scatter | solution.py:360
  742.0 219.2 %reduce-scatter.17.cloned.1.call-start = ((), (), s32[]{:S(2)}) async-start(), calls=%async_computation.18 | async-start | bytes 2359296 | tf_op jit(solution)/shard_map/reduce_scatter | solution.py:345
  748.3 283.4 %reduce-scatter.15.cloned.1.call-start = ((), (), s32[]{:S(2)}) async-start(), calls=%async_computation.17 | async-start | bytes 7077888 | tf_op jit(solution)/shard_map/reduce_scatter | solution.py:342
  767.9 12.9 copy-start.45
  793.7 328.3 %reduce-scatter.19.cloned.1.call-start = ((), (), s32[]{:S(2)}) async-start(), calls=%async_computation.19 | async-start | bytes 9437184 | tf_op jit(solution)/shard_map/reduce_scatter | solution.py:348
  814.6 397.5 %reduce-scatter.21.cloned.1.call-start = ((), (), s32[]{:S(2)}) async-start(), calls=%async_computation.20 | async-start | bytes 9437184 | tf_op jit(solution)/shard_map/reduce_scatter | solution.py:351
  828.9 62.4 %copy-start.82 = (f32[4,1024]{1,0:T(4,128)S(1)}, f32[4,1024]{1,0:T(4,128)}, u32[]{:S(2)}) copy-start(f32[4,1024]{1,0:T(4,128)} %copy-done.81) | copy-start | bytes 49156
  828.9 62.4 %copy-start.84 = (f32[4,1024]{1,0:T(4,128)S(1)}, f32[4,1024]{1,0:T(4,128)}, u32[]{:S(2)}) copy-start(f32[4,1024]{1,0:T(4,128)} %copy-done.83) | copy-start | bytes 49156
  828.9 62.4 %copy-start.92 = (f32[4,512]{1,0:T(4,128)S(1)}, f32[4,512]{1,0:T(4,128)}, u32[]{:S(2)}) copy-start(f32[4,512]{1,0:T(4,128)} %copy-done.91) | copy-start | bytes 24580
  828.9 415.2 %reduce-scatter.25.cloned.1.call-start = ((), (), s32[]{:S(2)}) async-start(), calls=%async_computation.22 | async-start | bytes 589824
  900.2 375.3 %reduce-scatter.27.cloned.1.call-start = ((), (), s32[]{:S(2)}) async-start(), calls=%async_computation.23 | async-start | bytes 589824
  904.4 458.0 %all-reduce.16.cloned.1.call-start = ((), (), s32[]{:S(2)}) async-start(), calls=%async_computation.16 | async-start | bytes 163840 | tf_op jit(solution)/shard_map/psum | solution.py:366
  (73 other events, 359.4 us)
Sparse Core Ops, SparseCore 0:
  9.6 67.4 all-gather.9
  79.9 155.7 all-gather.7
  237.3 82.0 all-gather.13
  320.9 81.0 all-gather.15
  403.4 29.0 all-gather.11
  441.1 102.8 all-reduce.13
  547.4 52.5 all-gather.17
  613.9 52.5 all-gather.19
  737.4 153.8 reduce-scatter.28
  894.1 30.2 reduce-scatter.22
  927.3 33.9 reduce-scatter.16
  963.4 68.2 reduce-scatter.14
  1034.0 87.9 reduce-scatter.18
  1124.2 87.9 reduce-scatter.20
  1214.8 29.2 reduce-scatter.24
  1246.4 29.0 reduce-scatter.26
  1324.9 37.4 all-reduce.15
where the time goes:
time: 1380 us; the launch traced here: 1370 us
  waiting for transfers between devices  869 us (63%)
  matrix products  183 us (13%)
  other arithmetic  108 us (8%)
  blocking collectives  103 us (7%)
  local copies, waits for them, and re-layouts  89.2 us (6%)
  between operations  16.6 us (1%)
    all_gather x1, waiting for transfers between devices, per_device(): normed = lax.all_gather(normed_own[None], 'tensor', axis=0, tiled=True)  137 us
    unnamed x20, waiting for transfers between devices  123 us
    psum x1, waiting for transfers between devices, per_device(): lax.psum(partial_branch.astype(jnp.bfloat16), 'tensor').astype(jnp.float32)  103 us
    reduce_scatter x1, waiting for transfers between devices, per_device(): lax.psum_scatter(up_part.astype(jnp.bfloat16), 'dp', scatter_dimension=0,...  87.8 us
    reduce_scatter x1, waiting for transfers between devices, per_device(): lax.psum_scatter(down_part.astype(jnp.bfloat16), 'dp', scatter_dimension=...  87.3 us
    reduce_scatter x1, waiting for transfers between devices, per_device(): lax.psum_scatter(qkv_part.astype(jnp.bfloat16), 'dp', scatter_dimension=1...  68.7 us
    all_gather x1, waiting for transfers between devices, per_device(): lax.all_gather(up_weight, 'dp', axis=0, tiled=True)  65.9 us
    all_gather x1, waiting for transfers between devices, per_device(): lax.all_gather(block_grad_own.astype(jnp.bfloat16), 'tensor', axis=1, til...  51.9 us
  transfers between devices with their start and end apart: 17, of which 15 were waited for; matrix products, arithmetic and copies ran while one was open for 17% of the time, Pallas kernels for 0%

commit v1 on v0

--- a/solution.py
+++ b/solution.py
@@ -65,22 +65,6 @@
     return lax.dot_general(
         left, right, (((1,), (1,)), ((), ())), preferred_element_type=jnp.float32
     )
-
-
-def blocked_project(pieces, weight):
-    count = pieces.shape[0]
-    split = weight.reshape(count, pieces.shape[2], weight.shape[1])
-    return jnp.einsum("ntw,nwk->tk", pieces, split, preferred_element_type=jnp.float32)
-
-
-def blocked_rows(pieces, grad):
-    whole = jnp.einsum("ntw,tk->nwk", pieces, grad, preferred_element_type=jnp.float32)
-    return whole.reshape(pieces.shape[0] * pieces.shape[2], grad.shape[1])
-
-
-def blocked_back(grad, weight, count):
-    split = weight.reshape(count, weight.shape[0] // count, weight.shape[1])
-    return jnp.einsum("tk,nwk->ntw", grad, split, preferred_element_type=jnp.float32)
 
 
 def masked_scores(queries, key_heads, block_start, block_stop):
@@ -169,6 +153,75 @@
     return (jnp.concatenate(query_grads, 0), key_grad, value_grad)
 
 
+def swap(values, axis, bit):
+    count = lax.axis_size(axis)
+    return lax.ppermute(values, axis, [(i, i ^ bit) for i in range(count)])
+
+
+def axis_bits(axis):
+    count = lax.axis_size(axis)
+    return [1 << b for b in range(count.bit_length() - 1)]
+
+
+def butterfly_sum(values, axis):
+    for bit in axis_bits(axis):
+        values = values + swap(values, axis, bit)
+    return values
+
+
+def gather_pieces(own):
+    bits = axis_bits("tensor")
+    half = own.shape[0] // 2
+    if len(bits) == 2:
+        one = swap(own, "tensor", 1)
+        two = swap(own, "tensor", 2)
+        top = swap(one[:half], "tensor", 2)
+        bottom = swap(two[half:], "tensor", 1)
+        return {0: own, 1: one, 2: two, 3: jnp.concatenate([top, bottom], 0)}
+    halves = []
+    for part, order in ((own[:half], bits), (own[half:], bits[::-1])):
+        held = {0: part}
+        for bit in order:
+            keys = list(held)
+            got = swap(jnp.stack([held[k] for k in keys]), "tensor", bit)
+            for number, k in enumerate(keys):
+                held[k ^ bit] = got[number]
+        halves.append(held)
+    return {k: jnp.concatenate([halves[0][k], halves[1][k]], 0) for k in halves[0]}
+
+
+def gather_columns(own):
+    place = lax.axis_index("tensor")
+    width = own.shape[1]
+    pieces = gather_pieces(own)
+    whole = jnp.zeros((own.shape[0], width * len(pieces)), own.dtype)
+    for key, piece in pieces.items():
+        whole = lax.dynamic_update_slice_in_dim(whole, piece, (place ^ key) * width, 1)
+    return whole
+
+
+def scatter_columns(partial):
+    place = lax.axis_index("tensor")
+    count = lax.axis_size("tensor")
+    width = partial.shape[1] // count
+    half = partial.shape[0] // 2
+    bits = axis_bits("tensor")
+    sums = []
+    for number, order in enumerate((bits, bits[::-1])):
+        rows = partial[number * half : (number + 1) * half]
+        held = {
+            k: lax.dynamic_slice_in_dim(rows, (place ^ k) * width, width, 1) for k in range(count)
+        }
+        for bit in order:
+            sent = [k for k in held if k & bit]
+            got = swap(jnp.stack([held[k] for k in sent]).astype(jnp.bfloat16), "tensor", bit)
+            for spot, k in enumerate(sent):
+                held[k ^ bit] = held[k ^ bit].astype(jnp.float32) + got[spot].astype(jnp.float32)
+                del held[k]
+        sums.append(held[0])
+    return jnp.concatenate(sums, 0)
+
+
 def per_device(
     history,
     mix_in,
@@ -187,20 +240,24 @@
 ):
     tensor_count = lax.axis_size("tensor")
     tensor_place = lax.axis_index("tensor")
+    dp_place = lax.axis_index("dp")
     tokens = history.shape[1]
     width_own = history.shape[2]
     width_all = width_own * tensor_count
     column_start = tensor_place * width_own
-    gathered = (
-        lax.all_gather(qkv_weight, "dp", axis=1, tiled=True),
-        lax.all_gather(out_weight, "dp", axis=1, tiled=True),
-        lax.all_gather(up_weight, "dp", axis=0, tiled=True),
-        lax.all_gather(down_weight, "dp", axis=1, tiled=True),
-        lax.all_gather(norm_gain, "dp", axis=1, tiled=True),
-        lax.all_gather(norm_bias, "dp", axis=1, tiled=True),
-        lax.all_gather(mix_weight, "dp", axis=0, tiled=True),
-    )
-    qkv_full, out_full, up_full, down_full, gain_full, bias_full, mix_full = gathered
+    share = norm_gain.shape[1]
+    mix_out = mix_weight.shape[1]
+
+    cot_full = gather_columns(block_cotangent)
+    smalls = jnp.concatenate([norm_gain.T, norm_bias.T, mix_weight], 1)
+    smalls = lax.all_gather(smalls, "dp", axis=0, tiled=True)
+    gain_flat = smalls[:, :STREAMS].T.astype(jnp.float32)
+    bias_flat = smalls[:, STREAMS : 2 * STREAMS].T.astype(jnp.float32)
+    mix_full = smalls[:, 2 * STREAMS :]
+    qkv_full = lax.all_gather(qkv_weight, "dp", axis=1, tiled=True)
+    up_full = lax.all_gather(up_weight, "dp", axis=0, tiled=True)
+    down_full = lax.all_gather(down_weight, "dp", axis=1, tiled=True)
+    out_full = lax.all_gather(out_weight, "dp", axis=1, tiled=True)
     heads_own = qkv_full.shape[2] // HEAD_DIM
     coeffs = mix_in.reshape(STREAMS, ENTRIES, tokens)
     streams_own = jnp.zeros((STREAMS, tokens, width_own), jnp.float32)
@@ -208,44 +265,40 @@
         streams_own = (
             streams_own + coeffs[:, entry, :, None] * history[entry].astype(jnp.float32)[None]
         )
-    gain_flat = gain_full.astype(jnp.float32)
-    bias_flat = bias_full.astype(jnp.float32)
     gain_own = lax.dynamic_slice_in_dim(gain_flat, column_start, width_own, 1)[:, None, :]
     bias_own = lax.dynamic_slice_in_dim(bias_flat, column_start, width_own, 1)[:, None, :]
     residual_own = streams_own[3]
-    total_sum, total_square = lax.psum(
-        (
-            jnp.sum(streams_own, axis=-1, keepdims=True),
-            jnp.sum(streams_own * streams_own, axis=-1, keepdims=True),
+    stats = butterfly_sum(
+        jnp.concatenate(
+            [jnp.sum(streams_own, axis=-1), jnp.sum(streams_own * streams_own, axis=-1)], 0
         ),
         "tensor",
     )
-    center = total_sum / width_all
-    inv_spread = lax.rsqrt(total_square / width_all - center * center + ln_eps)
+    center = stats[:STREAMS, :, None] / width_all
+    inv_spread = lax.rsqrt(stats[STREAMS:, :, None] / width_all - center * center + ln_eps)
     unit_own = (streams_own - center) * inv_spread
     normed_own = (unit_own * gain_own + bias_own).astype(jnp.bfloat16)
-    normed = lax.all_gather(normed_own[None], "tensor", axis=0, tiled=True)
+    normed = [gather_columns(normed_own[c]) for c in range(STREAMS)]
     cosine, sine = rotary_tables(tokens)
-    q_lin = blocked_project(normed[:, 0], qkv_full[0]).reshape(tokens, heads_own, HEAD_DIM)
-    k_lin = blocked_project(normed[:, 1], qkv_full[1]).reshape(tokens, heads_own, HEAD_DIM)
+    q_lin = local_dot(normed[0], qkv_full[0]).reshape(tokens, heads_own, HEAD_DIM)
+    k_lin = local_dot(normed[1], qkv_full[1]).reshape(tokens, heads_own, HEAD_DIM)
     q_rot, query_pull = jax.vjp(lambda values: rotate(values, cosine, sine), q_lin)
     k_rot, key_pull = jax.vjp(lambda values: rotate(values, cosine, sine), k_lin)
     queries = q_rot.astype(jnp.bfloat16)
     key_heads = k_rot.astype(jnp.bfloat16)
     value_heads = (
-        blocked_project(normed[:, 2], qkv_full[2])
+        local_dot(normed[2], qkv_full[2])
         .astype(jnp.bfloat16)
         .reshape(tokens, heads_own, HEAD_DIM)
     )
     result, totals = attention_forward(queries, key_heads, value_heads)
     attended = result.reshape(tokens, heads_own * HEAD_DIM)
-    hidden_pre = blocked_project(normed[:, 3], up_full)
+    hidden_pre = local_dot(normed[3], up_full)
     hidden = gelu_exact(hidden_pre).astype(jnp.bfloat16)
     partial_branch = local_dot(attended, out_full) + local_dot(hidden, down_full)
-    branch_total = lax.psum(partial_branch.astype(jnp.bfloat16), "tensor").astype(jnp.float32)
-    branch_own = lax.dynamic_slice_in_dim(branch_total, column_start, width_own, 1)
+    branch_own = scatter_columns(partial_branch.astype(jnp.bfloat16))
     block_own = (residual_own + branch_own).astype(jnp.bfloat16)
-    block_full = lax.all_gather(block_own, "tensor", axis=1, tiled=True)
+    block_full = gather_columns(block_own)
     block_wide = block_full.astype(jnp.float32)
     root_inv = lax.rsqrt(jnp.mean(block_wide * block_wide, axis=-1, keepdims=True) + rms_eps)
     scaled = (block_wide * root_inv).astype(jnp.bfloat16)
@@ -259,27 +312,37 @@
     next_part = contract_rows(mix_hidden, mix_seed)
     mix_hidden_grad = contract_cols(mix_seed, next_weight)
     pre_mix_grad = (mix_hidden_grad * gelu_slope(pre_mix)).astype(jnp.bfloat16)
-    mix_part = contract_rows(scaled, pre_mix_grad)
+    mix_part = contract_rows(pre_mix_grad, scaled)
     scaled_grad = contract_cols(pre_mix_grad, mix_full)
-    block_mix_grad = (
+    block_grad = (
         root_inv * scaled_grad
         - block_wide
         * root_inv
         * root_inv
         * root_inv
         * jnp.mean(scaled_grad * block_wide, axis=-1, keepdims=True)
-    )
-    block_grad_own = (
-        lax.dynamic_slice_in_dim(block_mix_grad, column_start, width_own, 1)
-        + block_cotangent.astype(jnp.float32) * token_scale[:, None]
-    )
-    branch_grad = lax.all_gather(block_grad_own.astype(jnp.bfloat16), "tensor", axis=1, tiled=True)
+        + cot_full.astype(jnp.float32) * token_scale[:, None]
+    )
+    branch_grad = block_grad.astype(jnp.bfloat16)
+    block_grad_own = lax.dynamic_slice_in_dim(block_grad, column_start, width_own, 1)
     down_part = contract_rows(hidden, branch_grad)
+    down_grad = lax.psum_scatter(
+        down_part.astype(jnp.bfloat16), "dp", scatter_dimension=1, tiled=True
+    ).astype(jnp.float32)
     hidden_grad = contract_cols(branch_grad, down_full)
     hidden_pre_grad = (hidden_grad * gelu_slope(hidden_pre)).astype(jnp.bfloat16)
-    up_part = blocked_rows(normed[:, 3], hidden_pre_grad)
-    normed_grad_mlp = blocked_back(hidden_pre_grad, up_full, tensor_count)
+    up_part = contract_rows(normed[3], hidden_pre_grad)
+    up_grad = lax.psum_scatter(
+        up_part.astype(jnp.bfloat16), "dp", scatter_dimension=0, tiled=True
+    ).astype(jnp.float32)
+    normed_grads = [None] * STREAMS
+    normed_grads[3] = scatter_columns(
+        contract_cols(hidden_pre_grad, up_full).astype(jnp.bfloat16)
+    )
     out_part = contract_rows(attended, branch_grad)
+    out_grad = lax.psum_scatter(
+        out_part.astype(jnp.bfloat16), "dp", scatter_dimension=1, tiled=True
+    ).astype(jnp.float32)
     attended_grad = (
         contract_cols(branch_grad, out_full)
         .astype(jnp.bfloat16)
@@ -288,47 +351,31 @@
     q_grad, k_grad, v_grad = attention_backward(
         queries, key_heads, value_heads, attended_grad, totals
     )
-    q_lin_grad = query_pull(q_grad)[0].astype(jnp.bfloat16).reshape(tokens, heads_own * HEAD_DIM)
-    k_lin_grad = key_pull(k_grad)[0].astype(jnp.bfloat16).reshape(tokens, heads_own * HEAD_DIM)
-    v_lin_grad = v_grad.astype(jnp.bfloat16).reshape(tokens, heads_own * HEAD_DIM)
+    lin_grads = [
+        query_pull(q_grad)[0].astype(jnp.bfloat16).reshape(tokens, heads_own * HEAD_DIM),
+        key_pull(k_grad)[0].astype(jnp.bfloat16).reshape(tokens, heads_own * HEAD_DIM),
+        v_grad.astype(jnp.bfloat16).reshape(tokens, heads_own * HEAD_DIM),
+    ]
+    for c in range(3):
+        normed_grads[c] = scatter_columns(
+            contract_cols(lin_grads[c], qkv_full[c]).astype(jnp.bfloat16)
+        )
     qkv_part = jnp.stack(
-        [
-            blocked_rows(normed[:, 0], q_lin_grad),
-            blocked_rows(normed[:, 1], k_lin_grad),
-            blocked_rows(normed[:, 2], v_lin_grad),
-        ],
-        0,
-    )
-    normed_grad = jnp.stack(
-        [
-            blocked_back(q_lin_grad, qkv_full[0], tensor_count),
-            blocked_back(k_lin_grad, qkv_full[1], tensor_count),
-            blocked_back(v_lin_grad, qkv_full[2], tensor_count),
-            normed_grad_mlp,
-        ],
-        1,
-    )
-    normed_grad_own = lax.psum_scatter(
-        normed_grad.astype(jnp.bfloat16), "tensor", scatter_dimension=0, tiled=True
-    ).astype(jnp.float32)[0]
+        [contract_rows(normed[c], lin_grads[c]).astype(jnp.bfloat16) for c in range(3)], 0
+    )
+    qkv_grad = lax.psum_scatter(qkv_part, "dp", scatter_dimension=1, tiled=True).astype(jnp.float32)
+    normed_grad_own = jnp.stack(normed_grads, 0)
     gain_scaled = normed_grad_own * gain_own
-    sum_plain, sum_unit = (
-        lax.psum(
-            jnp.sum(gain_scaled, axis=-1, keepdims=True).astype(jnp.bfloat16), "tensor"
-        ).astype(jnp.float32),
-        lax.psum(
-            jnp.sum(gain_scaled * unit_own, axis=-1, keepdims=True).astype(jnp.bfloat16), "tensor"
-        ).astype(jnp.float32),
-    )
+    sums = butterfly_sum(
+        jnp.concatenate(
+            [jnp.sum(gain_scaled, axis=-1), jnp.sum(gain_scaled * unit_own, axis=-1)], 0
+        ),
+        "tensor",
+    )
+    sum_plain = sums[:STREAMS, :, None]
+    sum_unit = sums[STREAMS:, :, None]
     stream_grad = inv_spread * (
         gain_scaled - sum_plain / width_all - unit_own * (sum_unit / width_all)
-    )
-    empty = jnp.zeros((STREAMS, width_all), jnp.float32)
-    gain_part = lax.dynamic_update_slice_in_dim(
-        empty, jnp.sum(normed_grad_own * unit_own, axis=1), column_start, 1
-    )
-    bias_part = lax.dynamic_update_slice_in_dim(
-        empty, jnp.sum(normed_grad_own, axis=1), column_start, 1
     )
     stream_grad = stream_grad.at[3].add(block_grad_own)
     entry_grads = []
@@ -337,37 +384,22 @@
         entry_grads.append(jnp.sum(coeffs[:, entry, :, None] * stream_grad, axis=0))
         entry_mixes.append(jnp.sum(stream_grad * history[entry].astype(jnp.float32)[None], axis=-1))
     history_grad = jnp.stack(entry_grads, 0)
-    mix_partial = jnp.stack(entry_mixes, 1).reshape(STREAMS * ENTRIES, tokens)
-    reduced = (
-        lax.psum_scatter(
-            qkv_part.astype(jnp.bfloat16), "dp", scatter_dimension=1, tiled=True
-        ).astype(jnp.float32),
-        lax.psum_scatter(
-            out_part.astype(jnp.bfloat16), "dp", scatter_dimension=1, tiled=True
-        ).astype(jnp.float32),
-        lax.psum_scatter(
-            up_part.astype(jnp.bfloat16), "dp", scatter_dimension=0, tiled=True
-        ).astype(jnp.float32),
-        lax.psum_scatter(
-            down_part.astype(jnp.bfloat16), "dp", scatter_dimension=1, tiled=True
-        ).astype(jnp.float32),
-        lax.psum_scatter(
-            gain_part.astype(jnp.bfloat16), "dp", scatter_dimension=1, tiled=True
-        ).astype(jnp.float32),
-        lax.psum_scatter(
-            bias_part.astype(jnp.bfloat16), "dp", scatter_dimension=1, tiled=True
-        ).astype(jnp.float32),
-        lax.psum_scatter(
-            mix_part.astype(jnp.bfloat16), "dp", scatter_dimension=0, tiled=True
-        ).astype(jnp.float32),
-    )
-    qkv_grad, out_grad, up_grad, down_grad, gain_shard, bias_shard, mix_proj_grad = reduced
-    mix_grad, gain_grad, bias_grad = (
-        lax.psum(mix_partial.astype(jnp.bfloat16), "tensor").astype(jnp.float32),
-        lax.psum(gain_shard.astype(jnp.bfloat16), "tensor").astype(jnp.float32),
-        lax.psum(bias_shard.astype(jnp.bfloat16), "tensor").astype(jnp.float32),
-    )
-    next_proj_grad = lax.psum(next_part, "dp")
+    mix_grad = butterfly_sum(
+        jnp.stack(entry_mixes, 1).reshape(STREAMS * ENTRIES, tokens), "tensor"
+    )
+    norm_part = butterfly_sum(
+        jnp.concatenate(
+            [jnp.sum(normed_grad_own * unit_own, axis=1), jnp.sum(normed_grad_own, axis=1)], 0
+        ),
+        "dp",
+    )
+    norm_whole = lax.dynamic_slice_in_dim(gather_columns(norm_part), dp_place * share, share, 1)
+    gain_grad = norm_whole[:STREAMS]
+    bias_grad = norm_whole[STREAMS:]
+    next_row = jnp.pad(next_part, ((0, 0), (0, width_all - next_part.shape[1])))
+    mix_sums = butterfly_sum(jnp.concatenate([mix_part, next_row], 0), "dp")
+    mix_proj_grad = lax.dynamic_slice_in_dim(mix_sums[:mix_out], dp_place * share, share, 1).T
+    next_proj_grad = mix_sums[mix_out:, : next_part.shape[1]]
     return (
         block_own,
         next_mix,

time: 1380 us -> 777 us (0.56)
  the two profiles are of different devices: /device:TPU:0 before, /device:TPU:9 now
where the time goes in v1:
time: 777 us; the launch traced here: 769 us
  waiting for transfers between devices  288 us (37%)
  matrix products  185 us (24%)
  other arithmetic  120 us (15%)
  local copies, waits for them, and re-layouts  72.6 us (9%)
  starting transfers between devices  69.5 us (9%)
  between operations  17.7 us (2%)
  blocking collectives  16.6 us (2%)
    ppermute x60, waiting for transfers between devices, swap(): return lax.ppermute(values, axis, [(i, i ^ bit) for i in range(count)])  260 us
    dot_general x8, matrix products, local_dot(): return jnp.dot(left, right, preferred_element_type=jnp.float32)  71.3 us
    ppermute x60, starting transfers between devices, swap(): return lax.ppermute(values, axis, [(i, i ^ bit) for i in range(count)])  68.8 us
    dot_general x8, matrix products, contract_rows(): lax.dot_general(left, right, (((0,), (0,)), ((), ())), preferred_element_...  49.7 us
    dot_general x8, matrix products, contract_cols(): lax.dot_general(left, right, (((1,), (1,)), ((), ())), preferred_element_...  42.9 us
    reduce_scatter x1, waiting for transfers between devices, per_device(): lax.psum_scatter(up_part.astype(jnp.bfloat16), 'dp', scatter_dimension=0,...  25.9 us
    unnamed x261, local copies, waits for them, and re-layouts  24.8 us
    reduce_sum x1, other arithmetic, per_device(): jnp.sum(stream_grad * history[entry].astype(jnp.float32)[None], axis=-1)  22 us
  transfers between devices with their start and end apart: 68, of which 30 were waited for; matrix products, arithmetic and copies ran while one was open for 40% of the time, Pallas kernels for 0%

profile of v1, /device:TPU:9, one launch (start us, length us, event | category | flops | bytes accessed | tf_op | source)
XLA Modules:
  0.0 769.2 jit_solution(4228252734500191891)
XLA Ops:
  10.7 5.1 bitcast_convert_fusion.8
  16.0 10.5 %fusion.129 = (f32[4,1024]{1,0:T(4,128)S(1)}, f32[4,1024]{1,0:T(4,128)S(1)}, f32[4,1024,512]{2,1,0:T(8,128)}) fusion(f32[1024,512]{1,0:T(8,128)S(1)} %get-tuple-element.127, f32[4,1024]{1,0:T(4,128)S(1)} %get-tuple-element.213, f32[1024,512]{1,0:T(8,128)S(1)} %get-tuple-element.128, f32[4,1024]{1,0:T(4,128)S(1)} %get-tuple-element.214, ...), kind=kLoop, calls=%fused_computation.402 | loop fusion | flops 41934848 | bytes 27443200 | tf_op jit(solution)/shard_map/reduce_sum | solution.py:273
  27.9 16.6 %all_gather.15 = bf16[2048,48]{0,1:T(8,128)(2,1)S(1)} all-gather(bf16[256,48]{0,1:T(8,128)(2,1)S(1)} %pad_maximum_fusion.23), channel_id=1, replica_groups=mesh['dp'=8,'tensor'=4] {'dp'}, dimensions={0}, use_global_device_ids=true | all-gather | bytes 221184 | tf_op jit(solution)/shard_map/all_gather | solution.py:253
  48.1 4.3 add_convert_fusion.1
  60.1 18.8 %collective-permute-done.6 = bf16[1024,512]{1,0:T(8,128)(2,1)S(1)} collective-permute-done((bf16[1024,512]{1,0:T(8,128)(2,1)}, bf16[1024,512]{1,0:T(8,128)(2,1)S(1)}, u32[]{:S(2)}, u32[]{:S(2)}) %collective-permute-start.6) | collective-permute-done | bytes 1048608 | tf_op jit(solution)/shard_map/ppermute | solution.py:158
  84.5 17.0 %collective-permute-done.10 = bf16[1024,512]{1,0:T(8,128)(2,1)S(1)} collective-permute-done((bf16[1024,512]{1,0:T(8,128)(2,1)}, bf16[1024,512]{1,0:T(8,128)(2,1)S(1)}, u32[]{:S(2)}, u32[]{:S(2)}) %collective-permute-start.10) | collective-permute-done | bytes 1048608 | tf_op jit(solution)/shard_map/ppermute | solution.py:158
  114.4 9.6 %collective-permute-done.2 = bf16[1024,512]{1,0:T(8,128)(2,1)S(1)} collective-permute-done((bf16[1024,512]{1,0:T(8,128)(2,1)}, bf16[1024,512]{1,0:T(8,128)(2,1)S(1)}, u32[]{:S(2)}, u32[]{:S(2)}) %collective-permute-start.2) | collective-permute-done | bytes 1048608 | tf_op jit(solution)/shard_map/ppermute | solution.py:158
  126.0 20.4 %collective-permute-done.14 = bf16[1024,512]{1,0:T(8,128)(2,1)S(1)} collective-permute-done((bf16[1024,512]{1,0:T(8,128)(2,1)S(1)}, bf16[1024,512]{1,0:T(8,128)(2,1)S(1)}, u32[]{:S(2)}, u32[]{:S(2)}) %collective-permute-start.14) | collective-permute-done | bytes 1048608 | tf_op jit(solution)/shard_map/ppermute | solution.py:158
  161.5 7.4 collective-permute-done.12
  173.4 6.9 collective-permute-done.4
  181.3 10.1 %collective-permute-done.16 = bf16[512,512]{1,0:T(8,128)(2,1)S(1)} collective-permute-done((bf16[512,512]{1,0:T(8,128)(2,1)S(1)}, bf16[512,512]{1,0:T(8,128)(2,1)S(1)}, u32[]{:S(2)}, u32[]{:S(2)}) %collective-permute-start.16) | collective-permute-done | bytes 524320 | tf_op jit(solution)/shard_map/ppermute | solution.py:158
  192.6 4.0 slice_bitcast_fusion.4
  196.6 4.2 copy.49
  200.8 5.2 fusion.30
  209.8 5.2 fusion.28
  215.2 5.6 fusion.59
  232.0 30.7 %fusion.8 = (bf16[1024,2048]{1,0:T(8,128)(2,1)}, f32[1024,2048]{1,0:T(8,128)}) fusion(bf16[1024,2048]{1,0:T(8,128)(2,1)} %maximum_dynamic-update-slice_fusion.3, bf16[2048,2048]{1,0:T(8,128)(2,1)} %all-gather.9.cloned.1.call-done), kind=kOutput, calls=%fused_computation.13 | convolution fusion | flops 8726249472 | bytes 25165824 | tf_op jit(solution)/shard_map/dot_general | solution.py:55
  262.8 14.8 %fusion.144 = f32[1024,2048]{1,0:T(8,128)} fusion(bf16[1024,2048]{1,0:T(8,128)(2,1)} %get-tuple-element.197, bf16[2048,2048]{1,0:T(8,128)(2,1)} %all-gather.11.cloned.1.call-done), kind=kOutput, calls=%fused_computation.415 | convolution fusion | flops 8589934592 | bytes 20971520 | tf_op jit(solution)/shard_map/dot_general | solution.py:55
  277.6 6.4 add_convert_fusion
  287.6 19.8 %collective-permute-done.18 = bf16[2,512,512]{2,1,0:T(8,128)(2,1)S(1)} collective-permute-done((bf16[2,512,512]{2,1,0:T(8,128)(2,1)S(1)}, bf16[2,512,512]{2,1,0:T(8,128)(2,1)S(1)}, u32[]{:S(2)}, u32[]{:S(2)}) %collective-permute-start.18) | collective-permute-done | bytes 1048608 | tf_op jit(solution)/shard_map/ppermute | solution.py:158
  311.6 8.6 %collective-permute-done.19 = bf16[1,512,512]{2,1,0:T(8,128)(2,1)S(1)} collective-permute-done((bf16[1,512,512]{2,1,0:T(8,128)(2,1)S(1)}, bf16[1,512,512]{2,1,0:T(8,128)(2,1)S(1)}, u32[]{:S(2)}, u32[]{:S(2)}) %collective-permute-start.19) | collective-permute-done | bytes 524320 | tf_op jit(solution)/shard_map/ppermute | solution.py:158
  325.4 16.9 %collective-permute-done.26 = bf16[1024,512]{1,0:T(8,128)(2,1)S(1)} collective-permute-done((bf16[1024,512]{1,0:T(8,128)(2,1)S(1)}, bf16[1024,512]{1,0:T(8,128)(2,1)S(1)}, u32[]{:S(2)}, u32[]{:S(2)}) %collective-permute-start.26) | collective-permute-done | bytes 1048608 | tf_op jit(solution)/shard_map/ppermute | solution.py:158
  345.4 31.1 %collective-permute-done.28 = bf16[512,512]{1,0:T(8,128)(2,1)S(1)} collective-permute-done((bf16[512,512]{1,0:T(8,128)(2,1)S(1)}, bf16[512,512]{1,0:T(8,128)(2,1)S(1)}, u32[]{:S(2)}, u32[]{:S(2)}) %collective-permute-start.28) | collective-permute-done | bytes 524320 | tf_op jit(solution)/shard_map/ppermute | solution.py:158
  378.5 8.0 %collective-permute-done.24 = bf16[512,512]{1,0:T(8,128)(2,1)S(1)} collective-permute-done((bf16[512,512]{1,0:T(8,128)(2,1)S(1)}, bf16[512,512]{1,0:T(8,128)(2,1)S(1)}, u32[]{:S(2)}, u32[]{:S(2)}) %collective-permute-start.24) | collective-permute-done | bytes 524320 | tf_op jit(solution)/shard_map/ppermute | solution.py:158
  394.1 7.5 fusion.130
  403.6 3.6 convolution_convert_fusion.6
  407.2 4.6 convolution_convert_fusion.10
  411.9 5.4 multiply_reduce_fusion.20
  438.0 4.6 fusion.36
  442.6 4.7 fusion.37
  447.3 4.7 fusion.38
  455.1 14.1 %convolution_convert_fusion = bf16[2048,2048]{1,0:T(8,128)(2,1)} fusion(bf16[1024,2048]{1,0:T(8,128)(2,1)} %get-tuple-element.197, bf16[1024,2048]{1,0:T(8,128)(2,1)} %copy-done.50), kind=kOutput, calls=%fused_computation.70 | convolution fusion | flops 8594128896 | bytes 16777216 | tf_op jit(solution)/shard_map/dot_general | solution.py:59
  475.1 4.5 collective-permute-start.57
  479.6 4.0 convolution_convert_fusion.5
  501.9 14.5 %fusion.16 = bf16[1024,2048]{1,0:T(8,128)(2,1)} fusion(f32[1024,2048]{1,0:T(8,128)} %get-tuple-element.198, bf16[1024,2048]{1,0:T(8,128)(2,1)S(1)} %copy-done.51, bf16[2048,2048]{1,0:T(8,128)(2,1)S(1)} %bitcast.433), kind=kOutput, calls=%fused_computation.21 | convolution fusion | flops 8610906112 | bytes 25165824 | tf_op jit(solution)/shard_map/dot_general | solution.py:65
  516.4 14.1 %convolution_convert_fusion.1 = bf16[2048,2048]{1,0:T(8,128)(2,1)} fusion(bf16[1024,2048]{1,0:T(8,128)(2,1)} %maximum_dynamic-update-slice_fusion.3, bf16[1024,2048]{1,0:T(8,128)(2,1)} %fusion.16), kind=kOutput, calls=%fused_computation.71 | convolution fusion | flops 8594128896 | bytes 16777216 | tf_op jit(solution)/shard_map/dot_general | solution.py:59
  530.5 12.8 %convolution_convert_fusion.2 = bf16[1024,2048]{1,0:T(8,128)(2,1)S(1)} fusion(bf16[1024,2048]{1,0:T(8,128)(2,1)} %fusion.16, bf16[2048,2048]{1,0:T(8,128)(2,1)} %all-gather.9.cloned.1.call-done), kind=kOutput, calls=%fused_computation.89 | convolution fusion | flops 8592031744 | bytes 16777216 | tf_op jit(solution)/shard_map/dot_general | solution.py:65
  556.0 13.5 %collective-permute-done.38 = bf16[2,512,512]{2,1,0:T(8,128)(2,1)S(1)} collective-permute-done((bf16[2,512,512]{2,1,0:T(8,128)(2,1)S(1)}, bf16[2,512,512]{2,1,0:T(8,128)(2,1)S(1)}, u32[]{:S(2)}, u32[]{:S(2)}) %collective-permute-start.38) | collective-permute-done | bytes 1048608 | tf_op jit(solution)/shard_map/ppermute | solution.py:158
  573.4 18.6 %collective-permute-done.42 = bf16[2,512,512]{2,1,0:T(8,128)(2,1)S(1)} collective-permute-done((bf16[2,512,512]{2,1,0:T(8,128)(2,1)S(1)}, bf16[2,512,512]{2,1,0:T(8,128)(2,1)S(1)}, u32[]{:S(2)}, u32[]{:S(2)}) %collective-permute-start.42) | collective-permute-done | bytes 1048608 | tf_op jit(solution)/shard_map/ppermute | solution.py:158
  595.8 9.3 %collective-permute-done.31 = bf16[1,512,512]{2,1,0:T(8,128)(2,1)S(1)} collective-permute-done((bf16[1,512,512]{2,1,0:T(8,128)(2,1)S(1)}, bf16[1,512,512]{2,1,0:T(8,128)(2,1)S(1)}, u32[]{:S(2)}, u32[]{:S(2)}) %collective-permute-start.31) | collective-permute-done | bytes 524320 | tf_op jit(solution)/shard_map/ppermute | solution.py:158
  611.0 5.4 collective-permute-done.35
  622.2 5.4 collective-permute-done.39
  628.7 10.0 %collective-permute-done.43 = bf16[1,512,512]{2,1,0:T(8,128)(2,1)S(1)} collective-permute-done((bf16[1,512,512]{2,1,0:T(8,128)(2,1)S(1)}, bf16[1,512,512]{2,1,0:T(8,128)(2,1)S(1)}, u32[]{:S(2)}, u32[]{:S(2)}) %collective-permute-start.43) | collective-permute-done | bytes 524320 | tf_op jit(solution)/shard_map/ppermute | solution.py:158
  639.5 3.7 multiply_reduce_fusion
  653.2 9.0 %fusion.128 = (f32[4,512]{1,0:T(4,128)S(1)}, f32[4,1024,512]{2,1,0:T(8,128)S(1)}) fusion(f32[1,1024,512]{2,1,0:T(8,128)} %copy-done.24, f32[1,1024,512]{2,1,0:T(8,128)} %copy-done.23, f32[1,1024,512]{2,1,0:T(8,128)} %copy-done.22, f32[1,1024,512]{2,1,0:T(8,128)S(1)} %maximum_bitcast_fusion, f32[4,1024]{1,0:T(4,128)S(1)} %get-tuple-element.192, ...), kind=kLoop, calls=%fused_computation.401 | loop fusion | flops 23066624 | bytes 25247744 | tf_op jit(solution)/shard_map/reduce_sum | solution.py:392
  668.0 22.0 %multiply_reduce_fusion.1 = (f32[4,1024]{1,0:T(4,128)S(1)}, f32[4,1024]{1,0:T(4,128)S(1)}, f32[4,1024]{1,0:T(4,128)S(1)}, f32[4,1024]{1,0:T(4,128)S(1)}, f32[4,1...) fusion(f32[4,1024,512]{2,1,0:T(8,128)S(1)} %fusion.41, ...), kind=kLoop, calls=%fused_computation.24 | loop fusion | flops 70742016 | bytes 46432256 | tf_op jit(solution)/shard_map/reduce_sum | solution.py:385
  703.4 9.3 %collective-permute-done.52 = f32[8,512]{1,0:T(8,128)S(1)} collective-permute-done((f32[8,512]{1,0:T(8,128)S(1)}, f32[8,512]{1,0:T(8,128)S(1)}, u32[]{:S(2)}, u32[]{:S(2)}) %collective-permute-start.52) | collective-permute-done | bytes 16416 | tf_op jit(solution)/shard_map/ppermute | solution.py:158
  733.5 25.9 %reduce-scatter.9.cloned.1.call-done = bf16[256,2048]{1,0:T(8,128)(2,1)} async-done(((bf16[2048,2048]{1,0:T(8,128)(2,1)}), bf16[256,2048]{1,0:T(8,128)(2,1)}) %reduce-scatter.9.cloned.1.call-update) | async-done | bytes 1048592 | tf_op jit(solution)/shard_map/reduce_scatter | solution.py:335
  (581 shorter events, 233.2 us)
Async XLA Ops:
  7.2 185.4 %all-gather.5.cloned.1.call-start = ((), (), s32[]{:S(2)}) async-start(), calls=%async_computation.4 | async-start | bytes 7077888 | tf_op jit(solution)/shard_map/all_gather | solution.py:257
  7.9 224.1 %all-gather.9.cloned.1.call-start = ((), (), s32[]{:S(2)}) async-start(), calls=%async_computation.6 | async-start | bytes 9437184 | tf_op jit(solution)/shard_map/all_gather | solution.py:258
  8.7 254.1 %all-gather.11.cloned.1.call-start = ((), (), s32[]{:S(2)}) async-start(), calls=%async_computation.7 | async-start | bytes 9437184 | tf_op jit(solution)/shard_map/all_gather | solution.py:259
  9.4 268.2 %all-gather.7.cloned.1.call-start = ((), (), s32[]{:S(2)}) async-start(), calls=%async_computation.5 | async-start | bytes 2359296 | tf_op jit(solution)/shard_map/all_gather | solution.py:260
  55.4 23.6 %collective-permute-start.6 = (bf16[1024,512]{1,0:T(8,128)(2,1)}, bf16[1024,512]{1,0:T(8,128)(2,1)S(1)}, u32[]{:S(2)}, u32[]{:S(2)}) collective-permute-start(bf16[1024,512]{1,0:T(8,128)(2,1)} %get-tuple-element.145), channel_id=1, source_target_pairs={{0,1},{1,0},{2,3},{3,2},{4,5},{5,4},{6,7},{7,6},{8,9},{9,8},{10,11... | collective-permute-start | bytes 3145736 | tf_op jit(solution)/shard_map/ppermute | solution.py:158
  55.4 25.2 %collective-permute-start.7 = (bf16[1024,512]{1,0:T(8,128)(2,1)}, bf16[1024,512]{1,0:T(8,128)(2,1)S(1)}, u32[]{:S(2)}, u32[]{:S(2)}) collective-permute-start(bf16[1024,512]{1,0:T(8,128)(2,1)} %get-tuple-element.145), channel_id=1, source_target_pairs={{0,2},{1,3},{2,0},{3,1},{4,6},{5,7},{6,4},{7,5},{8,10},{9,11},{10,... | collective-permute-start | bytes 3145736 | tf_op jit(solution)/shard_map/ppermute | solution.py:158
  56.8 669.6 %reduce-scatter.7.cloned.1.call-start = ((), (), s32[]{:S(2)}) async-start(), calls=%async_computation.9 | async-start | bytes 2359296 | tf_op jit(solution)/shard_map/reduce_scatter | solution.py:343
  56.9 44.6 %collective-permute-start.10 = (bf16[1024,512]{1,0:T(8,128)(2,1)}, bf16[1024,512]{1,0:T(8,128)(2,1)S(1)}, u32[]{:S(2)}, u32[]{:S(2)}) collective-permute-start(bf16[1024,512]{1,0:T(8,128)(2,1)} %get-tuple-element.143), channel_id=1, source_target_pairs={{0,1},{1,0},{2,3},{3,2},{4,5},{5,4},{6,7},{7,6},{8,9},{9,8},{10,11... | collective-permute-start | bytes 3145736 | tf_op jit(solution)/shard_map/ppermute | solution.py:158
  60.0 54.2 %collective-permute-start.11 = (bf16[1024,512]{1,0:T(8,128)(2,1)}, bf16[1024,512]{1,0:T(8,128)(2,1)S(1)}, u32[]{:S(2)}, u32[]{:S(2)}) collective-permute-start(bf16[1024,512]{1,0:T(8,128)(2,1)} %get-tuple-element.143), channel_id=1, source_target_pairs={{0,2},{1,3},{2,0},{3,1},{4,6},{5,7},{6,4},{7,5},{8,10},{9,11},{10,... | collective-permute-start | bytes 3145736 | tf_op jit(solution)/shard_map/ppermute | solution.py:158
  60.1 63.9 %collective-permute-start.2 = (bf16[1024,512]{1,0:T(8,128)(2,1)}, bf16[1024,512]{1,0:T(8,128)(2,1)S(1)}, u32[]{:S(2)}, u32[]{:S(2)}) collective-permute-start(bf16[1024,512]{1,0:T(8,128)(2,1)} %get-tuple-element.146), channel_id=1, source_target_pairs={{0,1},{1,0},{2,3},{3,2},{4,5},{5,4},{6,7},{7,6},{8,9},{9,8},{10,11... | collective-permute-start | bytes 3145736 | tf_op jit(solution)/shard_map/ppermute | solution.py:158
  79.0 45.3 %collective-permute-start.3 = (bf16[1024,512]{1,0:T(8,128)(2,1)}, bf16[1024,512]{1,0:T(8,128)(2,1)S(1)}, u32[]{:S(2)}, u32[]{:S(2)}) collective-permute-start(bf16[1024,512]{1,0:T(8,128)(2,1)} %get-tuple-element.146), channel_id=1, source_target_pairs={{0,2},{1,3},{2,0},{3,1},{4,6},{5,7},{6,4},{7,5},{8,10},{9,11},{10,... | collective-permute-start | bytes 3145736 | tf_op jit(solution)/shard_map/ppermute | solution.py:158
  80.6 65.8 %collective-permute-start.14 = (bf16[1024,512]{1,0:T(8,128)(2,1)S(1)}, bf16[1024,512]{1,0:T(8,128)(2,1)S(1)}, u32[]{:S(2)}, u32[]{:S(2)}) collective-permute-start(bf16[1024,512]{1,0:T(8,128)(2,1)S(1)} %get-tuple-element.144), channel_id=1, source_target_pairs={{0,1},{1,0},{2,3},{3,2},{4,5},{5,4},{6,7},{7,6},{8,9},{9,8},{10,11... | collective-permute-start | bytes 3145736 | tf_op jit(solution)/shard_map/ppermute | solution.py:158
  101.5 47.4 %collective-permute-start.15 = (bf16[1024,512]{1,0:T(8,128)(2,1)S(1)}, bf16[1024,512]{1,0:T(8,128)(2,1)S(1)}, u32[]{:S(2)}, u32[]{:S(2)}) collective-permute-start(bf16[1024,512]{1,0:T(8,128)(2,1)S(1)} %get-tuple-element.144), channel_id=1, source_target_pairs={{0,2},{1,3},{2,0},{3,1},{4,6},{5,7},{6,4},{7,5},{8,10},{9,11},{10,... | collective-permute-start | bytes 3145736 | tf_op jit(solution)/shard_map/ppermute | solution.py:158
  114.2 43.4 %collective-permute-start.8 = (bf16[512,512]{1,0:T(8,128)(2,1)S(1)}, bf16[512,512]{1,0:T(8,128)(2,1)S(1)}, u32[]{:S(2)}, u32[]{:S(2)}) collective-permute-start(bf16[512,512]{1,0:T(8,128)(2,1)S(1)} %slice.537), channel_id=1, source_target_pairs={{0,2},{1,3},{2,0},{3,1},{4,6},{5,7},{6,4},{7,5},{8,10},{9,11},{10,... | collective-permute-start | bytes 1572872 | tf_op jit(solution)/shard_map/ppermute | solution.py:158
  124.0 36.0 %collective-permute-start.9 = (bf16[512,512]{1,0:T(8,128)(2,1)S(1)}, bf16[512,512]{1,0:T(8,128)(2,1)S(1)}, u32[]{:S(2)}, u32[]{:S(2)}) collective-permute-start(bf16[512,512]{1,0:T(8,128)(2,1)S(1)} %slice.538), channel_id=1, source_target_pairs={{0,1},{1,0},{2,3},{3,2},{4,5},{5,4},{6,7},{7,6},{8,9},{9,8},{10,11... | collective-permute-start | bytes 1572872 | tf_op jit(solution)/shard_map/ppermute | solution.py:158
  124.2 44.7 %collective-permute-start.12 = (bf16[512,512]{1,0:T(8,128)(2,1)S(1)}, bf16[512,512]{1,0:T(8,128)(2,1)S(1)}, u32[]{:S(2)}, u32[]{:S(2)}) collective-permute-start(bf16[512,512]{1,0:T(8,128)(2,1)S(1)} %slice.545), channel_id=1, source_target_pairs={{0,2},{1,3},{2,0},{3,1},{4,6},{5,7},{6,4},{7,5},{8,10},{9,11},{10,... | collective-permute-start | bytes 1572872 | tf_op jit(solution)/shard_map/ppermute | solution.py:158
  146.4 25.9 %collective-permute-start.13 = (bf16[512,512]{1,0:T(8,128)(2,1)S(1)}, bf16[512,512]{1,0:T(8,128)(2,1)S(1)}, u32[]{:S(2)}, u32[]{:S(2)}) collective-permute-start(bf16[512,512]{1,0:T(8,128)(2,1)S(1)} %slice.546), channel_id=1, source_target_pairs={{0,1},{1,0},{2,3},{3,2},{4,5},{5,4},{6,7},{7,6},{8,9},{9,8},{10,11... | collective-permute-start | bytes 1572872 | tf_op jit(solution)/shard_map/ppermute | solution.py:158
  148.9 31.3 %collective-permute-start.4 = (bf16[512,512]{1,0:T(8,128)(2,1)S(1)}, bf16[512,512]{1,0:T(8,128)(2,1)S(1)}, u32[]{:S(2)}, u32[]{:S(2)}) collective-permute-start(bf16[512,512]{1,0:T(8,128)(2,1)S(1)} %slice.532), channel_id=1, source_target_pairs={{0,2},{1,3},{2,0},{3,1},{4,6},{5,7},{6,4},{7,5},{8,10},{9,11},{10,... | collective-permute-start | bytes 1572872 | tf_op jit(solution)/shard_map/ppermute | solution.py:158
  157.6 22.6 %collective-permute-start.5 = (bf16[512,512]{1,0:T(8,128)(2,1)S(1)}, bf16[512,512]{1,0:T(8,128)(2,1)S(1)}, u32[]{:S(2)}, u32[]{:S(2)}) collective-permute-start(bf16[512,512]{1,0:T(8,128)(2,1)S(1)} %slice.533), channel_id=1, source_target_pairs={{0,1},{1,0},{2,3},{3,2},{4,5},{5,4},{6,7},{7,6},{8,9},{9,8},{10,11... | collective-permute-start | bytes 1572872 | tf_op jit(solution)/shard_map/ppermute | solution.py:158
  160.0 31.5 %collective-permute-start.16 = (bf16[512,512]{1,0:T(8,128)(2,1)S(1)}, bf16[512,512]{1,0:T(8,128)(2,1)S(1)}, u32[]{:S(2)}, u32[]{:S(2)}) collective-permute-start(bf16[512,512]{1,0:T(8,128)(2,1)S(1)} %slice.553), channel_id=1, source_target_pairs={{0,2},{1,3},{2,0},{3,1},{4,6},{5,7},{6,4},{7,5},{8,10},{9,11},{10,... | collective-permute-start | bytes 1572872 | tf_op jit(solution)/shard_map/ppermute | solution.py:158
  284.6 22.8 %collective-permute-start.18 = (bf16[2,512,512]{2,1,0:T(8,128)(2,1)S(1)}, bf16[2,512,512]{2,1,0:T(8,128)(2,1)S(1)}, u32[]{:S(2)}, u32[]{:S(2)}) collective-permute-start(bf16[2,512,512]{2,1,0:T(8,128)(2,1)S(1)} %pad_maximum_fusion.5), channel_id=1, source_target_pairs={{0,1},{1,0},{2,3},{3,2},{4,5},{5,4},{6,7},{7,6},{8,9},{9,8},{10,11... | collective-permute-start | bytes 3145736 | tf_op jit(solution)/shard_map/ppermute | solution.py:158
  286.1 23.2 %collective-permute-start.20 = (bf16[2,512,512]{2,1,0:T(8,128)(2,1)S(1)}, bf16[2,512,512]{2,1,0:T(8,128)(2,1)S(1)}, u32[]{:S(2)}, u32[]{:S(2)}) collective-permute-start(bf16[2,512,512]{2,1,0:T(8,128)(2,1)S(1)} %pad_maximum_fusion.6), channel_id=1, source_target_pairs={{0,2},{1,3},{2,0},{3,1},{4,6},{5,7},{6,4},{7,5},{8,10},{9,11},{10,... | collective-permute-start | bytes 3145736 | tf_op jit(solution)/shard_map/ppermute | solution.py:158
  310.4 31.8 %collective-permute-start.26 = (bf16[1024,512]{1,0:T(8,128)(2,1)S(1)}, bf16[1024,512]{1,0:T(8,128)(2,1)S(1)}, u32[]{:S(2)}, u32[]{:S(2)}) collective-permute-start(bf16[1024,512]{1,0:T(8,128)(2,1)S(1)} %copy-done.61), channel_id=1, source_target_pairs={{0,1},{1,0},{2,3},{3,2},{4,5},{5,4},{6,7},{7,6},{8,9},{9,8},{10,11... | collective-permute-start | bytes 3145736 | tf_op jit(solution)/shard_map/ppermute | solution.py:158
  311.0 31.7 %collective-permute-start.27 = (bf16[1024,512]{1,0:T(8,128)(2,1)S(1)}, bf16[1024,512]{1,0:T(8,128)(2,1)S(1)}, u32[]{:S(2)}, u32[]{:S(2)}) collective-permute-start(bf16[1024,512]{1,0:T(8,128)(2,1)S(1)} %copy-done.61), channel_id=1, source_target_pairs={{0,2},{1,3},{2,0},{3,1},{4,6},{5,7},{6,4},{7,5},{8,10},{9,11},{10,... | collective-permute-start | bytes 3145736 | tf_op jit(solution)/shard_map/ppermute | solution.py:158
  323.2 53.4 %collective-permute-start.22 = (bf16[1024,512]{1,0:T(8,128)(2,1)S(1)}, bf16[1024,512]{1,0:T(8,128)(2,1)S(1)}, u32[]{:S(2)}, u32[]{:S(2)}) collective-permute-start(bf16[1024,512]{1,0:T(8,128)(2,1)S(1)} %get-tuple-element.118), channel_id=1, source_target_pairs={{0,1},{1,0},{2,3},{3,2},{4,5},{5,4},{6,7},{7,6},{8,9},{9,8},{10,11... | collective-permute-start | bytes 3145736 | tf_op jit(solution)/shard_map/ppermute | solution.py:158
  323.4 54.6 %collective-permute-start.23 = (bf16[1024,512]{1,0:T(8,128)(2,1)S(1)}, bf16[1024,512]{1,0:T(8,128)(2,1)S(1)}, u32[]{:S(2)}, u32[]{:S(2)}) collective-permute-start(bf16[1024,512]{1,0:T(8,128)(2,1)S(1)} %get-tuple-element.118), channel_id=1, source_target_pairs={{0,2},{1,3},{2,0},{3,1},{4,6},{5,7},{6,4},{7,5},{8,10},{9,11},{10,... | collective-permute-start | bytes 3145736 | tf_op jit(solution)/shard_map/ppermute | solution.py:158
  342.3 34.2 %collective-permute-start.28 = (bf16[512,512]{1,0:T(8,128)(2,1)S(1)}, bf16[512,512]{1,0:T(8,128)(2,1)S(1)}, u32[]{:S(2)}, u32[]{:S(2)}) collective-permute-start(bf16[512,512]{1,0:T(8,128)(2,1)S(1)} %slice.564), channel_id=1, source_target_pairs={{0,2},{1,3},{2,0},{3,1},{4,6},{5,7},{6,4},{7,5},{8,10},{9,11},{10,... | collective-permute-start | bytes 1572872 | tf_op jit(solution)/shard_map/ppermute | solution.py:158
  342.8 33.7 %collective-permute-start.29 = (bf16[512,512]{1,0:T(8,128)(2,1)S(1)}, bf16[512,512]{1,0:T(8,128)(2,1)S(1)}, u32[]{:S(2)}, u32[]{:S(2)}) collective-permute-start(bf16[512,512]{1,0:T(8,128)(2,1)S(1)} %slice.565), channel_id=1, source_target_pairs={{0,1},{1,0},{2,3},{3,2},{4,5},{5,4},{6,7},{7,6},{8,9},{9,8},{10,11... | collective-permute-start | bytes 1572872 | tf_op jit(solution)/shard_map/ppermute | solution.py:158
  427.4 300.8 %reduce-scatter.5.cloned.1.call-start = ((), (), s32[]{:S(2)}) async-start(), calls=%async_computation.8 | async-start | bytes 7077888 | tf_op jit(solution)/shard_map/reduce_scatter | solution.py:366
  455.1 275.6 %reduce-scatter.11.cloned.1.call-start = ((), (), s32[]{:S(2)}) async-start(), calls=%async_computation.11 | async-start | bytes 9437184 | tf_op jit(solution)/shard_map/reduce_scatter | solution.py:329
  469.3 290.1 %reduce-scatter.9.cloned.1.call-start = ((), (), s32[]{:S(2)}) async-start(), calls=%async_computation.10 | async-start | bytes 9437184 | tf_op jit(solution)/shard_map/reduce_scatter | solution.py:335
  475.1 70.6 %collective-permute-start.57 = (f32[80,2048]{1,0:T(8,128)}, f32[80,2048]{1,0:T(8,128)}, u32[]{:S(2)}, u32[]{:S(2)}) collective-permute-start(f32[80,2048]{1,0:T(8,128)} %select_maximum_fusion), channel_id=1, source_target_pairs={{0,4},{4,0},{8,12},{12,8},{16,20},{20,16},{24,28},{28,24},{1,5},{5... | collective-permute-start | bytes 1966088 | tf_op jit(solution)/shard_map/ppermute | solution.py:158
  485.3 62.7 %collective-permute-start.30 = (bf16[2,512,512]{2,1,0:T(8,128)(2,1)}, bf16[2,512,512]{2,1,0:T(8,128)(2,1)}, u32[]{:S(2)}, u32[]{:S(2)}) collective-permute-start(bf16[2,512,512]{2,1,0:T(8,128)(2,1)} %pad_maximum_fusion.7), channel_id=1, source_target_pairs={{0,1},{1,0},{2,3},{3,2},{4,5},{5,4},{6,7},{7,6},{8,9},{9,8},{10,11... | collective-permute-start | bytes 3145736 | tf_op jit(solution)/shard_map/ppermute | solution.py:158
  486.6 63.8 %collective-permute-start.32 = (bf16[2,512,512]{2,1,0:T(8,128)(2,1)}, bf16[2,512,512]{2,1,0:T(8,128)(2,1)}, u32[]{:S(2)}, u32[]{:S(2)}) collective-permute-start(bf16[2,512,512]{2,1,0:T(8,128)(2,1)} %pad_maximum_fusion.8), channel_id=1, source_target_pairs={{0,2},{1,3},{2,0},{3,1},{4,6},{5,7},{6,4},{7,5},{8,10},{9,11},{10,... | collective-permute-start | bytes 3145736 | tf_op jit(solution)/shard_map/ppermute | solution.py:158
  492.5 60.4 %collective-permute-start.34 = (bf16[2,512,512]{2,1,0:T(8,128)(2,1)}, bf16[2,512,512]{2,1,0:T(8,128)(2,1)}, u32[]{:S(2)}, u32[]{:S(2)}) collective-permute-start(bf16[2,512,512]{2,1,0:T(8,128)(2,1)} %pad_maximum_fusion.9), channel_id=1, source_target_pairs={{0,1},{1,0},{2,3},{3,2},{4,5},{5,4},{6,7},{7,6},{8,9},{9,8},{10,11... | collective-permute-start | bytes 3145736 | tf_op jit(solution)/shard_map/ppermute | solution.py:158
  494.4 60.3 %collective-permute-start.36 = (bf16[2,512,512]{2,1,0:T(8,128)(2,1)}, bf16[2,512,512]{2,1,0:T(8,128)(2,1)}, u32[]{:S(2)}, u32[]{:S(2)}) collective-permute-start(bf16[2,512,512]{2,1,0:T(8,128)(2,1)} %pad_maximum_fusion.10), channel_id=1, source_target_pairs={{0,2},{1,3},{2,0},{3,1},{4,6},{5,7},{6,4},{7,5},{8,10},{9,11},{10,... | collective-permute-start | bytes 3145736 | tf_op jit(solution)/shard_map/ppermute | solution.py:158
  545.7 23.8 %collective-permute-start.38 = (bf16[2,512,512]{2,1,0:T(8,128)(2,1)S(1)}, bf16[2,512,512]{2,1,0:T(8,128)(2,1)S(1)}, u32[]{:S(2)}, u32[]{:S(2)}) collective-permute-start(bf16[2,512,512]{2,1,0:T(8,128)(2,1)S(1)} %pad_maximum_fusion.11), channel_id=1, source_target_pairs={{0,1},{1,0},{2,3},{3,2},{4,5},{5,4},{6,7},{7,6},{8,9},{9,8},{10,11... | collective-permute-start | bytes 3145736 | tf_op jit(solution)/shard_map/ppermute | solution.py:158
  548.0 23.5 %collective-permute-start.40 = (bf16[2,512,512]{2,1,0:T(8,128)(2,1)S(1)}, bf16[2,512,512]{2,1,0:T(8,128)(2,1)S(1)}, u32[]{:S(2)}, u32[]{:S(2)}) collective-permute-start(bf16[2,512,512]{2,1,0:T(8,128)(2,1)S(1)} %pad_maximum_fusion.12), channel_id=1, source_target_pairs={{0,2},{1,3},{2,0},{3,1},{4,6},{5,7},{6,4},{7,5},{8,10},{9,11},{10,... | collective-permute-start | bytes 3145736 | tf_op jit(solution)/shard_map/ppermute | solution.py:158
  550.4 41.6 %collective-permute-start.42 = (bf16[2,512,512]{2,1,0:T(8,128)(2,1)S(1)}, bf16[2,512,512]{2,1,0:T(8,128)(2,1)S(1)}, u32[]{:S(2)}, u32[]{:S(2)}) collective-permute-start(bf16[2,512,512]{2,1,0:T(8,128)(2,1)S(1)} %pad_maximum_fusion.13), channel_id=1, source_target_pairs={{0,1},{1,0},{2,3},{3,2},{4,5},{5,4},{6,7},{7,6},{8,9},{9,8},{10,11... | collective-permute-start | bytes 3145736 | tf_op jit(solution)/shard_map/ppermute | solution.py:158
  552.9 41.0 %collective-permute-start.44 = (bf16[2,512,512]{2,1,0:T(8,128)(2,1)S(1)}, bf16[2,512,512]{2,1,0:T(8,128)(2,1)S(1)}, u32[]{:S(2)}, u32[]{:S(2)}) collective-permute-start(bf16[2,512,512]{2,1,0:T(8,128)(2,1)S(1)} %pad_maximum_fusion.14), channel_id=1, source_target_pairs={{0,2},{1,3},{2,0},{3,1},{4,6},{5,7},{6,4},{7,5},{8,10},{9,11},{10,... | collective-permute-start | bytes 3145736 | tf_op jit(solution)/shard_map/ppermute | solution.py:158
  554.7 94.1 %collective-permute-start.58 = (f32[80,2048]{1,0:T(8,128)S(1)}, f32[80,2048]{1,0:T(8,128)}, u32[]{:S(2)}, u32[]{:S(2)}) collective-permute-start(f32[80,2048]{1,0:T(8,128)S(1)} %fusion.127), channel_id=1, source_target_pairs={{0,8},{4,12},{8,0},{12,4},{16,24},{20,28},{24,16},{28,20},{1,9},{5... | collective-permute-start | bytes 1966088 | tf_op jit(solution)/shard_map/ppermute | solution.py:158
  569.5 35.6 %collective-permute-start.31 = (bf16[1,512,512]{2,1,0:T(8,128)(2,1)S(1)}, bf16[1,512,512]{2,1,0:T(8,128)(2,1)S(1)}, u32[]{:S(2)}, u32[]{:S(2)}) collective-permute-start(bf16[1,512,512]{2,1,0:T(8,128)(2,1)S(1)} %fusion.81), channel_id=1, source_target_pairs={{0,2},{1,3},{2,0},{3,1},{4,6},{5,7},{6,4},{7,5},{8,10},{9,11},{10,... | collective-permute-start | bytes 1572872 | tf_op jit(solution)/shard_map/ppermute | solution.py:158
  571.4 36.6 %collective-permute-start.33 = (bf16[1,512,512]{2,1,0:T(8,128)(2,1)S(1)}, bf16[1,512,512]{2,1,0:T(8,128)(2,1)S(1)}, u32[]{:S(2)}, u32[]{:S(2)}) collective-permute-start(bf16[1,512,512]{2,1,0:T(8,128)(2,1)S(1)} %fusion.82), channel_id=1, source_target_pairs={{0,1},{1,0},{2,3},{3,2},{4,5},{5,4},{6,7},{7,6},{8,9},{9,8},{10,11... | collective-permute-start | bytes 1572872 | tf_op jit(solution)/shard_map/ppermute | solution.py:158
  592.0 24.3 %collective-permute-start.35 = (bf16[1,512,512]{2,1,0:T(8,128)(2,1)S(1)}, bf16[1,512,512]{2,1,0:T(8,128)(2,1)S(1)}, u32[]{:S(2)}, u32[]{:S(2)}) collective-permute-start(bf16[1,512,512]{2,1,0:T(8,128)(2,1)S(1)} %fusion.83), channel_id=1, source_target_pairs={{0,2},{1,3},{2,0},{3,1},{4,6},{5,7},{6,4},{7,5},{8,10},{9,11},{10,... | collective-permute-start | bytes 1572872 | tf_op jit(solution)/shard_map/ppermute | solution.py:158
  593.9 25.4 %collective-permute-start.37 = (bf16[1,512,512]{2,1,0:T(8,128)(2,1)S(1)}, bf16[1,512,512]{2,1,0:T(8,128)(2,1)S(1)}, u32[]{:S(2)}, u32[]{:S(2)}) collective-permute-start(bf16[1,512,512]{2,1,0:T(8,128)(2,1)S(1)} %fusion.84), channel_id=1, source_target_pairs={{0,1},{1,0},{2,3},{3,2},{4,5},{5,4},{6,7},{7,6},{8,9},{9,8},{10,11... | collective-permute-start | bytes 1572872 | tf_op jit(solution)/shard_map/ppermute | solution.py:158
  651.0 72.8 %collective-permute-start.59 = (f32[80,2048]{1,0:T(8,128)}, f32[80,2048]{1,0:T(8,128)}, u32[]{:S(2)}, u32[]{:S(2)}) collective-permute-start(f32[80,2048]{1,0:T(8,128)} %add.489), channel_id=1, source_target_pairs={{0,16},{4,20},{8,24},{12,28},{16,0},{20,4},{24,8},{28,12},{1,17},{... | collective-permute-start | bytes 1966088 | tf_op jit(solution)/shard_map/ppermute | solution.py:158
  662.3 34.8 %collective-permute-start.50 = (f32[8,512]{1,0:T(8,128)S(1)}, f32[8,512]{1,0:T(8,128)S(1)}, u32[]{:S(2)}, u32[]{:S(2)}) collective-permute-start(f32[8,512]{1,0:T(8,128)S(1)} %pad_maximum_fusion.24), channel_id=1, source_target_pairs={{0,4},{4,0},{8,12},{12,8},{16,20},{20,16},{24,28},{28,24},{1,5},{5... | collective-permute-start | bytes 49160 | tf_op jit(solution)/shard_map/ppermute | solution.py:158
  690.4 28.2 %collective-permute-start.48 = (f32[36,1024]{1,0:T(8,128)S(1)}, f32[36,1024]{1,0:T(8,128)S(1)}, u32[]{:S(2)}, u32[]{:S(2)}) collective-permute-start(f32[36,1024]{1,0:T(8,128)S(1)} %reshape.451), channel_id=1, source_target_pairs={{0,1},{1,0},{2,3},{3,2},{4,5},{5,4},{6,7},{7,6},{8,9},{9,8},{10,11... | collective-permute-start | bytes 442376 | tf_op jit(solution)/shard_map/ppermute | solution.py:158
  (145 other events, 1876.9 us)
Sparse Core Ops, SparseCore 0:
  9.6 65.5 all-gather.4
  76.9 80.2 all-gather.8
  158.7 80.6 all-gather.10
  240.9 33.8 all-gather.6
  427.5 33.7 reduce-scatter.6
  463.5 72.1 reduce-scatter.4
  538.0 91.2 reduce-scatter.10
  631.6 127.7 reduce-scatter.8

commit v2 on v1

v2 whole, which is shorter than its diff:
```python
import functools

import jax
import jax.numpy as jnp
import numpy as np
from jax import lax
from jax.experimental import pallas as pl
from jax.experimental.pallas import tpu as pltpu
from jax.sharding import PartitionSpec as P

HEAD_DIM = 128
ROT = 32
STREAMS = 4
ENTRIES = 9
LENGTH = 1024
LANES = 128

ln_eps = 1e-05
rms_eps = 1e-06
big_negative = -1e30
root_half = 0.7071067811865476
inv_root_tau = 0.3989422804014327
F32 = jnp.float32
BF16 = jnp.bfloat16
VMEM_BYTES = 56 * 1024 * 1024

NN = (((1,), (0,)), ((), ()))
NT = (((1,), (1,)), ((), ()))
TN = (((0,), (0,)), ((), ()))


def mul(left, right, dims=NN):
    return lax.dot_general(left, right, dims, preferred_element_type=F32)


def kernel_call(body, grid, place, ins, outs, name, flops=0, scratch=()):
    moved = sum(a.size * a.dtype.itemsize for a, _, _ in ins)
    moved += sum(int(np.prod(s)) * jnp.dtype(d).itemsize for s, d, _, _ in outs)
    call = pl.pallas_call(
        body,
        out_shape=[jax.ShapeDtypeStruct(s, d) for s, d, _, _ in outs],
        grid_spec=pltpu.PrefetchScalarGridSpec(
            num_scalar_prefetch=1,
            grid=grid,
            in_specs=[pl.BlockSpec(b, m) for _, b, m in ins],
            out_specs=[pl.BlockSpec(b, m) for _, _, b, m in outs],
            scratch_shapes=[pltpu.VMEM(shape, dtype) for shape, dtype in scratch],
        ),
        compiler_params=pltpu.CompilerParams(
            vmem_limit_bytes=VMEM_BYTES,
            dimension_semantics=("arbitrary",) * len(grid),
        ),
        cost_estimate=pl.CostEstimate(
            flops=int(flops), bytes_accessed=int(moved), transcendentals=0
        ),
        name=name,
    )
    return call(place, *[a for a, _, _ in ins])


def const(*zeros):
    return lambda *_: zeros


def group_parts(refs, shape):
    groups, spot = [], 0
    for parts in shape:
        groups.append(refs[spot : spot + parts])
        spot += parts
    return groups, refs[spot:]


def joined(parts):
    if len(parts) == 1:
        return parts[0][...]
    return jnp.concatenate([part[...] for part in parts], 0)


def normal_parts(x):
    size = jnp.abs(x) * root_half
    lower = 1.0 + 0.3275911 * size
    t = 1.0 / lower
    poly = t * (
        0.254829592
        + t * (-0.284496736 + t * (1.421413741 + t * (-1.453152027 + t * 1.061405429)))
    )
    bell = jnp.exp(-0.5 * x * x)
    tail = 0.5 * poly * bell
    cumulative = jnp.where(x < 0, tail, 1.0 - tail)
    return cumulative, bell * inv_root_tau


def lanes_to_rows(columns, rows):
    lane = lax.broadcasted_iota(jnp.int32, (columns[0].shape[0], LANES), 1)
    wide = jnp.zeros((columns[0].shape[0], LANES), F32)
    for number, column in enumerate(columns):
        wide = jnp.where(lane == number, column, wide)
    return wide.T[:rows]


def mix_kernel(place, hist, coef, streams, stats):
    totals = [None] * STREAMS
    for e in range(ENTRIES):
        entry = hist[e].astype(F32)
        for c in range(STREAMS):
            k = c * ENTRIES + e
            term = coef[:, k : k + 1] * entry
            totals[c] = term if totals[c] is None else totals[c] + term
    columns = []
    for c in range(STREAMS):
        streams[c] = totals[c]
        columns.append(jnp.sum(totals[c], axis=1, keepdims=True))
    for c in range(STREAMS):
        columns.append(jnp.sum(totals[c] * totals[c], axis=1, keepdims=True))
    stats[...] = lanes_to_rows(columns, 2 * STREAMS)


def rows_to_lanes(rows):
    tall = jnp.concatenate([rows, jnp.zeros((LANES - rows.shape[0], LANES), F32)], 0)
    return tall.T


def center_and_spread(stats, width_all):
    turned = rows_to_lanes(stats)
    centers, spreads = [], []
    for c in range(STREAMS):
        center = turned[:, c : c + 1] / width_all
        square = turned[:, STREAMS + c : STREAMS + c + 1] / width_all
        centers.append(center)
        spreads.append(lax.rsqrt(square - center * center + ln_eps))
    return centers, spreads


def norm_kernel(width_all, place, streams, stats, gain, bias, first, last):
    centers, spreads = center_and_spread(stats[...], width_all)
    for c in range(STREAMS):
        unit = (streams[c] - centers[c]) * spreads[c]
        normed = (unit * gain[c : c + 1] + bias[c : c + 1]).astype(BF16)
        if c < STREAMS - 1:
            first[c] = normed
        else:
            last[...] = normed


def spread_kernel(width_all, place, streams, stats, hist, out):
    centers, spreads = center_and_spread(stats[...], width_all)
    units = [(streams[c] - centers[c]) * spreads[c] for c in range(STREAMS)]
    columns = []
    entries = [hist[e].astype(F32) for e in range(ENTRIES)]
    for c in range(STREAMS):
        for e in range(ENTRIES):
            columns.append(jnp.sum(units[c] * entries[e], axis=1, keepdims=True))
    for e in range(ENTRIES):
        columns.append(jnp.sum(entries[e], axis=1, keepdims=True))
    out[...] = lanes_to_rows(columns, out.shape[0])


def turn(x, cosine, ahead, behind):
    half = ROT // 2
    return x * cosine + pltpu.roll(x, half, 1) * ahead + pltpu.roll(x, LANES - half, 1) * behind


def qkv_kernel(shape, place, *refs):
    pieces, refs = group_parts(refs, shape)
    count = len(shape)
    weights, (cosine, ahead, behind, out) = refs[:count], refs[count:]
    total = mul(joined(pieces[0]), weights[0][...])
    for r in range(1, count):
        total += mul(joined(pieces[r]), weights[r][...])
    c = pl.program_id(0)

    @pl.when(c < 2)
    def _():
        for h in range(total.shape[1] // HEAD_DIM):
            spot = slice(h * HEAD_DIM, (h + 1) * HEAD_DIM)
            turned = turn(total[:, spot], cosine[...], ahead[...], behind[...])
            out[:, spot] = turned.astype(BF16)

    @pl.when(c == 2)
    def _():
        out[...] = total.astype(BF16)


ROWS = 256


def attend_kernel(place, q, k, v, out):
    scale = HEAD_DIM**-0.5
    for number in range(q.shape[0] // ROWS):
        start, stop = number * ROWS, (number + 1) * ROWS
        scores = mul(q[start:stop], k[:stop], NT) * scale
        row = lax.broadcasted_iota(jnp.int32, scores.shape, 0) + start
        col = lax.broadcasted_iota(jnp.int32, scores.shape, 1)
        scores = jnp.where(col <= row, scores, big_negative)
        summit = jnp.max(scores, axis=1, keepdims=True)
        exponent = jnp.exp(scores - summit)
        part = jnp.sum(exponent, axis=1, keepdims=True)
        probs = (exponent * (1.0 / part)).astype(BF16)
        out[start:stop] = mul(probs, v[:stop]).astype(BF16)


def attend_back_kernel(place, q, k, v, grad, cosine, ahead, behind, out, dk, dv):
    scale = HEAD_DIM**-0.5
    dk[...] = jnp.zeros_like(dk)
    dv[...] = jnp.zeros_like(dv)
    for number in range(q.shape[0] // ROWS):
        start, stop = number * ROWS, (number + 1) * ROWS
        here = slice(start, stop)
        scores = mul(k[:stop], q[here], NT) * scale
        row = lax.broadcasted_iota(jnp.int32, scores.shape, 0)
        col = lax.broadcasted_iota(jnp.int32, scores.shape, 1) + start
        scores = jnp.where(row <= col, scores, big_negative)
        summit = jnp.max(scores, axis=0, keepdims=True)
        exponent = jnp.exp(scores - summit)
        part = jnp.sum(exponent, axis=0, keepdims=True)
        probs = exponent * (1.0 / part)
        prob_grad = mul(v[:stop], grad[here], NT)
        dv[:stop] += mul(probs.astype(BF16), grad[here])
        center = jnp.sum(probs * prob_grad, axis=0, keepdims=True)
        score_grad = (probs * (prob_grad - center)).astype(BF16)
        dk[:stop] += mul(score_grad, q[here])
        query_grad = mul(score_grad, k[:stop], TN) * scale
        out[0, here] = turn(
            query_grad, cosine[here], -ahead[here], -behind[here]
        ).astype(BF16)
    out[1] = turn(dk[...] * scale, cosine[...], -ahead[...], -behind[...]).astype(BF16)
    out[2] = dv[...].astype(BF16)


def part_rows(parts, start, rows):
    for part in parts:
        if start < part.shape[0]:
            return part[start : start + rows]
        start -= part.shape[0]


def up_kernel(shape, place, *refs):
    pieces, refs = group_parts(refs, shape)
    count = len(shape)
    weights, (hidden, slope) = refs[:count], refs[count:]
    for m in range(hidden.shape[0] // ROWS):
        here = slice(m * ROWS, (m + 1) * ROWS)
        total = mul(part_rows(pieces[0], m * ROWS, ROWS), weights[0][...])
        for r in range(1, count):
            total += mul(part_rows(pieces[r], m * ROWS, ROWS), weights[r][...])
        cumulative, density = normal_parts(total)
        hidden[here] = (total * cumulative).astype(BF16)
        slope[here] = (cumulative + total * density).astype(BF16)


def down_kernel(place, hidden, attended, down, out, branch):
    for m in range(hidden.shape[0] // ROWS):
        here = slice(m * ROWS, (m + 1) * ROWS)
        branch[here] = (
            mul(hidden[here], down[...]) + mul(attended[here], out[...])
        ).astype(BF16)


def spans(pieces, rows):
    ins = []
    for parts in pieces:
        before = 0
        for part in parts:
            steps = part.shape[0] // rows

            def block_map(i, p, before=before, steps=steps):
                return (jnp.clip(i - before, 0, steps - 1), 0)

            ins.append((part, (rows, part.shape[1]), block_map))
            before += steps
    return ins


def pick(parts, steps):
    value, before = parts[0][...], 0
    for number in range(1, len(parts)):
        before += steps[number - 1]
        value = jnp.where(pl.program_id(0) < before, value, parts[number][...])
    return value


def middle_kernel(block_steps, cot_steps, width_all, place, *refs):
    block, refs = group_parts(refs, [len(steps) for steps in block_steps])
    cot, refs = group_parts(refs, [len(steps) for steps in cot_steps])
    count = len(block)
    block = [pick(parts, steps) for parts, steps in zip(block, block_steps)]
    cot = [pick(parts, steps) for parts, steps in zip(cot, cot_steps)]
    weights = refs[:count]
    next_weight, seed, factor = refs[count : 3 + count]
    branch_grad, block_grad, next_mix, next_part, mix_part = refs[3 + count :]
    width = block[0].shape[1]

    @pl.when(pl.program_id(0) == 0)
    def _():
        next_part[...] = jnp.zeros_like(next_part)
        mix_part[...] = jnp.zeros_like(mix_part)

    raw = mul(block[0], weights[0][...])
    for r in range(1, count):
        raw += mul(block[r], weights[r][...])
    square = 0.0
    for r in range(count):
        wide = block[r].astype(F32)
        square += jnp.sum(wide * wide, axis=1, keepdims=True)
    root_inv = lax.rsqrt(square / width_all + rms_eps)
    pre_mix = raw * root_inv
    cumulative, density = normal_parts(pre_mix)
    mix_hidden = (pre_mix * cumulative).astype(BF16)
    next_mix[...] = mul(next_weight[...], mix_hidden, (((0,), (1,)), ((), ())))
    next_part[...] += mul(mix_hidden, seed[...], TN)
    hidden_grad = mul(seed[...], next_weight[...], NT)
    pre_grad = (hidden_grad * (cumulative + pre_mix * density)).astype(BF16)
    inner = jnp.sum(pre_grad.astype(F32) * raw, axis=1, keepdims=True) / width_all
    coef = root_inv * root_inv * root_inv * inner
    for r in range(count):
        offset = pl.multiple_of((place[0] ^ r) * width, LANES)
        wide = block[r].astype(F32)
        scaled = (wide * root_inv).astype(BF16)
        mix_part[:, pl.ds(offset, width)] += mul(pre_grad, scaled, TN)
        scaled_grad = mul(pre_grad, weights[r][...], NT)
        total = (
            root_inv * scaled_grad - wide * coef + cot[r].astype(F32) * factor[...]
        )
        branch_grad[:, pl.ds(offset, width)] = total.astype(BF16)
        if r == 0:
            block_grad[...] = total


def down_grad_kernel(hidden_steps, place, hidden, attended, branch_grad, out):
    def work(left):
        turned = left.T
        for m in range(out.shape[1] // 512):
            here = slice(m * 512, (m + 1) * 512)
            out[:, here] = mul(turned, branch_grad[:, here]).astype(BF16)

    j = pl.program_id(0)

    @pl.when(j < hidden_steps)
    def _():
        work(hidden[...])

    @pl.when(j == hidden_steps)
    def _():
        work(attended[...])


def hidden_grad_kernel(place, branch_grad, weight, slope, hidden_grad):
    for m in range(branch_grad.shape[0] // ROWS):
        here = slice(m * ROWS, (m + 1) * ROWS)
        total = mul(branch_grad[here], weight[...], NT)
        hidden_grad[here] = (total * slope[here].astype(F32)).astype(BF16)


def back_kernel(place, grad, weight, out):
    for m in range(grad.shape[0] // ROWS):
        here = slice(m * ROWS, (m + 1) * ROWS)
        out[here] = mul(grad[here], weight[...], NT).astype(BF16)


def weight_grad_kernel(shape, hidden_steps, place, *refs):
    last, refs = group_parts(refs, shape)
    first, refs = group_parts(refs, shape)
    hidden_grad, lin_grad, out, turned = refs
    j, r = pl.program_id(0), pl.program_id(1)
    for k in range(len(shape)):

        @pl.when((j == 0) & (r == k))
        def _():
            turned[k] = joined(last[k]).T

        @pl.when((j >= hidden_steps) & (r == k))
        def _():
            out[...] = mul(joined(first[k]), lin_grad[...], TN).astype(BF16)

    @pl.when(j < hidden_steps)
    def _():
        out[...] = mul(turned[r], hidden_grad[...]).astype(BF16)


def sums_kernel(
    width_all, place, first, last, streams, stats, gain, hist, block_grad, out, norm_part
):
    @pl.when(pl.program_id(0) == 0)
    def _():
        norm_part[...] = jnp.zeros_like(norm_part)

    centers, spreads = center_and_spread(stats[...], width_all)
    terms, plain, other = [], [], []
    for c in range(STREAMS):
        unit = (streams[c] - centers[c]) * spreads[c]
        grad = first[c] if c < STREAMS - 1 else last[...]
        times = grad * unit
        norm_part[c : c + 1] += jnp.sum(times, axis=0, keepdims=True)
        norm_part[STREAMS + c : STREAMS + c + 1] += jnp.sum(grad, axis=0, keepdims=True)
        scaled = grad * gain[c : c + 1]
        plain.append(jnp.sum(scaled, axis=1, keepdims=True))
        other.append(jnp.sum(scaled * unit, axis=1, keepdims=True))
        term = scaled * spreads[c]
        terms.append(term + block_grad[...] if c == STREAMS - 1 else term)
    columns = [None] * (STREAMS * ENTRIES)
    for e in range(ENTRIES):
        entry = hist[e].astype(F32)
        for c in range(STREAMS):
            columns[c * ENTRIES + e] = jnp.sum(terms[c] * entry, axis=1, keepdims=True)
    out[...] = lanes_to_rows(columns + plain + other, out.shape[0])


def history_kernel(
    width_all, place, first, last, streams, stats, gain, sums, coef, block_grad, out
):
    centers, spreads = center_and_spread(stats[...], width_all)
    turned = rows_to_lanes(sums[...])
    grads = []
    for c in range(STREAMS):
        unit = (streams[c] - centers[c]) * spreads[c]
        grad = first[c] if c < STREAMS - 1 else last[...]
        plain = turned[:, c : c + 1] / width_all
        other = turned[:, STREAMS + c : STREAMS + c + 1] / width_all
        value = spreads[c] * (grad * gain[c : c + 1] - plain - unit * other)
        grads.append(value + block_grad[...] if c == STREAMS - 1 else value)
    for e in range(ENTRIES):
        total = coef[:, e : e + 1] * grads[0]
        for c in range(1, STREAMS):
            k = c * ENTRIES + e
            total += coef[:, k : k + 1] * grads[c]
        out[e] = total


def swap(values, axis, bit):
    count = lax.axis_size(axis)
    return lax.ppermute(values, axis, [(i, i ^ bit) for i in range(count)])


def after(value, *earlier):
    return lax.optimization_barrier((value, earlier))[0]


def axis_bits(axis):
    count = lax.axis_size(axis)
    return [1 << b for b in range(count.bit_length() - 1)]


def butterfly_sum(values, axis):
    for bit in axis_bits(axis):
        values = values + swap(values, axis, bit)
    return values


def gather_start(own):
    bits = axis_bits("tensor")
    if len(bits) == 2:
        return own, [swap(own, "tensor", bit) for bit in bits]
    return own, []


def gather_finish(state):
    own, arrived = state
    bits = axis_bits("tensor")
    half = own.shape[-2] // 2
    if len(bits) == 2:
        one, two = arrived
        top = swap(one[..., :half, :], "tensor", 2)
        bottom = swap(two[..., half:, :], "tensor", 1)
        return [[own], [one], [two], [top, bottom]]
    halves = []
    for part, order in ((own[..., :half, :], bits), (own[..., half:, :], bits[::-1])):
        held = {0: part}
        for bit in order:
            keys = list(held)
            got = swap(jnp.stack([held[k] for k in keys]), "tensor", bit)
            for number, k in enumerate(keys):
                held[k ^ bit] = got[number]
        halves.append(held)
    return [[halves[0][k], halves[1][k]] for k in sorted(halves[0])]


def gather_pieces(own):
    return gather_finish(gather_start(own))


def scatter_start(pieces):
    half = pieces.shape[-2] // 2
    bits = axis_bits("tensor")
    states = []
    for number, order in enumerate((bits, bits[::-1])):
        rows = pieces[..., number * half : (number + 1) * half, :]
        held = {k: rows[k] for k in range(pieces.shape[0])}
        states.append((order, held, *scatter_send(held, order[0])))
    return states


def scatter_send(held, bit):
    sent = [k for k in held if k & bit]
    return sent, swap(jnp.stack([held[k] for k in sent]).astype(BF16), "tensor", bit)


def scatter_arrived(states):
    return [state[3] for state in states]


def scatter_finish(states):
    sums = []
    for order, held, sent, got in states:
        for number, bit in enumerate(order):
            if number:
                sent, got = scatter_send(held, bit)
            for spot, k in enumerate(sent):
                held[k ^ bit] = held[k ^ bit].astype(F32) + got[spot].astype(F32)
                del held[k]
        sums.append(held[0])
    return jnp.concatenate(sums, -2)


def scatter_pieces(pieces):
    return scatter_finish(scatter_start(pieces))


def per_device(
    history,
    mix_in,
    group_ids,
    group_weight,
    block_cotangent,
    mix_cotangent,
    qkv_weight,
    out_weight,
    up_weight,
    down_weight,
    norm_gain,
    norm_bias,
    mix_weight,
    next_weight,
):
    count = lax.axis_size("tensor")
    tensor_place = lax.axis_index("tensor")
    dp_place = lax.axis_index("dp")
    tokens, width = history.shape[1:]
    width_all = width * count
    share = norm_gain.shape[1]
    mix_out = mix_weight.shape[1]
    heads_width = qkv_weight.shape[2]
    heads = heads_width // HEAD_DIM
    hidden_width = up_weight.shape[1]
    hidden_steps = hidden_width // heads_width
    place = jnp.stack([tensor_place, dp_place]).astype(jnp.int32)
    call = functools.partial(kernel_call, place=place)

    def other(r, *rest):
        return lambda *g: (g[-1][0] ^ r,) + rest

    cot_state = gather_start(block_cotangent)

    smalls = jnp.concatenate([norm_gain.T, norm_bias.T, mix_weight], 1)
    smalls = lax.all_gather(smalls, "dp", axis=0, tiled=True)
    mix_full = smalls[:, 2 * STREAMS :]
    norm_own = lax.dynamic_slice_in_dim(
        smalls[:, : 2 * STREAMS].astype(F32), tensor_place * width, width, 0
    ).T
    gain_own, bias_own = norm_own[:STREAMS], norm_own[STREAMS:]
    qkv_full = lax.all_gather(qkv_weight, "dp", axis=1, tiled=True)
    up_full = lax.all_gather(up_weight, "dp", axis=0, tiled=True)
    both_full = lax.all_gather(
        jnp.concatenate([down_weight, out_weight], 0), "dp", axis=1, tiled=True
    )

    coef = mix_in.T
    token_steps = tokens // LANES
    hist_in = (history, (ENTRIES, LANES, width), lambda i, p: (0, i, 0))
    coef_in = (coef, (LANES, coef.shape[1]), lambda i, p: (i, 0))
    wide_map = lambda i, p: (0, i, 0)
    row_map = lambda i, p: (0, i)
    streams, stats = call(
        mix_kernel,
        (token_steps,),
        ins=[hist_in, coef_in],
        outs=[
            ((STREAMS, tokens, width), F32, (STREAMS, LANES, width), wide_map),
            ((2 * STREAMS, tokens), F32, (2 * STREAMS, LANES), row_map),
        ],
        name="mix",
        flops=2 * STREAMS * history.size,
    )
    stats = butterfly_sum(after(stats, *cot_state[1]), "tensor")
    cot_pieces = gather_finish(cot_state)
    streams_in = (streams, (STREAMS, LANES, width), wide_map)
    stats_in = (stats, (2 * STREAMS, LANES), row_map)
    gain_in = (gain_own, (STREAMS, width), const(0, 0))
    normed_first, normed_last = call(
        functools.partial(norm_kernel, width_all),
        (token_steps,),
        ins=[streams_in, stats_in, gain_in, (bias_own, (STREAMS, width), const(0, 0))],
        outs=[
            ((STREAMS - 1, tokens, width), BF16, (STREAMS - 1, LANES, width), wide_map),
            ((tokens, width), BF16, (LANES, width), lambda i, p: (i, 0)),
        ],
        name="norm",
    )
    streams_in = (after(streams, normed_last), *streams_in[1:])
    (fixed_part,) = call(
        functools.partial(spread_kernel, width_all),
        (token_steps,),
        ins=[streams_in, stats_in, hist_in],
        outs=[((48, tokens), F32, (48, LANES), row_map)],
        name="spread",
    )
    fixed_sums = butterfly_sum(fixed_part, "tensor")

    first_own, first_arrived = gather_start(normed_first)
    first_arrived = [after(arrived, fixed_part) for arrived in first_arrived]
    first_pieces = gather_finish((first_own, first_arrived))
    last_pieces = gather_pieces(normed_last)
    first_pieces = after(first_pieces, cot_pieces, fixed_sums)

    places = (jnp.arange(tokens, dtype=jnp.int32) % LENGTH).astype(F32)
    freqs = jnp.power(10000.0, -jnp.arange(0, ROT, 2).astype(F32) / ROT)
    angles = places[:, None] * freqs[None, :]
    cosine, sine = jnp.cos(angles), jnp.sin(angles)
    rest = jnp.zeros((tokens, HEAD_DIM - ROT), F32)
    blank = jnp.zeros_like(sine)
    tables = [
        jnp.concatenate([cosine, cosine, rest + 1.0], 1),
        jnp.concatenate([blank, sine, rest], 1),
        jnp.concatenate([-sine, blank, rest], 1),
    ]
    table_ins = [(t, (tokens, HEAD_DIM), const(0, 0)) for t in tables]

    (qkv,) = call(
        functools.partial(qkv_kernel, [len(parts) for parts in first_pieces]),
        (3,),
        ins=[
            (part, (None, *part.shape[1:]), lambda c, p: (c, 0, 0))
            for parts in first_pieces
            for part in parts
        ]
        + [
            (qkv_full, (None, width, heads_width), lambda c, p, r=r: (c, p[0] ^ r, 0))
            for r in range(count)
        ]
        + table_ins,
        outs=[((3, tokens, heads_width), BF16, (None, tokens, heads_width), lambda c, p: (c, 0, 0))],
        name="qkv",
        flops=6 * tokens * width_all * heads_width,
    )
    head_ins = [
        (qkv, (None, tokens, HEAD_DIM), lambda h, p, c=c: (c, 0, h)) for c in range(3)
    ]
    (attended,) = call(
        attend_kernel,
        (heads,),
        ins=head_ins,
        outs=[((tokens, heads_width), BF16, (tokens, HEAD_DIM), lambda h, p: (0, h))],
        name="attend",
        flops=4 * tokens * tokens * heads_width,
    )
    step = min(512, hidden_width)
    hidden, slope = call(
        functools.partial(up_kernel, [len(parts) for parts in last_pieces]),
        (hidden_width // step,),
        ins=[(part, part.shape, const(0, 0)) for parts in last_pieces for part in parts]
        + [(up_full, (width, step), lambda j, p, r=r: (p[0] ^ r, j)) for r in range(count)],
        outs=[((tokens, hidden_width), BF16, (tokens, step), lambda j, p: (0, j))] * 2,
        name="up",
        flops=2 * tokens * width_all * hidden_width,
    )
    member = (group_ids[:, None] == jnp.arange(group_weight.shape[0])[None, :]).astype(F32)
    seq_scale = jnp.sum(member * group_weight[None, :], axis=1)
    seed = (mix_cotangent * jnp.repeat(seq_scale, LENGTH)[None, :]).T.astype(BF16)
    factor = jnp.repeat(seq_scale, LENGTH)[:, None]
    seed, factor, mix_full = lax.optimization_barrier((seed, factor, mix_full))
    hidden = after(hidden, seed, factor, mix_full)
    chunks = 1
    rows = tokens // chunks
    block_owns, block_states, held = [], [], hidden
    for number in range(chunks):
        (branch_pieces,) = call(
            down_kernel,
            (count,),
            ins=[
                (held, (rows, hidden_width), const(number, 0)),
                (attended, (rows, heads_width), const(number, 0)),
                (both_full, (hidden_width, width), lambda r, p: (0, p[0] ^ r)),
                (both_full, (heads_width, width), lambda r, p: (hidden_steps, p[0] ^ r)),
            ],
            outs=[((count, rows, width), BF16, (None, rows, width), lambda r, p: (r, 0, 0))],
            name="down",
            flops=2 * rows * width_all * (hidden_width + heads_width),
        )
        held = after(held, branch_pieces)
        block_states.append(scatter_start(branch_pieces))
    for number in range(chunks):
        residual = streams[STREAMS - 1, number * rows : (number + 1) * rows]
        if number:
            residual = after(residual, *block_states[number - 1][1])
        total = residual + scatter_finish(block_states[number])
        block_owns.append(lax.optimization_barrier(total.astype(BF16)))
        block_states[number] = gather_start(block_owns[number])
    block_chunks = [gather_finish(state) for state in block_states]
    block_own = jnp.concatenate(block_owns, 0)
    block_pieces = [[part for chunk in block_chunks for part in chunk[r]] for r in range(count)]

    mid = min(256, tokens)
    branch_grad, block_grad, next_mix, next_part, mix_part = call(
        functools.partial(
            middle_kernel,
            [[part.shape[0] // mid for part in parts] for parts in block_pieces],
            [[part.shape[0] // mid for part in parts] for parts in cot_pieces],
            width_all,
        ),
        (tokens // mid,),
        ins=spans(block_pieces, mid)
        + spans(cot_pieces, mid)
        + [(mix_full, (width, mix_out), other(r, 0)) for r in range(count)]
        + [
            (next_weight, next_weight.shape, const(0, 0)),
            (seed, (mid, mix_out), lambda i, p: (i, 0)),
            (factor, (mid, 1), lambda i, p: (i, 0)),
        ],
        outs=[
            ((tokens, width_all), BF16, (mid, width_all), lambda i, p: (i, 0)),
            ((tokens, width), F32, (mid, width), lambda i, p: (i, 0)),
            ((mix_out, tokens), F32, (mix_out, mid), row_map),
            ((mix_out, mix_out), F32, (mix_out, mix_out), const(0, 0)),
            ((mix_out, width_all), F32, (mix_out, width_all), const(0, 0)),
        ],
        name="middle",
        flops=6 * tokens * width_all * mix_out,
    )

    last_step = hidden_steps - 1
    mix_rows = -(-mix_out // 16) * 16
    branch_in = (branch_grad, (tokens, width_all), const(0, 0))
    (both_part,) = call(
        functools.partial(down_grad_kernel, hidden_steps),
        (hidden_steps + 1,),
        ins=[
            (hidden, (tokens, heads_width), lambda j, p: (0, jnp.minimum(j, last_step))),
            (attended, (tokens, heads_width), const(0, 0)),
            branch_in,
        ],
        outs=[
            (
                (hidden_width + heads_width + mix_rows, width_all),
                BF16,
                (heads_width, width_all),
                lambda j, p: (j, 0),
            )
        ],
        name="down_grad",
        flops=2 * tokens * width_all * (hidden_width + heads_width),
    )
    both_part = lax.dynamic_update_slice_in_dim(
        both_part,
        jnp.pad(mix_part, ((0, mix_rows - mix_out), (0, 0))).astype(BF16),
        hidden_width + heads_width,
        0,
    )
    branch_grad = after(branch_grad, both_part)
    branch_in = (branch_grad, (tokens, width_all), const(0, 0))
    (attended_grad,) = call(
        back_kernel,
        (1,),
        ins=[
            branch_in,
            (both_full, (heads_width, width_all), const(hidden_steps, 0)),
        ],
        outs=[((tokens, heads_width), BF16, (tokens, heads_width), const(0, 0))],
        name="attended_grad",
        flops=2 * tokens * width_all * heads_width,
    )
    next_bits = axis_bits("dp")
    next_sum = next_part + swap(next_part, "dp", next_bits[0])
    lin_grads = pl.pallas_call(
        attend_back_kernel,
        out_shape=jax.ShapeDtypeStruct((3, tokens, heads_width), BF16),
        grid_spec=pltpu.PrefetchScalarGridSpec(
            num_scalar_prefetch=1,
            grid=(heads,),
            in_specs=[pl.BlockSpec(b, m) for _, b, m in head_ins]
            + [pl.BlockSpec((tokens, HEAD_DIM), lambda h, p: (0, h))]
            + [pl.BlockSpec(b, m) for _, b, m in table_ins],
            out_specs=pl.BlockSpec((3, tokens, HEAD_DIM), lambda h, p: (0, 0, h)),
            scratch_shapes=[pltpu.VMEM((tokens, HEAD_DIM), F32)] * 2,
        ),
        compiler_params=pltpu.CompilerParams(vmem_limit_bytes=VMEM_BYTES),
        cost_estimate=pl.CostEstimate(
            flops=10 * tokens * tokens * heads_width,
            bytes_accessed=8 * tokens * heads_width * 2,
            transcendentals=heads * tokens * tokens,
        ),
        name="attend_back",
    )(place, qkv, qkv, qkv, attended_grad, *tables)
    def qkv_back(grads, begin, end):
        return call(
            back_kernel,
            (end - begin, count),
            ins=[
                (grads, (None, tokens, heads_width), lambda c, r, p: (c + begin, 0, 0)),
                (qkv_full, (None, width, heads_width), lambda c, r, p: (c + begin, p[0] ^ r, 0)),
            ],
            outs=[
                (
                    (count, end - begin, tokens, width),
                    BF16,
                    (None, None, tokens, width),
                    lambda c, r, p: (r, c, 0, 0),
                )
            ],
            name="qkv_back",
            flops=2 * (end - begin) * tokens * width_all * heads_width,
        )[0]

    grads_a = qkv_back(lin_grads, 0, 1)
    states_a = scatter_start(grads_a)
    lin_grads = after(lin_grads, grads_a)
    grads_b = qkv_back(lin_grads, 1, 3)
    states_b = scatter_start(grads_b)
    branch_grad = after(branch_grad, grads_b, next_sum)
    branch_in = (branch_grad, (tokens, width_all), const(0, 0))
    (hidden_grad,) = call(
        hidden_grad_kernel,
        (hidden_steps,),
        ins=[
            branch_in,
            (both_full, (heads_width, width_all), lambda j, p: (j, 0)),
            (slope, (tokens, heads_width), lambda j, p: (0, j)),
        ],
        outs=[((tokens, hidden_width), BF16, (tokens, heads_width), lambda j, p: (0, j))],
        name="hidden_grad",
        flops=2 * tokens * width_all * hidden_width,
    )
    hidden_grad = after(hidden_grad, *scatter_arrived(states_a))
    grad_a = scatter_finish(states_a)
    (last_grads,) = call(
        back_kernel,
        (count,),
        ins=[
            (hidden_grad, (tokens, hidden_width), const(0, 0)),
            (up_full, (width, hidden_width), lambda r, p: (p[0] ^ r, 0)),
        ],
        outs=[((count, tokens, width), BF16, (None, tokens, width), lambda r, p: (r, 0, 0))],
        name="up_back",
        flops=2 * tokens * width_all * hidden_width,
    )
    last_states = scatter_start(last_grads)
    hidden_grad = after(hidden_grad, last_grads)
    for bit in next_bits[1:]:
        next_sum = next_sum + swap(next_sum, "dp", bit)
    all_steps = hidden_steps + 3
    lin_step = lambda j: jnp.maximum(j - hidden_steps, 0)
    (wide_part,) = call(
        functools.partial(
            weight_grad_kernel, [len(parts) for parts in last_pieces], hidden_steps
        ),
        (all_steps, count),
        ins=[(part, part.shape, const(0, 0)) for parts in last_pieces for part in parts]
        + [
            (part, (None, *part.shape[1:]), lambda j, r, p: (lin_step(j), 0, 0))
            for parts in first_pieces
            for part in parts
        ]
        + [
            (
                hidden_grad,
                (tokens, heads_width),
                lambda j, r, p: (0, jnp.minimum(j, hidden_steps - 1)),
            ),
            (lin_grads, (None, tokens, heads_width), lambda j, r, p: (lin_step(j), 0, 0)),
        ],
        outs=[
            (
                (width_all, all_steps * heads_width),
                BF16,
                (width, heads_width),
                lambda j, r, p: (p[0] ^ r, j),
            )
        ],
        name="weight_grad",
        flops=2 * tokens * width_all * (hidden_width + 3 * heads_width),
        scratch=[((count, width, tokens), BF16)],
    )
    wide_part = after(
        wide_part, grad_a, *scatter_arrived(states_b), *scatter_arrived(last_states)
    )
    grad_b = scatter_finish(states_b)
    last_grad = scatter_finish(last_states)
    first_grad = jnp.concatenate([grad_a, grad_b], 0)
    both_grad = lax.psum_scatter(both_part, "dp", scatter_dimension=1, tiled=True).astype(F32)
    out_end = hidden_width + heads_width
    down_grad, out_grad = both_grad[:hidden_width], both_grad[hidden_width:out_end]
    mix_proj_grad = both_grad[out_end : out_end + mix_out].T
    wide_grad = lax.psum_scatter(wide_part, "dp", scatter_dimension=0, tiled=True).astype(F32)
    up_grad = wide_grad[:, :hidden_width]
    qkv_grad = jnp.stack(
        [
            wide_grad[:, hidden_width + c * heads_width : hidden_width + (c + 1) * heads_width]
            for c in range(3)
        ]
    )

    grad_ins = [
        (first_grad, (STREAMS - 1, LANES, width), wide_map),
        (last_grad, (LANES, width), lambda i, p: (i, 0)),
        streams_in,
        stats_in,
        gain_in,
    ]
    block_grad_in = (block_grad, (LANES, width), lambda i, p: (i, 0))
    sums, norm_part = call(
        functools.partial(sums_kernel, width_all),
        (token_steps,),
        ins=grad_ins + [hist_in, block_grad_in],
        outs=[
            ((48, tokens), F32, (48, LANES), row_map),
            ((2 * STREAMS, width), F32, (2 * STREAMS, width), const(0, 0)),
        ],
        name="sums",
    )
    sums = butterfly_sum(sums, "tensor")
    pairs = STREAMS * ENTRIES
    feature_sums = sums[pairs : pairs + 2 * STREAMS]
    (history_grad,) = call(
        functools.partial(history_kernel, width_all),
        (token_steps,),
        ins=grad_ins
        + [(feature_sums, (2 * STREAMS, LANES), row_map), coef_in, block_grad_in],
        outs=[((ENTRIES, tokens, width), F32, (ENTRIES, LANES, width), wide_map)],
        name="history",
    )
    center = stats[:STREAMS] / width_all
    spread = lax.rsqrt(stats[STREAMS:] / width_all - center * center + ln_eps)
    mix_grad = (
        sums[:pairs].reshape(STREAMS, ENTRIES, tokens)
        - (spread * feature_sums[:STREAMS] / width_all)[:, None]
        * fixed_sums[None, pairs : pairs + ENTRIES]
        - (spread * feature_sums[STREAMS:] / width_all)[:, None]
        * fixed_sums[:pairs].reshape(STREAMS, ENTRIES, tokens)
    ).reshape(pairs, tokens)

    norm_part = butterfly_sum(after(norm_part, sums), "dp")
    norm_whole = lax.dynamic_update_slice_in_dim(
        jnp.zeros((2 * STREAMS, width_all), F32), norm_part, tensor_place * width, 1
    )
    norm_whole = butterfly_sum(norm_whole, "tensor")
    norm_whole = lax.dynamic_slice_in_dim(norm_whole, dp_place * share, share, 1)
    next_proj_grad = next_sum
    return (
        block_own,
        next_mix,
        history_grad,
        mix_grad,
        qkv_grad,
        out_grad,
        up_grad,
        down_grad,
        norm_whole[:STREAMS],
        norm_whole[STREAMS:],
        mix_proj_grad,
        next_proj_grad,
    )


def solution(mesh):
    placed = (
        P(None, "dp", "tensor"),
        P(None, "dp"),
        P("dp"),
        P(),
        P("dp", "tensor"),
        P(None, "dp"),
        P(None, "dp", "tensor"),
        P("tensor", "dp"),
        P("dp", "tensor"),
        P("tensor", "dp"),
        P(None, "dp"),
        P(None, "dp"),
        P("dp", None),
        P(),
    )
    return jax.shard_map(
        per_device,
        mesh=mesh,
        in_specs=placed,
        out_specs=(
            P("dp", "tensor"),
            P(None, "dp"),
            P(None, "dp", "tensor"),
            P(None, "dp"),
            P(None, "dp", "tensor"),
            P("tensor", "dp"),
            P("dp", "tensor"),
            P("tensor", "dp"),
            P(None, "dp"),
            P(None, "dp"),
            P("dp", None),
            P(),
        ),
        check_vma=False,
    )
```

time: 777 us -> 729 us (0.938)
  the two profiles are of different devices: /device:TPU:9 before, /device:TPU:0 now
where the time goes in v2:
time: 729 us; the launch traced here: 719 us
  Pallas kernels  287 us (39%)
  waiting for transfers between devices  279 us (38%)
  starting transfers between devices  43.7 us (6%)
  other arithmetic  43.7 us (6%)
  local copies, waits for them, and re-layouts  35.3 us (5%)
  between operations  15.4 us (2%)
  blocking collectives  15.1 us (2%)
    ppermute x46, waiting for transfers between devices, swap(): return lax.ppermute(values, axis, [(i, i ^ bit) for i in range(count)])  278 us
    pallas_call x17, Pallas kernels, kernel_call(): return call(place, *[a for a, _, _ in ins])  269 us
    ppermute x46, starting transfers between devices, swap(): return lax.ppermute(values, axis, [(i, i ^ bit) for i in range(count)])  43.5 us
    pallas_call x1, Pallas kernels, per_device(): pl.pallas_call(attend_back_kernel, out_shape=jax.ShapeDtypeStruct((3, tok...  17.9 us
    all_gather x1, blocking collectives, per_device(): smalls = lax.all_gather(smalls, 'dp', axis=0, tiled=True)  15.1 us
  transfers between devices with their start and end apart: 51, of which 27 were waited for; matrix products, arithmetic and copies ran while one was open for 9% of the time, Pallas kernels for 34%

profile of v2, /device:TPU:0, one launch (start us, length us, event | category | flops | bytes accessed | tf_op | source)
XLA Modules:
  0.0 718.9 jit_solution(5397008915456367004)
XLA Ops:
  8.8 2.2 pad_maximum_fusion.3
  11.0 3.0 collective-permute-start.1
  15.6 15.1 %all_gather.12 = bf16[2048,48]{0,1:T(8,128)(2,1)S(1)} all-gather(bf16[256,48]{0,1:T(8,128)(2,1)S(1)} %pad_maximum_fusion.7), channel_id=1, replica_groups=mesh['dp'=8,'tensor'=4] {'dp'}, dimensions={0}, use_global_device_ids=true | all-gather | bytes 221184 | tf_op jit(solution)/shard_map/all_gather | solution.py:554
  32.3 14.3 %mix.1 = (f32[4,1024,512]{2,1,0:T(8,128)}, f32[8,1024]{1,0:T(8,128)}) custom-call(s32[2]{0:T(128)} %pad_add_fusion.place, bf16[9,1024,512]{2,1,0:T(8,128)(2,1)} %hist.5, f32[1024,36]{1,0:T(8,128)} %bitcast.37), custom_call_target="tpu_custom_call" | custom-call | flops 37748736 | bytes 18006016 | tf_op jit(solution)/shard_map/mix/pallas_call | solution.py:58
  47.0 3.8 collective-permute-done.2
  52.5 3.0 collective-permute-done.3
  56.1 9.6 %norm.1 = (bf16[3,1024,512]{2,1,0:T(8,128)(2,1)}, bf16[1024,512]{1,0:T(8,128)(2,1)}) custom-call(s32[2]{0:T(128)} %pad_add_fusion.place, f32[4,1024,512]{2,1,0:T(8,128)} %get-tuple-element.55.streams, f32[8,1024]{1,0:T(8,128)} %add.235.stats, f32[4,512]{1,0:T(4,128)} %get-tuple-element.104.gain, f32[4,512]{1,0:T(4,128)} %get-tuple-element.103.bias), custom_call_target="tpu_custom_call" | custom-call | bytes 12632064 | tf_op jit(solution)/shard_map/norm/pallas_call | solution.py:58
  68.2 14.8 %spread.1 = f32[48,1024]{1,0:T(8,128)} custom-call(s32[2]{0:T(128)} %pad_add_fusion.place, f32[4,1024,512]{2,1,0:T(8,128)} %get-tuple-element.55.streams, f32[8,1024]{1,0:T(8,128)} %add.235.stats, bf16[9,1024,512]{2,1,0:T(8,128)(2,1)} %hist.5), custom_call_target="tpu_custom_call" | custom-call | bytes 18055168 | tf_op jit(solution)/shard_map/spread/pallas_call | solution.py:58
  83.0 54.0 %collective-permute-done.9.refs_2_.refs_7_ = bf16[3,1024,512]{2,1,0:T(8,128)(2,1)S(1)} collective-permute-done((bf16[3,1024,512]{2,1,0:T(8,128)(2,1)}, bf16[3,1024,512]{2,1,0:T(8,128)(2,1)S(1)}, u32[]{:S(2)}, u32[]{:S(2)}) %collective-permute-start.9) | collective-permute-done | bytes 3145760 | tf_op jit(solution)/shard_map/ppermute | solution.py:431
  146.4 33.9 %collective-permute-done.14 = f32[48,1024]{1,0:T(8,128)} collective-permute-done((f32[48,1024]{1,0:T(8,128)S(1)}, f32[48,1024]{1,0:T(8,128)}, u32[]{:S(2)}, u32[]{:S(2)}) %collective-permute-start.14) | collective-permute-done | bytes 196640 | tf_op jit(solution)/shard_map/ppermute | solution.py:431
  183.6 11.6 %collective-permute-done.15 = f32[48,1024]{1,0:T(8,128)S(1)} collective-permute-done((f32[48,1024]{1,0:T(8,128)S(1)}, f32[48,1024]{1,0:T(8,128)S(1)}, u32[]{:S(2)}, u32[]{:S(2)}) %collective-permute-start.15) | collective-permute-done | bytes 196640 | tf_op jit(solution)/shard_map/ppermute | solution.py:431
  205.6 4.5 collective-permute-done.13.refs_9_
  210.5 15.4 %qkv.1.q.k.v = bf16[3,1024,512]{2,1,0:T(8,128)(2,1)} custom-call(s32[2]{0:T(128)} %pad_add_fusion.place, bf16[3,1024,512]{2,1,0:T(8,128)(2,1)} %get-tuple-element.58.refs_0_.refs_5_, bf16[3,1024,512]{2,1,0:T(8,128)(2,1)} %copy-done.3, bf16[3,1024,512]{2,1,0:T(8,128)(2,1)} %copy-done.2, bf16[3,512,512]{2,1,0:T(8,128)(2,1)} %collective-permute-done.10.refs_3_.refs_8_, ...), custom_call_target="tpu_custom_call" | custom-call | flops 6442450944 | bytes 42467328 | tf_op jit(solution)/shard_map/qkv/pallas_call | solution.py:58
  225.9 11.5 %attend.1.attended = bf16[1024,512]{1,0:T(8,128)(2,1)} custom-call(s32[2]{0:T(128)} %pad_add_fusion.place, bf16[3,1024,512]{2,1,0:T(8,128)(2,1)} %qkv.1.q.k.v, bf16[3,1024,512]{2,1,0:T(8,128)(2,1)} %qkv.1.q.k.v, bf16[3,1024,512]{2,1,0:T(8,128)(2,1)} %qkv.1.q.k.v), custom_call_target="tpu_custom_call" | custom-call | flops 2147483648 | bytes 10485760 | tf_op jit(solution)/shard_map/attend/pallas_call | solution.py:58
  238.4 30.7 %up.1 = (bf16[1024,2048]{1,0:T(8,128)(2,1)}, bf16[1024,2048]{1,0:T(8,128)(2,1)}) custom-call(s32[2]{0:T(128)} %pad_add_fusion.place, bf16[1024,512]{1,0:T(8,128)(2,1)} %get-tuple-element.48.refs_0_, bf16[1024,512]{1,0:T(8,128)(2,1)} %copy-done.7, bf16[1024,512]{1,0:T(8,128)(2,1)} %collective-permute-done.5.refs_2_, bf16[512,512]{1,0:T(8,128)(2,1)} %copy-done.25, ...), custom_call_target="tpu_custom_call" | custom-call | flops 8589934592 | bytes 46137344 | tf_op jit(solution)/shard_map/up/pallas_call | solution.py:58
  269.1 16.5 %down.1 = bf16[4,1024,512]{2,1,0:T(8,128)(2,1)} custom-call(s32[2]{0:T(128)} %pad_add_fusion.place, bf16[1024,2048]{1,0:T(8,128)(2,1)} %get-tuple-element.53.hidden, bf16[1024,512]{1,0:T(8,128)(2,1)} %attend.1.attended, bf16[2560,2048]{1,0:T(8,128)(2,1)} %all-gather.8.cloned.1.call-done.down.out.weight, ...), custom_call_target="tpu_custom_call" | custom-call | flops 10737418240 | bytes 30408704 | tf_op jit(solution)/shard_map/down/pallas_call | solution.py:58
  290.0 19.5 %collective-permute-done.16 = bf16[2,512,512]{2,1,0:T(8,128)(2,1)S(1)} collective-permute-done((bf16[2,512,512]{2,1,0:T(8,128)(2,1)S(1)}, bf16[2,512,512]{2,1,0:T(8,128)(2,1)S(1)}, u32[]{:S(2)}, u32[]{:S(2)}) %collective-permute-start.16) | collective-permute-done | bytes 1048608 | tf_op jit(solution)/shard_map/ppermute | solution.py:431
  312.4 9.3 %collective-permute-done.17 = bf16[1,512,512]{2,1,0:T(8,128)(2,1)S(1)} collective-permute-done((bf16[1,512,512]{2,1,0:T(8,128)(2,1)S(1)}, bf16[1,512,512]{2,1,0:T(8,128)(2,1)S(1)}, u32[]{:S(2)}, u32[]{:S(2)}) %collective-permute-start.17) | collective-permute-done | bytes 524320 | tf_op jit(solution)/shard_map/ppermute | solution.py:431
  323.0 10.3 %collective-permute-done.19 = bf16[1,512,512]{2,1,0:T(8,128)(2,1)S(1)} collective-permute-done((bf16[1,512,512]{2,1,0:T(8,128)(2,1)S(1)}, bf16[1,512,512]{2,1,0:T(8,128)(2,1)S(1)}, u32[]{:S(2)}, u32[]{:S(2)}) %collective-permute-start.19) | collective-permute-done | bytes 524320 | tf_op jit(solution)/shard_map/ppermute | solution.py:431
  333.5 2.0 fusion.refs_0_
  338.2 18.8 %collective-permute-done.21.refs_2_ = bf16[1024,512]{1,0:T(8,128)(2,1)S(1)} collective-permute-done((bf16[1024,512]{1,0:T(8,128)(2,1)S(1)}, bf16[1024,512]{1,0:T(8,128)(2,1)S(1)}, u32[]{:S(2)}, u32[]{:S(2)}) %collective-permute-start.21) | collective-permute-done | bytes 1048608 | tf_op jit(solution)/shard_map/ppermute | solution.py:431
  362.8 6.8 collective-permute-done.23.refs_4_
  370.3 11.4 %middle.1 = (bf16[1024,2048]{1,0:T(8,128)(2,1)}, f32[1024,512]{1,0:T(8,128)}, f32[40,1024]{1,0:T(8,128)}, f32[40,40]{1,0:T(8,128)}, f32[40,2048]{1,0:T(8,128)}) custom-call(s32[2]{0:T(128)} %pad_add_fusion.place, bf16[1024,512]{1,0:T(8,128)(2,1)} %copy-done.6, bf16[1024,512]{1,0:T(8,128)(2,1)} %copy-done.13, bf16[1024,512]{1,0:T(8,128)(2,1)} %copy-done.12, ...), custom_call_target="tpu_custom_call" | custom-call | flops 503316480 | bytes 15922560 | tf_op jit(solution)/shard_map/middle/pallas_call | solution.py:58
  382.7 16.9 %down_grad.1 = bf16[2608,2048]{1,0:T(8,128)(2,1)} custom-call(s32[2]{0:T(128)} %pad_add_fusion.place, bf16[1024,2048]{1,0:T(8,128)(2,1)} %get-tuple-element.53.hidden, bf16[1024,512]{1,0:T(8,128)(2,1)} %attend.1.attended, bf16[1024,2048]{1,0:T(8,128)(2,1)} %get-tuple-element.69.branch_grad.grad), custom_call_target="tpu_custom_call" | custom-call | flops 10737418240 | bytes 20119552 | tf_op jit(solution)/shard_map/down_grad/pallas_call | solution.py:58
  400.3 6.9 attended_grad.1.grad
  407.2 17.9 %attend_back.1.grad.refs_11_ = bf16[3,1024,512]{2,1,0:T(8,128)(2,1)} custom-call(s32[2]{0:T(128)} %pad_add_fusion.place, bf16[3,1024,512]{2,1,0:T(8,128)(2,1)} %qkv.1.q.k.v, bf16[3,1024,512]{2,1,0:T(8,128)(2,1)} %qkv.1.q.k.v, bf16[3,1024,512]{2,1,0:T(8,128)(2,1)} %qkv.1.q.k.v, bf16[1024,512]{1,0:T(8,128)(2,1)} %attended_grad.1.grad, ...), custom_call_target="tpu_custom_call" | custom-call | flops 5368709120 | bytes 8388608 | tf_op jit(solution)/shard_map/attend_back/pallas_call | solution.py:772
  425.0 6.9 qkv_back.2
  436.7 11.5 %qkv_back.3 = bf16[4,2,1024,512]{3,2,1,0:T(8,128)(2,1)} custom-call(s32[2]{0:T(128)} %pad_add_fusion.place, bf16[3,1024,512]{2,1,0:T(8,128)(2,1)} %attend_back.1.grad.refs_11_, bf16[3,2048,512]{2,1,0:T(8,128)(2,1)} %all-gather.6.cloned.1.call-done.refs_5_.refs_6_.refs_7_.refs_8_.weight), custom_call_target="tpu_custom_call" | custom-call | flops 4294967296 | bytes 17825792 | tf_op jit(solution)/shard_map/qkv_back/pallas_call | solution.py:58
  455.4 15.1 %hidden_grad.1.grad.refs_10_ = bf16[1024,2048]{1,0:T(8,128)(2,1)} custom-call(s32[2]{0:T(128)} %pad_add_fusion.place, bf16[1024,2048]{1,0:T(8,128)(2,1)} %get-tuple-element.69.branch_grad.grad, bf16[2560,2048]{1,0:T(8,128)(2,1)} %all-gather.8.cloned.1.call-done.down.out.weight, bf16[1024,2048]{1,0:T(8,128)(2,1)} %get-tuple-element.70.slope), custom_call_target="tpu_custom_call" | custom-call | flops 8589934592 | bytes 23068672 | tf_op jit(solution)/shard_map/hidden_grad/pallas_call | solution.py:58
  470.6 14.1 %up_back.1 = bf16[4,1024,512]{2,1,0:T(8,128)(2,1)} custom-call(s32[2]{0:T(128)} %pad_add_fusion.place, bf16[1024,2048]{1,0:T(8,128)(2,1)} %hidden_grad.1.grad.refs_10_, bf16[2048,2048]{1,0:T(8,128)(2,1)} %all-gather.4.cloned.1.call-done.refs_5_.refs_6_.refs_7_.refs_8_.weight), custom_call_target="tpu_custom_call" | custom-call | flops 8589934592 | bytes 16777216 | tf_op jit(solution)/shard_map/up_back/pallas_call | solution.py:58
  489.9 35.8 %weight_grad.1 = bf16[2048,3584]{1,0:T(8,128)(2,1)} custom-call(s32[2]{0:T(128)} %pad_add_fusion.place, bf16[1024,512]{1,0:T(8,128)(2,1)} %get-tuple-element.48.refs_0_, bf16[1024,512]{1,0:T(8,128)(2,1)} %copy-done.7, bf16[1024,512]{1,0:T(8,128)(2,1)} %collective-permute-done.5.refs_2_, bf16[512,512]{1,0:T(8,128)(2,1)} %copy-done.25, ...), custom_call_target="tpu_custom_call" | custom-call | flops 15032385536 | bytes 38797312 | tf_op jit(solution)/shard_map/weight_grad/pallas_call | solution.py:58
  525.8 2.1 collective-permute-done.33
  536.1 32.2 %collective-permute-done.25 = bf16[1,1,512,512]{3,2,1,0:T(8,128)(2,1)S(1)} collective-permute-done((bf16[1,1,512,512]{3,2,1,0:T(8,128)(2,1)S(1)}, bf16[1,1,512,512]{3,2,1,0:T(8,128)(2,1)S(1)}, u32[]{:S(2)}, u32[]{:S(2)}) %collective-permute-start.25) | collective-permute-done | bytes 524320 | tf_op jit(solution)/shard_map/ppermute | solution.py:431
  570.6 2.9 add_bitcast_fusion.1
  575.0 2.9 collective-permute-done.34
  580.2 4.5 collective-permute-done.27
  586.0 28.3 %collective-permute-done.36 = bf16[1,512,512]{2,1,0:T(8,128)(2,1)S(1)} collective-permute-done((bf16[1,512,512]{2,1,0:T(8,128)(2,1)S(1)}, bf16[1,512,512]{2,1,0:T(8,128)(2,1)S(1)}, u32[]{:S(2)}, u32[]{:S(2)}) %collective-permute-start.36) | collective-permute-done | bytes 524320 | tf_op jit(solution)/shard_map/ppermute | solution.py:431
  619.0 3.1 maximum_maximum_fusion.first
  622.1 18.1 %sums.1 = (f32[48,1024]{1,0:T(8,128)}, f32[8,512]{1,0:T(8,128)}) custom-call(s32[2]{0:T(128)} %pad_add_fusion.place, f32[3,1024,512]{2,1,0:T(8,128)} %maximum_maximum_fusion.first, f32[1024,512]{1,0:T(8,128)} %pad_maximum_fusion.1.last, f32[4,1024,512]{2,1,0:T(8,128)} %get-tuple-element.55.streams, f32[8,1024]{1,0:T(8,128)} %add.235.stats, ...), custom_call_target="tpu_custom_call" | custom-call | bytes 28565504 | tf_op jit(solution)/shard_map/sums/pallas_call | solution.py:58
  640.9 5.2 collective-permute-done.37
  647.6 5.2 collective-permute-done.38
  655.0 3.2 collective-permute-start.40
  658.2 4.4 collective-permute-done.44
  663.8 4.6 collective-permute-done.45
  669.8 4.6 collective-permute-done.41
  675.5 3.3 collective-permute-done.42
  681.1 19.3 %history.1 = f32[9,1024,512]{2,1,0:T(8,128)} custom-call(s32[2]{0:T(128)} %pad_add_fusion.place, f32[3,1024,512]{2,1,0:T(8,128)} %maximum_maximum_fusion.first, f32[1024,512]{1,0:T(8,128)} %pad_maximum_fusion.1.last, f32[4,1024,512]{2,1,0:T(8,128)} %get-tuple-element.55.streams, f32[8,1024]{1,0:T(8,128)} %add.235.stats, f32[4,512]{1,0:T(4,128)} %get-tuple-element.104.gain, ...), custom_call_target="tpu_custom_call" | custom-call | bytes 37969920 | tf_op jit(solution)/shard_map/history/pallas_call | solution.py:58
  702.8 2.8 slice.397
  (237 shorter events, 109.6 us)
Async XLA Ops:
  7.2 203.3 %all-gather.6.cloned.1.call-start = ((), (), s32[]{:S(2)}) async-start(), calls=%async_computation.3 | async-start | bytes 7077888 | tf_op jit(solution)/shard_map/all_gather | solution.py:560
  7.9 229.5 %all-gather.4.cloned.1.call-start = ((), (), s32[]{:S(2)}) async-start(), calls=%async_computation.2 | async-start | bytes 9437184 | tf_op jit(solution)/shard_map/all_gather | solution.py:561
  8.7 260.4 %all-gather.8.cloned.1.call-start = ((), (), s32[]{:S(2)}) async-start(), calls=%async_computation.4 | async-start | bytes 11796480 | tf_op jit(solution)/shard_map/all_gather | solution.py:562
  11.0 690.0 %reduce-scatter.5.cloned.1.call-start = ((), (), s32[]{:S(2)}) async-start(), calls=%async_computation.6 | async-start | bytes 12017664 | tf_op jit(solution)/shard_map/reduce_scatter | solution.py:887
  11.0 35.6 %collective-permute-start.1 = (bf16[1024,512]{1,0:T(8,128)(2,1)S(1)}, bf16[1024,512]{1,0:T(8,128)(2,1)S(1)}, u32[]{:S(2)}, u32[]{:S(2)}) collective-permute-start(bf16[1024,512]{1,0:T(8,128)(2,1)S(1)} %copy-done.21), channel_id=1, source_target_pairs={{0,2},{1,3},{2,0},{3,1},{4,6},{5,7},{6,4},{7,5},{8,10},{9,11},{10,... | collective-permute-start | bytes 3145736 | tf_op jit(solution)/shard_map/ppermute | solution.py:431
  14.1 32.5 %collective-permute-start = (bf16[1024,512]{1,0:T(8,128)(2,1)S(1)}, bf16[1024,512]{1,0:T(8,128)(2,1)S(1)}, u32[]{:S(2)}, u32[]{:S(2)}) collective-permute-start(bf16[1024,512]{1,0:T(8,128)(2,1)S(1)} %copy-done.21), channel_id=1, source_target_pairs={{0,1},{1,0},{2,3},{3,2},{4,5},{5,4},{6,7},{7,6},{8,9},{9,8},{10,11... | collective-permute-start | bytes 3145736 | tf_op jit(solution)/shard_map/ppermute | solution.py:431
  65.7 71.3 %collective-permute-start.9 = (bf16[3,1024,512]{2,1,0:T(8,128)(2,1)}, bf16[3,1024,512]{2,1,0:T(8,128)(2,1)S(1)}, u32[]{:S(2)}, u32[]{:S(2)}) collective-permute-start(bf16[3,1024,512]{2,1,0:T(8,128)(2,1)} %get-tuple-element.58.refs_0_.refs_5_), channel_id=1, source_target_pairs={{0,2},{1,3},{2,0},{3,1},{4,6},{5,7},{6,4},{7,5},{8,10},{9,11},{10,... | collective-permute-start | bytes 9437192 | tf_op jit(solution)/shard_map/ppermute | solution.py:431
  66.1 72.6 %collective-permute-start.8 = (bf16[3,1024,512]{2,1,0:T(8,128)(2,1)}, bf16[3,1024,512]{2,1,0:T(8,128)(2,1)S(1)}, u32[]{:S(2)}, u32[]{:S(2)}) collective-permute-start(bf16[3,1024,512]{2,1,0:T(8,128)(2,1)} %get-tuple-element.58.refs_0_.refs_5_), channel_id=1, source_target_pairs={{0,1},{1,0},{2,3},{3,2},{4,5},{5,4},{6,7},{7,6},{8,9},{9,8},{10,11... | collective-permute-start | bytes 9437192 | tf_op jit(solution)/shard_map/ppermute | solution.py:431
  66.5 129.1 %collective-permute-start.5 = (bf16[1024,512]{1,0:T(8,128)(2,1)}, bf16[1024,512]{1,0:T(8,128)(2,1)}, u32[]{:S(2)}, u32[]{:S(2)}) collective-permute-start(bf16[1024,512]{1,0:T(8,128)(2,1)} %get-tuple-element.48.refs_0_), channel_id=1, source_target_pairs={{0,2},{1,3},{2,0},{3,1},{4,6},{5,7},{6,4},{7,5},{8,10},{9,11},{10,... | collective-permute-start | bytes 3145736 | tf_op jit(solution)/shard_map/ppermute | solution.py:431
  138.4 72.1 %collective-permute-start.11 = (bf16[3,512,512]{2,1,0:T(8,128)(2,1)}, bf16[3,512,512]{2,1,0:T(8,128)(2,1)}, u32[]{:S(2)}, u32[]{:S(2)}) collective-permute-start(bf16[3,512,512]{2,1,0:T(8,128)(2,1)} %slice.272), channel_id=1, source_target_pairs={{0,1},{1,0},{2,3},{3,2},{4,5},{5,4},{6,7},{7,6},{8,9},{9,8},{10,11... | collective-permute-start | bytes 4718600 | tf_op jit(solution)/shard_map/ppermute | solution.py:431
  140.0 70.5 %collective-permute-start.10 = (bf16[3,512,512]{2,1,0:T(8,128)(2,1)}, bf16[3,512,512]{2,1,0:T(8,128)(2,1)}, u32[]{:S(2)}, u32[]{:S(2)}) collective-permute-start(bf16[3,512,512]{2,1,0:T(8,128)(2,1)} %slice.271), channel_id=1, source_target_pairs={{0,2},{1,3},{2,0},{3,1},{4,6},{5,7},{6,4},{7,5},{8,10},{9,11},{10,... | collective-permute-start | bytes 4718600 | tf_op jit(solution)/shard_map/ppermute | solution.py:431
  142.4 37.8 %collective-permute-start.14 = (f32[48,1024]{1,0:T(8,128)S(1)}, f32[48,1024]{1,0:T(8,128)}, u32[]{:S(2)}, u32[]{:S(2)}) collective-permute-start(f32[48,1024]{1,0:T(8,128)S(1)} %copy-done.23), channel_id=1, source_target_pairs={{0,1},{1,0},{2,3},{3,2},{4,5},{5,4},{6,7},{7,6},{8,9},{9,8},{10,11... | collective-permute-start | bytes 589832 | tf_op jit(solution)/shard_map/ppermute | solution.py:431
  144.1 59.1 %collective-permute-start.4 = (bf16[1024,512]{1,0:T(8,128)(2,1)}, bf16[1024,512]{1,0:T(8,128)(2,1)S(1)}, u32[]{:S(2)}, u32[]{:S(2)}) collective-permute-start(bf16[1024,512]{1,0:T(8,128)(2,1)} %get-tuple-element.48.refs_0_), channel_id=1, source_target_pairs={{0,1},{1,0},{2,3},{3,2},{4,5},{5,4},{6,7},{7,6},{8,9},{9,8},{10,11... | collective-permute-start | bytes 3145736 | tf_op jit(solution)/shard_map/ppermute | solution.py:431
  181.2 14.0 %collective-permute-start.15 = (f32[48,1024]{1,0:T(8,128)S(1)}, f32[48,1024]{1,0:T(8,128)S(1)}, u32[]{:S(2)}, u32[]{:S(2)}) collective-permute-start(f32[48,1024]{1,0:T(8,128)S(1)} %add.237), channel_id=1, source_target_pairs={{0,2},{1,3},{2,0},{3,1},{4,6},{5,7},{6,4},{7,5},{8,10},{9,11},{10,... | collective-permute-start | bytes 589832 | tf_op jit(solution)/shard_map/ppermute | solution.py:431
  195.2 14.9 %collective-permute-start.13 = (bf16[512,512]{1,0:T(8,128)(2,1)S(1)}, bf16[512,512]{1,0:T(8,128)(2,1)}, u32[]{:S(2)}, u32[]{:S(2)}) collective-permute-start(bf16[512,512]{1,0:T(8,128)(2,1)S(1)} %slice.341), channel_id=1, source_target_pairs={{0,1},{1,0},{2,3},{3,2},{4,5},{5,4},{6,7},{7,6},{8,9},{9,8},{10,11... | collective-permute-start | bytes 1572872 | tf_op jit(solution)/shard_map/ppermute | solution.py:431
  195.6 14.9 %collective-permute-start.12 = (bf16[512,512]{1,0:T(8,128)(2,1)S(1)}, bf16[512,512]{1,0:T(8,128)(2,1)S(1)}, u32[]{:S(2)}, u32[]{:S(2)}) collective-permute-start(bf16[512,512]{1,0:T(8,128)(2,1)S(1)} %slice.340), channel_id=1, source_target_pairs={{0,2},{1,3},{2,0},{3,1},{4,6},{5,7},{6,4},{7,5},{8,10},{9,11},{10,... | collective-permute-start | bytes 1572872 | tf_op jit(solution)/shard_map/ppermute | solution.py:431
  203.2 34.2 %collective-permute-start.7 = (bf16[512,512]{1,0:T(8,128)(2,1)}, bf16[512,512]{1,0:T(8,128)(2,1)S(1)}, u32[]{:S(2)}, u32[]{:S(2)}) collective-permute-start(bf16[512,512]{1,0:T(8,128)(2,1)} %slice.338), channel_id=1, source_target_pairs={{0,1},{1,0},{2,3},{3,2},{4,5},{5,4},{6,7},{7,6},{8,9},{9,8},{10,11... | collective-permute-start | bytes 1572872 | tf_op jit(solution)/shard_map/ppermute | solution.py:431
  210.2 27.3 %collective-permute-start.6 = (bf16[512,512]{1,0:T(8,128)(2,1)}, bf16[512,512]{1,0:T(8,128)(2,1)S(1)}, u32[]{:S(2)}, u32[]{:S(2)}) collective-permute-start(bf16[512,512]{1,0:T(8,128)(2,1)} %slice.337), channel_id=1, source_target_pairs={{0,2},{1,3},{2,0},{3,1},{4,6},{5,7},{6,4},{7,5},{8,10},{9,11},{10,... | collective-permute-start | bytes 1572872 | tf_op jit(solution)/shard_map/ppermute | solution.py:431
  287.2 22.3 %collective-permute-start.16 = (bf16[2,512,512]{2,1,0:T(8,128)(2,1)S(1)}, bf16[2,512,512]{2,1,0:T(8,128)(2,1)S(1)}, u32[]{:S(2)}, u32[]{:S(2)}) collective-permute-start(bf16[2,512,512]{2,1,0:T(8,128)(2,1)S(1)} %pad_maximum_fusion.4), channel_id=1, source_target_pairs={{0,1},{1,0},{2,3},{3,2},{4,5},{5,4},{6,7},{7,6},{8,9},{9,8},{10,11... | collective-permute-start | bytes 3145736 | tf_op jit(solution)/shard_map/ppermute | solution.py:431
  288.2 24.2 %collective-permute-start.18 = (bf16[2,512,512]{2,1,0:T(8,128)(2,1)S(1)}, bf16[2,512,512]{2,1,0:T(8,128)(2,1)S(1)}, u32[]{:S(2)}, u32[]{:S(2)}) collective-permute-start(bf16[2,512,512]{2,1,0:T(8,128)(2,1)S(1)} %stack.68), channel_id=1, source_target_pairs={{0,2},{1,3},{2,0},{3,1},{4,6},{5,7},{6,4},{7,5},{8,10},{9,11},{10,... | collective-permute-start | bytes 3145736 | tf_op jit(solution)/shard_map/ppermute | solution.py:431
  309.6 12.1 %collective-permute-start.17 = (bf16[1,512,512]{2,1,0:T(8,128)(2,1)S(1)}, bf16[1,512,512]{2,1,0:T(8,128)(2,1)S(1)}, u32[]{:S(2)}, u32[]{:S(2)}) collective-permute-start(bf16[1,512,512]{2,1,0:T(8,128)(2,1)S(1)} %add_convert_fusion.7), channel_id=1, source_target_pairs={{0,2},{1,3},{2,0},{3,1},{4,6},{5,7},{6,4},{7,5},{8,10},{9,11},{10,... | collective-permute-start | bytes 1572872 | tf_op jit(solution)/shard_map/ppermute | solution.py:431
  322.1 11.2 %collective-permute-start.19 = (bf16[1,512,512]{2,1,0:T(8,128)(2,1)S(1)}, bf16[1,512,512]{2,1,0:T(8,128)(2,1)S(1)}, u32[]{:S(2)}, u32[]{:S(2)}) collective-permute-start(bf16[1,512,512]{2,1,0:T(8,128)(2,1)S(1)} %get-tuple-element.93), channel_id=1, source_target_pairs={{0,1},{1,0},{2,3},{3,2},{4,5},{5,4},{6,7},{7,6},{8,9},{9,8},{10,11... | collective-permute-start | bytes 1572872 | tf_op jit(solution)/shard_map/ppermute | solution.py:431
  335.5 21.5 %collective-permute-start.21 = (bf16[1024,512]{1,0:T(8,128)(2,1)S(1)}, bf16[1024,512]{1,0:T(8,128)(2,1)S(1)}, u32[]{:S(2)}, u32[]{:S(2)}) collective-permute-start(bf16[1024,512]{1,0:T(8,128)(2,1)S(1)} %fusion.refs_0_), channel_id=1, source_target_pairs={{0,2},{1,3},{2,0},{3,1},{4,6},{5,7},{6,4},{7,5},{8,10},{9,11},{10,... | collective-permute-start | bytes 3145736 | tf_op jit(solution)/shard_map/ppermute | solution.py:431
  337.1 22.8 %collective-permute-start.20 = (bf16[1024,512]{1,0:T(8,128)(2,1)S(1)}, bf16[1024,512]{1,0:T(8,128)(2,1)S(1)}, u32[]{:S(2)}, u32[]{:S(2)}) collective-permute-start(bf16[1024,512]{1,0:T(8,128)(2,1)S(1)} %fusion.refs_0_), channel_id=1, source_target_pairs={{0,1},{1,0},{2,3},{3,2},{4,5},{5,4},{6,7},{7,6},{8,9},{9,8},{10,11... | collective-permute-start | bytes 3145736 | tf_op jit(solution)/shard_map/ppermute | solution.py:431
  358.0 11.6 %collective-permute-start.23 = (bf16[512,512]{1,0:T(8,128)(2,1)}, bf16[512,512]{1,0:T(8,128)(2,1)}, u32[]{:S(2)}, u32[]{:S(2)}) collective-permute-start(bf16[512,512]{1,0:T(8,128)(2,1)} %slice.353), channel_id=1, source_target_pairs={{0,1},{1,0},{2,3},{3,2},{4,5},{5,4},{6,7},{7,6},{8,9},{9,8},{10,11... | collective-permute-start | bytes 1572872 | tf_op jit(solution)/shard_map/ppermute | solution.py:431
  360.8 9.5 %collective-permute-start.22 = (bf16[512,512]{1,0:T(8,128)(2,1)}, bf16[512,512]{1,0:T(8,128)(2,1)}, u32[]{:S(2)}, u32[]{:S(2)}) collective-permute-start(bf16[512,512]{1,0:T(8,128)(2,1)} %slice.352), channel_id=1, source_target_pairs={{0,2},{1,3},{2,0},{3,1},{4,6},{5,7},{6,4},{7,5},{8,10},{9,11},{10,... | collective-permute-start | bytes 1572872 | tf_op jit(solution)/shard_map/ppermute | solution.py:431
  400.2 306.2 %reduce-scatter.3.cloned.1.call-start = ((), (), s32[]{:S(2)}) async-start(), calls=%async_computation.5 | async-start | bytes 16515072 | tf_op jit(solution)/shard_map/reduce_scatter | solution.py:891
  433.2 22.2 %collective-permute-start.32 = (f32[40,40]{1,0:T(8,128)S(1)}, f32[40,40]{1,0:T(8,128)S(1)}, u32[]{:S(2)}, u32[]{:S(2)}) collective-permute-start(f32[40,40]{1,0:T(8,128)S(1)} %copy-done.29), channel_id=1, source_target_pairs={{0,4},{4,0},{8,12},{12,8},{16,20},{20,16},{24,28},{28,24},{1,5},{5... | collective-permute-start | bytes 19208 | tf_op jit(solution)/shard_map/ppermute | solution.py:431
  434.7 35.8 %collective-permute-start.24 = (bf16[2,1,512,512]{3,2,1,0:T(8,128)(2,1)S(1)}, bf16[2,1,512,512]{3,2,1,0:T(8,128)(2,1)S(1)}, u32[]{:S(2)}, u32[]{:S(2)}) collective-permute-start(bf16[2,1,512,512]{3,2,1,0:T(8,128)(2,1)S(1)} %pad_maximum_fusion.5), channel_id=1, source_target_pairs={{0,1},{1,0},{2,3},{3,2},{4,5},{5,4},{6,7},{7,6},{8,9},{9,8},{10,11... | collective-permute-start | bytes 3145736 | tf_op jit(solution)/shard_map/ppermute | solution.py:431
  436.1 34.5 %collective-permute-start.26 = (bf16[2,1,512,512]{3,2,1,0:T(8,128)(2,1)S(1)}, bf16[2,1,512,512]{3,2,1,0:T(8,128)(2,1)S(1)}, u32[]{:S(2)}, u32[]{:S(2)}) collective-permute-start(bf16[2,1,512,512]{3,2,1,0:T(8,128)(2,1)S(1)} %stack.69), channel_id=1, source_target_pairs={{0,2},{1,3},{2,0},{3,1},{4,6},{5,7},{6,4},{7,5},{8,10},{9,11},{10,... | collective-permute-start | bytes 3145736 | tf_op jit(solution)/shard_map/ppermute | solution.py:431
  453.1 72.7 %collective-permute-start.28 = (bf16[2,2,512,512]{3,2,1,0:T(8,128)(2,1)}, bf16[2,2,512,512]{3,2,1,0:T(8,128)(2,1)}, u32[]{:S(2)}, u32[]{:S(2)}) collective-permute-start(bf16[2,2,512,512]{3,2,1,0:T(8,128)(2,1)} %pad_maximum_fusion), channel_id=1, source_target_pairs={{0,1},{1,0},{2,3},{3,2},{4,5},{5,4},{6,7},{7,6},{8,9},{9,8},{10,11... | collective-permute-start | bytes 6291464 | tf_op jit(solution)/shard_map/ppermute | solution.py:431
  454.5 71.2 %collective-permute-start.30 = (bf16[2,2,512,512]{3,2,1,0:T(8,128)(2,1)S(1)}, bf16[2,2,512,512]{3,2,1,0:T(8,128)(2,1)}, u32[]{:S(2)}, u32[]{:S(2)}) collective-permute-start(bf16[2,2,512,512]{3,2,1,0:T(8,128)(2,1)S(1)} %stack.70), channel_id=1, source_target_pairs={{0,2},{1,3},{2,0},{3,1},{4,6},{5,7},{6,4},{7,5},{8,10},{9,11},{10,... | collective-permute-start | bytes 6291464 | tf_op jit(solution)/shard_map/ppermute | solution.py:431
  488.3 39.5 %collective-permute-start.33 = (bf16[2,512,512]{2,1,0:T(8,128)(2,1)}, bf16[2,512,512]{2,1,0:T(8,128)(2,1)}, u32[]{:S(2)}, u32[]{:S(2)}) collective-permute-start(bf16[2,512,512]{2,1,0:T(8,128)(2,1)} %pad_maximum_fusion.6), channel_id=1, source_target_pairs={{0,1},{1,0},{2,3},{3,2},{4,5},{5,4},{6,7},{7,6},{8,9},{9,8},{10,11... | collective-permute-start | bytes 3145736 | tf_op jit(solution)/shard_map/ppermute | solution.py:431
  489.5 39.3 %collective-permute-start.35 = (bf16[2,512,512]{2,1,0:T(8,128)(2,1)S(1)}, bf16[2,512,512]{2,1,0:T(8,128)(2,1)}, u32[]{:S(2)}, u32[]{:S(2)}) collective-permute-start(bf16[2,512,512]{2,1,0:T(8,128)(2,1)S(1)} %stack.71), channel_id=1, source_target_pairs={{0,2},{1,3},{2,0},{3,1},{4,6},{5,7},{6,4},{7,5},{8,10},{9,11},{10,... | collective-permute-start | bytes 3145736 | tf_op jit(solution)/shard_map/ppermute | solution.py:431
  530.9 39.8 %collective-permute-start.29 = (bf16[1,2,512,512]{3,2,1,0:T(8,128)(2,1)S(1)}, bf16[1,2,512,512]{3,2,1,0:T(8,128)(2,1)S(1)}, u32[]{:S(2)}, u32[]{:S(2)}) collective-permute-start(bf16[1,2,512,512]{3,2,1,0:T(8,128)(2,1)S(1)} %add_convert_fusion.1), channel_id=1, source_target_pairs={{0,2},{1,3},{2,0},{3,1},{4,6},{5,7},{6,4},{7,5},{8,10},{9,11},{10,... | collective-permute-start | bytes 3145736 | tf_op jit(solution)/shard_map/ppermute | solution.py:431
  532.7 35.5 %collective-permute-start.25 = (bf16[1,1,512,512]{3,2,1,0:T(8,128)(2,1)S(1)}, bf16[1,1,512,512]{3,2,1,0:T(8,128)(2,1)S(1)}, u32[]{:S(2)}, u32[]{:S(2)}) collective-permute-start(bf16[1,1,512,512]{3,2,1,0:T(8,128)(2,1)S(1)} %add_convert_fusion.5), channel_id=1, source_target_pairs={{0,2},{1,3},{2,0},{3,1},{4,6},{5,7},{6,4},{7,5},{8,10},{9,11},{10,... | collective-permute-start | bytes 1572872 | tf_op jit(solution)/shard_map/ppermute | solution.py:431
  535.5 42.3 %collective-permute-start.34 = (bf16[1,512,512]{2,1,0:T(8,128)(2,1)S(1)}, bf16[1,512,512]{2,1,0:T(8,128)(2,1)S(1)}, u32[]{:S(2)}, u32[]{:S(2)}) collective-permute-start(bf16[1,512,512]{2,1,0:T(8,128)(2,1)S(1)} %add_convert_fusion.3), channel_id=1, source_target_pairs={{0,2},{1,3},{2,0},{3,1},{4,6},{5,7},{6,4},{7,5},{8,10},{9,11},{10,... | collective-permute-start | bytes 1572872 | tf_op jit(solution)/shard_map/ppermute | solution.py:431
  569.8 14.9 %collective-permute-start.27 = (bf16[1,1,512,512]{3,2,1,0:T(8,128)(2,1)S(1)}, bf16[1,1,512,512]{3,2,1,0:T(8,128)(2,1)S(1)}, u32[]{:S(2)}, u32[]{:S(2)}) collective-permute-start(bf16[1,1,512,512]{3,2,1,0:T(8,128)(2,1)S(1)} %get-tuple-element.89), channel_id=1, source_target_pairs={{0,1},{1,0},{2,3},{3,2},{4,5},{5,4},{6,7},{7,6},{8,9},{9,8},{10,11... | collective-permute-start | bytes 1572872 | tf_op jit(solution)/shard_map/ppermute | solution.py:431
  573.6 43.5 %collective-permute-start.31 = (bf16[1,2,512,512]{3,2,1,0:T(8,128)(2,1)S(1)}, bf16[1,2,512,512]{3,2,1,0:T(8,128)(2,1)S(1)}, u32[]{:S(2)}, u32[]{:S(2)}) collective-permute-start(bf16[1,2,512,512]{3,2,1,0:T(8,128)(2,1)S(1)} %get-tuple-element.81), channel_id=1, source_target_pairs={{0,1},{1,0},{2,3},{3,2},{4,5},{5,4},{6,7},{7,6},{8,9},{9,8},{10,11... | collective-permute-start | bytes 3145736 | tf_op jit(solution)/shard_map/ppermute | solution.py:431
  579.4 35.0 %collective-permute-start.36 = (bf16[1,512,512]{2,1,0:T(8,128)(2,1)S(1)}, bf16[1,512,512]{2,1,0:T(8,128)(2,1)S(1)}, u32[]{:S(2)}, u32[]{:S(2)}) collective-permute-start(bf16[1,512,512]{2,1,0:T(8,128)(2,1)S(1)} %get-tuple-element.85), channel_id=1, source_target_pairs={{0,1},{1,0},{2,3},{3,2},{4,5},{5,4},{6,7},{7,6},{8,9},{9,8},{10,11... | collective-permute-start | bytes 1572872 | tf_op jit(solution)/shard_map/ppermute | solution.py:431
  640.2 5.9 collective-permute-start.37
  647.0 5.7 collective-permute-start.38
  655.0 14.0 %collective-permute-start.40 = (f32[8,512]{1,0:T(8,128)S(1)}, f32[8,512]{1,0:T(8,128)S(1)}, u32[]{:S(2)}, u32[]{:S(2)}) collective-permute-start(f32[8,512]{1,0:T(8,128)S(1)} %add.279), channel_id=1, source_target_pairs={{0,8},{4,12},{8,0},{12,4},{16,24},{20,28},{24,16},{28,20},{1,9},{5... | collective-permute-start | bytes 49160 | tf_op jit(solution)/shard_map/ppermute | solution.py:431
  658.2 4.4 collective-permute-start.44
  662.7 5.7 collective-permute-start.45
  669.0 5.4 collective-permute-start.41
  674.5 4.3 collective-permute-start.42
  678.8 21.6 %collective-permute-start.43 = (f32[8,2048]{1,0:T(8,128)S(1)}, f32[8,2048]{1,0:T(8,128)S(1)}, u32[]{:S(2)}, u32[]{:S(2)}) collective-permute-start(f32[8,2048]{1,0:T(8,128)S(1)} %add_dynamic-update-slice_fusion), channel_id=1, source_target_pairs={{0,2},{1,3},{2,0},{3,1},{4,6},{5,7},{6,4},{7,5},{8,10},{9,11},{10,... | collective-permute-start | bytes 196616 | tf_op jit(solution)/shard_map/ppermute | solution.py:431
  (37 other events, 662.9 us)
Sparse Core Ops, SparseCore 0:
  9.6 68.0 all-gather.5
  79.4 80.7 all-gather.3
  162.3 98.3 all-gather.7
  400.4 111.6 reduce-scatter.4
  529.0 150.6 reduce-scatter.2

commit v3 on v2

--- a/solution.py
+++ b/solution.py
@@ -485,34 +485,52 @@
     for number, order in enumerate((bits, bits[::-1])):
         rows = pieces[..., number * half : (number + 1) * half, :]
         held = {k: rows[k] for k in range(pieces.shape[0])}
-        states.append((order, held, *scatter_send(held, order[0])))
+        states.append([held, *scatter_send(held, order[0])])
     return states
 
 
 def scatter_send(held, bit):
     sent = [k for k in held if k & bit]
-    return sent, swap(jnp.stack([held[k] for k in sent]).astype(BF16), "tensor", bit)
+    return sent, swap(jnp.stack([held[k] for k in sent]).astype(BF16), "tensor", bit), bit
+
+
+def scatter_add(held, sent, got, bit):
+    for spot, k in enumerate(sent):
+        held[k ^ bit] = held[k ^ bit].astype(F32) + got[spot].astype(F32)
+        del held[k]
 
 
 def scatter_arrived(states):
-    return [state[3] for state in states]
-
-
-def scatter_finish(states):
+    return [state[2] for state in states]
+
+
+def together(states):
+    arrived = lax.optimization_barrier(tuple(scatter_arrived(states)))
+    for state, got in zip(states, arrived):
+        state[2] = got
+    return states
+
+
+def scatter_second(states):
+    bits = axis_bits("tensor")
+    later = []
+    for (held, sent, got, first), order in zip(states, (bits, bits[::-1])):
+        held = dict(held)
+        scatter_add(held, sent, got, first)
+        for bit in order[1:-1]:
+            sent, got, _ = scatter_send(held, bit)
+            scatter_add(held, sent, got, bit)
+        later.append([held, *scatter_send(held, order[-1])])
+    return later
+
+
+def scatter_end(states):
     sums = []
-    for order, held, sent, got in states:
-        for number, bit in enumerate(order):
-            if number:
-                sent, got = scatter_send(held, bit)
-            for spot, k in enumerate(sent):
-                held[k ^ bit] = held[k ^ bit].astype(F32) + got[spot].astype(F32)
-                del held[k]
+    for held, sent, got, bit in states:
+        held = dict(held)
+        scatter_add(held, sent, got, bit)
         sums.append(held[0])
     return jnp.concatenate(sums, -2)
-
-
-def scatter_pieces(pieces):
-    return scatter_finish(scatter_start(pieces))
 
 
 def per_device(
@@ -603,13 +621,12 @@
         outs=[((48, tokens), F32, (48, LANES), row_map)],
         name="spread",
     )
-    fixed_sums = butterfly_sum(fixed_part, "tensor")
 
     first_own, first_arrived = gather_start(normed_first)
     first_arrived = [after(arrived, fixed_part) for arrived in first_arrived]
     first_pieces = gather_finish((first_own, first_arrived))
     last_pieces = gather_pieces(normed_last)
-    first_pieces = after(first_pieces, cot_pieces, fixed_sums)
+    first_pieces = after(first_pieces, cot_pieces)
 
     places = (jnp.arange(tokens, dtype=jnp.int32) % LENGTH).astype(F32)
     freqs = jnp.power(10000.0, -jnp.arange(0, ROT, 2).astype(F32) / ROT)
@@ -691,7 +708,7 @@
         residual = streams[STREAMS - 1, number * rows : (number + 1) * rows]
         if number:
             residual = after(residual, *block_states[number - 1][1])
-        total = residual + scatter_finish(block_states[number])
+        total = residual + scatter_end(together(scatter_second(together(block_states[number]))))
         block_owns.append(lax.optimization_barrier(total.astype(BF16)))
         block_states[number] = gather_start(block_owns[number])
     block_chunks = [gather_finish(state) for state in block_states]
@@ -756,17 +773,24 @@
     )
     branch_grad = after(branch_grad, both_part)
     branch_in = (branch_grad, (tokens, width_all), const(0, 0))
+    tensor_bits = axis_bits("tensor")
+    fixed_sums = after(fixed_part, branch_pieces)
+    fixed_sums = fixed_sums + swap(fixed_sums, "tensor", tensor_bits[0])
+    branch_grad = after(branch_grad, fixed_sums)
+    branch_in = (branch_grad, (tokens, width_all), const(0, 0))
     (attended_grad,) = call(
         back_kernel,
-        (1,),
+        (tokens // ROWS,),
         ins=[
-            branch_in,
+            (branch_grad, (ROWS, width_all), lambda i, p: (i, 0)),
             (both_full, (heads_width, width_all), const(hidden_steps, 0)),
         ],
-        outs=[((tokens, heads_width), BF16, (tokens, heads_width), const(0, 0))],
+        outs=[((tokens, heads_width), BF16, (ROWS, heads_width), lambda i, p: (i, 0))],
         name="attended_grad",
         flops=2 * tokens * width_all * heads_width,
     )
+    for bit in tensor_bits[1:]:
+        fixed_sums = fixed_sums + swap(fixed_sums, "tensor", bit)
     next_bits = axis_bits("dp")
     next_sum = next_part + swap(next_part, "dp", next_bits[0])
     lin_grads = pl.pallas_call(
@@ -814,7 +838,7 @@
     lin_grads = after(lin_grads, grads_a)
     grads_b = qkv_back(lin_grads, 1, 3)
     states_b = scatter_start(grads_b)
-    branch_grad = after(branch_grad, grads_b, next_sum)
+    branch_grad = after(branch_grad, grads_b, next_sum, fixed_sums)
     branch_in = (branch_grad, (tokens, width_all), const(0, 0))
     (hidden_grad,) = call(
         hidden_grad_kernel,
@@ -829,7 +853,6 @@
         flops=2 * tokens * width_all * hidden_width,
     )
     hidden_grad = after(hidden_grad, *scatter_arrived(states_a))
-    grad_a = scatter_finish(states_a)
     (last_grads,) = call(
         back_kernel,
         (count,),
@@ -879,11 +902,15 @@
         scratch=[((count, width, tokens), BF16)],
     )
     wide_part = after(
-        wide_part, grad_a, *scatter_arrived(states_b), *scatter_arrived(last_states)
-    )
-    grad_b = scatter_finish(states_b)
-    last_grad = scatter_finish(last_states)
-    first_grad = jnp.concatenate([grad_a, grad_b], 0)
+        wide_part,
+        *scatter_arrived(states_b),
+        *scatter_arrived(last_states),
+    )
+    together(states_b + last_states)
+    later = [scatter_second(states) for states in (states_a, states_b, last_states)]
+    together([state for states in later for state in states])
+    first_grad = jnp.concatenate([scatter_end(later[0]), scatter_end(later[1])], 0)
+    last_grad = scatter_end(later[2])
     both_grad = lax.psum_scatter(both_part, "dp", scatter_dimension=1, tiled=True).astype(F32)
     out_end = hidden_width + heads_width
     down_grad, out_grad = both_grad[:hidden_width], both_grad[hidden_width:out_end]
@@ -904,6 +931,7 @@
         stats_in,
         gain_in,
     ]
+    grad_ins[0] = (after(first_grad, next_sum), *grad_ins[0][1:])
     block_grad_in = (block_grad, (LANES, width), lambda i, p: (i, 0))
     sums, norm_part = call(
         functools.partial(sums_kernel, width_all),
@@ -915,7 +943,14 @@
         ],
         name="sums",
     )
-    sums = butterfly_sum(sums, "tensor")
+    dp_bits = axis_bits("dp")
+    sums = sums + swap(sums, "tensor", tensor_bits[0])
+    norm_part = norm_part + swap(norm_part, "dp", dp_bits[0])
+    sums, norm_part = lax.optimization_barrier((sums, norm_part))
+    for bit in tensor_bits[1:]:
+        sums = sums + swap(sums, "tensor", bit)
+    norm_part = norm_part + swap(norm_part, "dp", dp_bits[1])
+    sums, norm_part = lax.optimization_barrier((sums, norm_part))
     pairs = STREAMS * ENTRIES
     feature_sums = sums[pairs : pairs + 2 * STREAMS]
     (history_grad,) = call(
@@ -936,7 +971,8 @@
         * fixed_sums[:pairs].reshape(STREAMS, ENTRIES, tokens)
     ).reshape(pairs, tokens)
 
-    norm_part = butterfly_sum(after(norm_part, sums), "dp")
+    for bit in dp_bits[2:]:
+        norm_part = norm_part + swap(norm_part, "dp", bit)
     norm_whole = lax.dynamic_update_slice_in_dim(
         jnp.zeros((2 * STREAMS, width_all), F32), norm_part, tensor_place * width, 1
     )

time: 729 us -> 702 us (0.963)
  waiting for transfers between devices: 279 us -> 264 us
  Pallas kernels: 287 us -> 277 us
    ppermute x46, waiting for transfers between devices: 278 us -> 244 us  [swap(): return lax.ppermute(values, axis, [(i, i ^ bit) for i in range(count)])]
    reduce_scatter x1, waiting for transfers between devices: 0.01 us -> 17.7 us  [per_device(): lax.psum_scatter(wide_part, 'dp', scatter_dimension=0, tiled=True)]
    pallas_call x17, Pallas kernels: 269 us -> 260 us  [kernel_call(): return call(place, *[a for a, _, _ in ins])]
  transfers between devices with their start and end apart: 51 -> 51, of which waited for: 27 -> 29; matrix products, arithmetic and copies ran while one was open for 9% -> 9% of each run, Pallas kernels for 34% -> 34%
where the time goes in v3:
time: 702 us; the launch traced here: 691 us
  Pallas kernels  277 us (39%)
  waiting for transfers between devices  264 us (38%)
  starting transfers between devices  43.3 us (6%)
  other arithmetic  41.3 us (6%)
  local copies, waits for them, and re-layouts  35 us (5%)
  between operations  15.3 us (2%)
  blocking collectives  14.9 us (2%)
    pallas_call x17, Pallas kernels, kernel_call(): return call(place, *[a for a, _, _ in ins])  260 us
    ppermute x46, waiting for transfers between devices, swap(): return lax.ppermute(values, axis, [(i, i ^ bit) for i in range(count)])  244 us
    ppermute x46, starting transfers between devices, swap(): return lax.ppermute(values, axis, [(i, i ^ bit) for i in range(count)])  43.1 us
    reduce_scatter x1, waiting for transfers between devices, per_device(): lax.psum_scatter(wide_part, 'dp', scatter_dimension=0, tiled=True)  17.7 us
    pallas_call x1, Pallas kernels, per_device(): pl.pallas_call(attend_back_kernel, out_shape=jax.ShapeDtypeStruct((3, tok...  17.5 us
    all_gather x1, blocking collectives, per_device(): smalls = lax.all_gather(smalls, 'dp', axis=0, tiled=True)  14.9 us
  transfers between devices with their start and end apart: 51, of which 29 were waited for; matrix products, arithmetic and copies ran while one was open for 9% of the time, Pallas kernels for 34%

profile of v3, /device:TPU:0, one launch (start us, length us, event | category | flops | bytes accessed | tf_op | source)
XLA Modules:
  0.0 690.8 jit_solution(8620342990973611803)
XLA Ops:
  8.8 2.2 pad_maximum_fusion.3
  11.0 3.0 collective-permute-start
  16.6 14.9 %all_gather.12 = bf16[2048,48]{0,1:T(8,128)(2,1)S(1)} all-gather(bf16[256,48]{0,1:T(8,128)(2,1)S(1)} %pad_maximum_fusion.7), channel_id=1, replica_groups=mesh['dp'=8,'tensor'=4] {'dp'}, dimensions={0}, use_global_device_ids=true | all-gather | bytes 221184 | tf_op jit(solution)/shard_map/all_gather | solution.py:572
  32.1 14.3 %mix.1 = (f32[4,1024,512]{2,1,0:T(8,128)}, f32[8,1024]{1,0:T(8,128)}) custom-call(s32[2]{0:T(128)} %pad_add_fusion.place, bf16[9,1024,512]{2,1,0:T(8,128)(2,1)} %hist.5, f32[1024,36]{1,0:T(8,128)} %bitcast.37), custom_call_target="tpu_custom_call" | custom-call | flops 37748736 | bytes 18006016 | tf_op jit(solution)/shard_map/mix/pallas_call | solution.py:58
  47.3 3.4 collective-permute-done.2
  52.7 2.6 collective-permute-done.3
  56.0 9.6 %norm.1 = (bf16[3,1024,512]{2,1,0:T(8,128)(2,1)}, bf16[1024,512]{1,0:T(8,128)(2,1)}) custom-call(s32[2]{0:T(128)} %pad_add_fusion.place, f32[4,1024,512]{2,1,0:T(8,128)} %get-tuple-element.75.streams, f32[8,1024]{1,0:T(8,128)} %add.235.stats, f32[4,512]{1,0:T(4,128)} %get-tuple-element.152.gain, f32[4,512]{1,0:T(4,128)} %get-tuple-element.151.bias), custom_call_target="tpu_custom_call" | custom-call | bytes 12632064 | tf_op jit(solution)/shard_map/norm/pallas_call | solution.py:58
  68.4 14.9 %spread.1 = f32[48,1024]{1,0:T(8,128)} custom-call(s32[2]{0:T(128)} %pad_add_fusion.place, f32[4,1024,512]{2,1,0:T(8,128)} %get-tuple-element.75.streams, f32[8,1024]{1,0:T(8,128)} %add.235.stats, bf16[9,1024,512]{2,1,0:T(8,128)(2,1)} %hist.5), custom_call_target="tpu_custom_call" | custom-call | bytes 18055168 | tf_op jit(solution)/shard_map/spread/pallas_call | solution.py:58
  83.3 51.5 %collective-permute-done.9.refs_2_.refs_7_ = bf16[3,1024,512]{2,1,0:T(8,128)(2,1)S(1)} collective-permute-done((bf16[3,1024,512]{2,1,0:T(8,128)(2,1)}, bf16[3,1024,512]{2,1,0:T(8,128)(2,1)S(1)}, u32[]{:S(2)}, u32[]{:S(2)}) %collective-permute-start.9) | collective-permute-done | bytes 3145760 | tf_op jit(solution)/shard_map/ppermute | solution.py:431
  147.0 13.2 %collective-permute-done.4.refs_1_ = bf16[1024,512]{1,0:T(8,128)(2,1)} collective-permute-done((bf16[1024,512]{1,0:T(8,128)(2,1)}, bf16[1024,512]{1,0:T(8,128)(2,1)}, u32[]{:S(2)}, u32[]{:S(2)}) %collective-permute-start.4) | collective-permute-done | bytes 1048608 | tf_op jit(solution)/shard_map/ppermute | solution.py:431
  167.0 32.0 %collective-permute-done.5.refs_2_ = bf16[1024,512]{1,0:T(8,128)(2,1)S(1)} collective-permute-done((bf16[1024,512]{1,0:T(8,128)(2,1)}, bf16[1024,512]{1,0:T(8,128)(2,1)S(1)}, u32[]{:S(2)}, u32[]{:S(2)}) %collective-permute-start.5) | collective-permute-done | bytes 1048608 | tf_op jit(solution)/shard_map/ppermute | solution.py:431
  201.1 9.2 %collective-permute-done.12.refs_8_ = bf16[512,512]{1,0:T(8,128)(2,1)} collective-permute-done((bf16[512,512]{1,0:T(8,128)(2,1)S(1)}, bf16[512,512]{1,0:T(8,128)(2,1)}, u32[]{:S(2)}, u32[]{:S(2)}) %collective-permute-start.12) | collective-permute-done | bytes 524320 | tf_op jit(solution)/shard_map/ppermute | solution.py:431
  210.9 15.4 %qkv.1.q.k.v = bf16[3,1024,512]{2,1,0:T(8,128)(2,1)} custom-call(s32[2]{0:T(128)} %pad_add_fusion.place, bf16[3,1024,512]{2,1,0:T(8,128)(2,1)} %get-tuple-element.78.refs_0_.refs_5_, bf16[3,1024,512]{2,1,0:T(8,128)(2,1)} %copy-done.3, bf16[3,1024,512]{2,1,0:T(8,128)(2,1)} %copy-done.2, bf16[3,512,512]{2,1,0:T(8,128)(2,1)} %collective-permute-done.10.refs_3_.refs_8_, ...), custom_call_target="tpu_custom_call" | custom-call | flops 6442450944 | bytes 42467328 | tf_op jit(solution)/shard_map/qkv/pallas_call | solution.py:58
  226.3 11.5 %attend.1.attended = bf16[1024,512]{1,0:T(8,128)(2,1)} custom-call(s32[2]{0:T(128)} %pad_add_fusion.place, bf16[3,1024,512]{2,1,0:T(8,128)(2,1)} %qkv.1.q.k.v, bf16[3,1024,512]{2,1,0:T(8,128)(2,1)} %qkv.1.q.k.v, bf16[3,1024,512]{2,1,0:T(8,128)(2,1)} %qkv.1.q.k.v), custom_call_target="tpu_custom_call" | custom-call | flops 2147483648 | bytes 10485760 | tf_op jit(solution)/shard_map/attend/pallas_call | solution.py:58
  238.8 20.9 %up.1 = (bf16[1024,2048]{1,0:T(8,128)(2,1)}, bf16[1024,2048]{1,0:T(8,128)(2,1)}) custom-call(s32[2]{0:T(128)} %pad_add_fusion.place, bf16[1024,512]{1,0:T(8,128)(2,1)} %get-tuple-element.68.refs_0_, bf16[1024,512]{1,0:T(8,128)(2,1)} %collective-permute-done.4.refs_1_, bf16[1024,512]{1,0:T(8,128)(2,1)} %copy-done.7, bf16[512,512]{1,0:T(8,128)(2,1)} %copy-done.20, ...), custom_call_target="tpu_custom_call" | custom-call | flops 8589934592 | bytes 46137344 | tf_op jit(solution)/shard_map/up/pallas_call | solution.py:58
  260.8 16.5 %down.1 = bf16[4,1024,512]{2,1,0:T(8,128)(2,1)} custom-call(s32[2]{0:T(128)} %pad_add_fusion.place, bf16[1024,2048]{1,0:T(8,128)(2,1)} %get-tuple-element.73.hidden, bf16[1024,512]{1,0:T(8,128)(2,1)} %attend.1.attended, bf16[2560,2048]{1,0:T(8,128)(2,1)} %all-gather.8.cloned.1.call-done.down.out.weight, ...), custom_call_target="tpu_custom_call" | custom-call | flops 10737418240 | bytes 30408704 | tf_op jit(solution)/shard_map/down/pallas_call | solution.py:58
  283.1 22.4 %collective-permute-done.14 = bf16[2,512,512]{2,1,0:T(8,128)(2,1)S(1)} collective-permute-done((bf16[2,512,512]{2,1,0:T(8,128)(2,1)S(1)}, bf16[2,512,512]{2,1,0:T(8,128)(2,1)S(1)}, u32[]{:S(2)}, u32[]{:S(2)}) %collective-permute-start.14) | collective-permute-done | bytes 1048608 | tf_op jit(solution)/shard_map/ppermute | solution.py:431
  309.1 10.9 %collective-permute-done.16 = bf16[1,512,512]{2,1,0:T(8,128)(2,1)S(1)} collective-permute-done((bf16[1,512,512]{2,1,0:T(8,128)(2,1)S(1)}, bf16[1,512,512]{2,1,0:T(8,128)(2,1)S(1)}, u32[]{:S(2)}, u32[]{:S(2)}) %collective-permute-start.16) | collective-permute-done | bytes 524320 | tf_op jit(solution)/shard_map/ppermute | solution.py:431
  324.9 21.8 %collective-permute-done.18.refs_1_ = bf16[1024,512]{1,0:T(8,128)(2,1)S(1)} collective-permute-done((bf16[1024,512]{1,0:T(8,128)(2,1)S(1)}, bf16[1024,512]{1,0:T(8,128)(2,1)S(1)}, u32[]{:S(2)}, u32[]{:S(2)}) %collective-permute-start.18) | collective-permute-done | bytes 1048608 | tf_op jit(solution)/shard_map/ppermute | solution.py:431
  350.7 8.0 %collective-permute-done.20.refs_3_ = bf16[512,512]{1,0:T(8,128)(2,1)} collective-permute-done((bf16[512,512]{1,0:T(8,128)(2,1)}, bf16[512,512]{1,0:T(8,128)(2,1)}, u32[]{:S(2)}, u32[]{:S(2)}) %collective-permute-start.20) | collective-permute-done | bytes 524320 | tf_op jit(solution)/shard_map/ppermute | solution.py:431
  359.9 11.4 %middle.1 = (bf16[1024,2048]{1,0:T(8,128)(2,1)}, f32[1024,512]{1,0:T(8,128)}, f32[40,1024]{1,0:T(8,128)}, f32[40,40]{1,0:T(8,128)}, f32[40,2048]{1,0:T(8,128)}) custom-call(s32[2]{0:T(128)} %pad_add_fusion.place, bf16[1024,512]{1,0:T(8,128)(2,1)} %copy-done.6, bf16[1024,512]{1,0:T(8,128)(2,1)} %copy-done.11, bf16[1024,512]{1,0:T(8,128)(2,1)} %copy-done.12, ...), custom_call_target="tpu_custom_call" | custom-call | flops 503316480 | bytes 15922560 | tf_op jit(solution)/shard_map/middle/pallas_call | solution.py:58
  371.4 17.0 %down_grad.1 = bf16[2608,2048]{1,0:T(8,128)(2,1)} custom-call(s32[2]{0:T(128)} %pad_add_fusion.place, bf16[1024,2048]{1,0:T(8,128)(2,1)} %get-tuple-element.73.hidden, bf16[1024,512]{1,0:T(8,128)(2,1)} %attend.1.attended, bf16[1024,2048]{1,0:T(8,128)(2,1)} %get-tuple-element.95.branch_grad.grad), custom_call_target="tpu_custom_call" | custom-call | flops 10737418240 | bytes 20119552 | tf_op jit(solution)/shard_map/down_grad/pallas_call | solution.py:58
  390.7 5.0 collective-permute-done.22
  397.2 4.2 collective-permute-done.30
  401.5 7.4 %attended_grad.1.grad = bf16[1024,512]{1,0:T(8,128)(2,1)} custom-call(s32[2]{0:T(128)} %pad_add_fusion.place, bf16[1024,2048]{1,0:T(8,128)(2,1)} %get-tuple-element.95.branch_grad.grad, bf16[2560,2048]{1,0:T(8,128)(2,1)} %all-gather.8.cloned.1.call-done.down.out.weight), custom_call_target="tpu_custom_call" | custom-call | flops 2147483648 | bytes 15728640 | tf_op jit(solution)/shard_map/attended_grad/pallas_call | solution.py:58
  408.8 17.5 %attend_back.1.grad.refs_11_ = bf16[3,1024,512]{2,1,0:T(8,128)(2,1)} custom-call(s32[2]{0:T(128)} %pad_add_fusion.place, bf16[3,1024,512]{2,1,0:T(8,128)(2,1)} %qkv.1.q.k.v, bf16[3,1024,512]{2,1,0:T(8,128)(2,1)} %qkv.1.q.k.v, bf16[3,1024,512]{2,1,0:T(8,128)(2,1)} %qkv.1.q.k.v, bf16[1024,512]{1,0:T(8,128)(2,1)} %attended_grad.1.grad, ...), custom_call_target="tpu_custom_call" | custom-call | flops 5368709120 | bytes 8388608 | tf_op jit(solution)/shard_map/attend_back/pallas_call | solution.py:796
  426.4 6.8 qkv_back.2
  438.2 11.7 %qkv_back.3 = bf16[4,2,1024,512]{3,2,1,0:T(8,128)(2,1)} custom-call(s32[2]{0:T(128)} %pad_add_fusion.place, bf16[3,1024,512]{2,1,0:T(8,128)(2,1)} %attend_back.1.grad.refs_11_, bf16[3,2048,512]{2,1,0:T(8,128)(2,1)} %all-gather.6.cloned.1.call-done.refs_5_.refs_6_.refs_7_.refs_8_.weight), custom_call_target="tpu_custom_call" | custom-call | flops 4294967296 | bytes 17825792 | tf_op jit(solution)/shard_map/qkv_back/pallas_call | solution.py:58
  453.2 3.0 stack.70
  457.9 15.0 %hidden_grad.1.grad.refs_10_ = bf16[1024,2048]{1,0:T(8,128)(2,1)} custom-call(s32[2]{0:T(128)} %pad_add_fusion.place, bf16[1024,2048]{1,0:T(8,128)(2,1)} %get-tuple-element.95.branch_grad.grad, bf16[2560,2048]{1,0:T(8,128)(2,1)} %all-gather.8.cloned.1.call-done.down.out.weight, bf16[1024,2048]{1,0:T(8,128)(2,1)} %get-tuple-element.96.slope), custom_call_target="tpu_custom_call" | custom-call | flops 8589934592 | bytes 23068672 | tf_op jit(solution)/shard_map/hidden_grad/pallas_call | solution.py:58
  473.0 14.0 %up_back.1 = bf16[4,1024,512]{2,1,0:T(8,128)(2,1)} custom-call(s32[2]{0:T(128)} %pad_add_fusion.place, bf16[1024,2048]{1,0:T(8,128)(2,1)} %hidden_grad.1.grad.refs_10_, bf16[2048,2048]{1,0:T(8,128)(2,1)} %all-gather.4.cloned.1.call-done.refs_5_.refs_6_.refs_7_.refs_8_.weight), custom_call_target="tpu_custom_call" | custom-call | flops 8589934592 | bytes 16777216 | tf_op jit(solution)/shard_map/up_back/pallas_call | solution.py:58
  487.0 2.3 stack.71
  494.0 35.8 %weight_grad.1 = bf16[2048,3584]{1,0:T(8,128)(2,1)} custom-call(s32[2]{0:T(128)} %pad_add_fusion.place, bf16[1024,512]{1,0:T(8,128)(2,1)} %get-tuple-element.68.refs_0_, bf16[1024,512]{1,0:T(8,128)(2,1)} %collective-permute-done.4.refs_1_, bf16[1024,512]{1,0:T(8,128)(2,1)} %copy-done.7, bf16[512,512]{1,0:T(8,128)(2,1)} %copy-done.20, ...), custom_call_target="tpu_custom_call" | custom-call | flops 15032385536 | bytes 38797312 | tf_op jit(solution)/shard_map/weight_grad/pallas_call | solution.py:58
  532.8 3.5 add_convert_fusion
  537.9 4.2 collective-permute-done.37
  544.8 2.7 collective-permute-done.38
  550.7 23.5 %collective-permute-done.26 = bf16[1,1,512,512]{3,2,1,0:T(8,128)(2,1)S(1)} collective-permute-done((bf16[1,1,512,512]{3,2,1,0:T(8,128)(2,1)S(1)}, bf16[1,1,512,512]{3,2,1,0:T(8,128)(2,1)S(1)}, u32[]{:S(2)}, u32[]{:S(2)}) %collective-permute-start.26) | collective-permute-done | bytes 524320 | tf_op jit(solution)/shard_map/ppermute | solution.py:431
  574.1 4.1 collective-permute-done.35
  578.2 4.2 collective-permute-done.36
  584.1 2.8 add_bitcast_fusion.1
  586.8 3.2 maximum_maximum_fusion.first
  593.1 18.1 %sums.1 = (f32[48,1024]{1,0:T(8,128)}, f32[8,512]{1,0:T(8,128)}) custom-call(s32[2]{0:T(128)} %pad_add_fusion.place, f32[3,1024,512]{2,1,0:T(8,128)} %maximum_maximum_fusion.first, f32[1024,512]{1,0:T(8,128)} %pad_maximum_fusion.1.last, f32[4,1024,512]{2,1,0:T(8,128)} %get-tuple-element.75.streams, f32[8,1024]{1,0:T(8,128)} %add.235.stats, ...), custom_call_target="tpu_custom_call" | custom-call | bytes 28565504 | tf_op jit(solution)/shard_map/sums/pallas_call | solution.py:58
  614.6 2.5 collective-permute-done.39
  619.4 4.3 collective-permute-done.42
  624.1 5.1 collective-permute-done.43
  630.7 2.8 collective-permute-done.44
  636.1 19.3 %history.1 = f32[9,1024,512]{2,1,0:T(8,128)} custom-call(s32[2]{0:T(128)} %pad_add_fusion.place, f32[3,1024,512]{2,1,0:T(8,128)} %maximum_maximum_fusion.first, f32[1024,512]{1,0:T(8,128)} %pad_maximum_fusion.1.last, f32[4,1024,512]{2,1,0:T(8,128)} %get-tuple-element.75.streams, f32[8,1024]{1,0:T(8,128)} %add.235.stats, f32[4,512]{1,0:T(4,128)} %get-tuple-element.152.gain, ...), custom_call_target="tpu_custom_call" | custom-call | bytes 37969920 | tf_op jit(solution)/shard_map/history/pallas_call | solution.py:58
  660.8 17.7 %reduce-scatter.3.cloned.1.call-done = bf16[256,3584]{1,0:T(8,128)(2,1)} async-done(((bf16[2048,3584]{1,0:T(8,128)(2,1)}), bf16[256,3584]{1,0:T(8,128)(2,1)}) %reduce-scatter.3.cloned.1.call-update) | async-done | bytes 1835024 | tf_op jit(solution)/shard_map/reduce_scatter | solution.py:918
  (229 shorter events, 108.2 us)
Async XLA Ops:
  7.2 203.7 %all-gather.6.cloned.1.call-start = ((), (), s32[]{:S(2)}) async-start(), calls=%async_computation.3 | async-start | bytes 7077888 | tf_op jit(solution)/shard_map/all_gather | solution.py:578
  7.9 229.9 %all-gather.4.cloned.1.call-start = ((), (), s32[]{:S(2)}) async-start(), calls=%async_computation.2 | async-start | bytes 9437184 | tf_op jit(solution)/shard_map/all_gather | solution.py:579
  8.7 252.1 %all-gather.8.cloned.1.call-start = ((), (), s32[]{:S(2)}) async-start(), calls=%async_computation.4 | async-start | bytes 11796480 | tf_op jit(solution)/shard_map/all_gather | solution.py:580
  11.0 645.1 %reduce-scatter.5.cloned.1.call-start = ((), (), s32[]{:S(2)}) async-start(), calls=%async_computation.6 | async-start | bytes 12017664 | tf_op jit(solution)/shard_map/reduce_scatter | solution.py:914
  11.0 35.5 %collective-permute-start = (bf16[1024,512]{1,0:T(8,128)(2,1)S(1)}, bf16[1024,512]{1,0:T(8,128)(2,1)S(1)}, u32[]{:S(2)}, u32[]{:S(2)}) collective-permute-start(bf16[1024,512]{1,0:T(8,128)(2,1)S(1)} %copy-done.17), channel_id=1, source_target_pairs={{0,1},{1,0},{2,3},{3,2},{4,5},{5,4},{6,7},{7,6},{8,9},{9,8},{10,11... | collective-permute-start | bytes 3145736 | tf_op jit(solution)/shard_map/ppermute | solution.py:431
  14.0 32.5 %collective-permute-start.1 = (bf16[1024,512]{1,0:T(8,128)(2,1)S(1)}, bf16[1024,512]{1,0:T(8,128)(2,1)S(1)}, u32[]{:S(2)}, u32[]{:S(2)}) collective-permute-start(bf16[1024,512]{1,0:T(8,128)(2,1)S(1)} %copy-done.17), channel_id=1, source_target_pairs={{0,2},{1,3},{2,0},{3,1},{4,6},{5,7},{6,4},{7,5},{8,10},{9,11},{10,... | collective-permute-start | bytes 3145736 | tf_op jit(solution)/shard_map/ppermute | solution.py:431
  65.6 69.2 %collective-permute-start.9 = (bf16[3,1024,512]{2,1,0:T(8,128)(2,1)}, bf16[3,1024,512]{2,1,0:T(8,128)(2,1)S(1)}, u32[]{:S(2)}, u32[]{:S(2)}) collective-permute-start(bf16[3,1024,512]{2,1,0:T(8,128)(2,1)} %get-tuple-element.78.refs_0_.refs_5_), channel_id=1, source_target_pairs={{0,2},{1,3},{2,0},{3,1},{4,6},{5,7},{6,4},{7,5},{8,10},{9,11},{10,... | collective-permute-start | bytes 9437192 | tf_op jit(solution)/shard_map/ppermute | solution.py:431
  66.4 71.2 %collective-permute-start.8 = (bf16[3,1024,512]{2,1,0:T(8,128)(2,1)}, bf16[3,1024,512]{2,1,0:T(8,128)(2,1)S(1)}, u32[]{:S(2)}, u32[]{:S(2)}) collective-permute-start(bf16[3,1024,512]{2,1,0:T(8,128)(2,1)} %get-tuple-element.78.refs_0_.refs_5_), channel_id=1, source_target_pairs={{0,1},{1,0},{2,3},{3,2},{4,5},{5,4},{6,7},{7,6},{8,9},{9,8},{10,11... | collective-permute-start | bytes 9437192 | tf_op jit(solution)/shard_map/ppermute | solution.py:431
  66.7 93.6 %collective-permute-start.4 = (bf16[1024,512]{1,0:T(8,128)(2,1)}, bf16[1024,512]{1,0:T(8,128)(2,1)}, u32[]{:S(2)}, u32[]{:S(2)}) collective-permute-start(bf16[1024,512]{1,0:T(8,128)(2,1)} %get-tuple-element.68.refs_0_), channel_id=1, source_target_pairs={{0,1},{1,0},{2,3},{3,2},{4,5},{5,4},{6,7},{7,6},{8,9},{9,8},{10,11... | collective-permute-start | bytes 3145736 | tf_op jit(solution)/shard_map/ppermute | solution.py:431
  136.1 74.7 %collective-permute-start.11 = (bf16[3,512,512]{2,1,0:T(8,128)(2,1)}, bf16[3,512,512]{2,1,0:T(8,128)(2,1)}, u32[]{:S(2)}, u32[]{:S(2)}) collective-permute-start(bf16[3,512,512]{2,1,0:T(8,128)(2,1)} %slice.272), channel_id=1, source_target_pairs={{0,1},{1,0},{2,3},{3,2},{4,5},{5,4},{6,7},{7,6},{8,9},{9,8},{10,11... | collective-permute-start | bytes 4718600 | tf_op jit(solution)/shard_map/ppermute | solution.py:431
  139.0 71.9 %collective-permute-start.10 = (bf16[3,512,512]{2,1,0:T(8,128)(2,1)}, bf16[3,512,512]{2,1,0:T(8,128)(2,1)}, u32[]{:S(2)}, u32[]{:S(2)}) collective-permute-start(bf16[3,512,512]{2,1,0:T(8,128)(2,1)} %slice.271), channel_id=1, source_target_pairs={{0,2},{1,3},{2,0},{3,1},{4,6},{5,7},{6,4},{7,5},{8,10},{9,11},{10,... | collective-permute-start | bytes 4718600 | tf_op jit(solution)/shard_map/ppermute | solution.py:431
  141.7 57.4 %collective-permute-start.5 = (bf16[1024,512]{1,0:T(8,128)(2,1)}, bf16[1024,512]{1,0:T(8,128)(2,1)S(1)}, u32[]{:S(2)}, u32[]{:S(2)}) collective-permute-start(bf16[1024,512]{1,0:T(8,128)(2,1)} %get-tuple-element.68.refs_0_), channel_id=1, source_target_pairs={{0,2},{1,3},{2,0},{3,1},{4,6},{5,7},{6,4},{7,5},{8,10},{9,11},{10,... | collective-permute-start | bytes 3145736 | tf_op jit(solution)/shard_map/ppermute | solution.py:431
  145.7 64.7 %collective-permute-start.12 = (bf16[512,512]{1,0:T(8,128)(2,1)S(1)}, bf16[512,512]{1,0:T(8,128)(2,1)}, u32[]{:S(2)}, u32[]{:S(2)}) collective-permute-start(bf16[512,512]{1,0:T(8,128)(2,1)S(1)} %slice.340), channel_id=1, source_target_pairs={{0,2},{1,3},{2,0},{3,1},{4,6},{5,7},{6,4},{7,5},{8,10},{9,11},{10,... | collective-permute-start | bytes 1572872 | tf_op jit(solution)/shard_map/ppermute | solution.py:431
  160.2 50.6 %collective-permute-start.13 = (bf16[512,512]{1,0:T(8,128)(2,1)S(1)}, bf16[512,512]{1,0:T(8,128)(2,1)S(1)}, u32[]{:S(2)}, u32[]{:S(2)}) collective-permute-start(bf16[512,512]{1,0:T(8,128)(2,1)S(1)} %slice.341), channel_id=1, source_target_pairs={{0,1},{1,0},{2,3},{3,2},{4,5},{5,4},{6,7},{7,6},{8,9},{9,8},{10,11... | collective-permute-start | bytes 1572872 | tf_op jit(solution)/shard_map/ppermute | solution.py:431
  199.0 38.7 %collective-permute-start.6 = (bf16[512,512]{1,0:T(8,128)(2,1)S(1)}, bf16[512,512]{1,0:T(8,128)(2,1)S(1)}, u32[]{:S(2)}, u32[]{:S(2)}) collective-permute-start(bf16[512,512]{1,0:T(8,128)(2,1)S(1)} %slice.337), channel_id=1, source_target_pairs={{0,2},{1,3},{2,0},{3,1},{4,6},{5,7},{6,4},{7,5},{8,10},{9,11},{10,... | collective-permute-start | bytes 1572872 | tf_op jit(solution)/shard_map/ppermute | solution.py:431
  210.4 27.4 %collective-permute-start.7 = (bf16[512,512]{1,0:T(8,128)(2,1)}, bf16[512,512]{1,0:T(8,128)(2,1)S(1)}, u32[]{:S(2)}, u32[]{:S(2)}) collective-permute-start(bf16[512,512]{1,0:T(8,128)(2,1)} %slice.338), channel_id=1, source_target_pairs={{0,1},{1,0},{2,3},{3,2},{4,5},{5,4},{6,7},{7,6},{8,9},{9,8},{10,11... | collective-permute-start | bytes 1572872 | tf_op jit(solution)/shard_map/ppermute | solution.py:431
  280.1 25.4 %collective-permute-start.14 = (bf16[2,512,512]{2,1,0:T(8,128)(2,1)S(1)}, bf16[2,512,512]{2,1,0:T(8,128)(2,1)S(1)}, u32[]{:S(2)}, u32[]{:S(2)}) collective-permute-start(bf16[2,512,512]{2,1,0:T(8,128)(2,1)S(1)} %pad_maximum_fusion.4), channel_id=1, source_target_pairs={{0,1},{1,0},{2,3},{3,2},{4,5},{5,4},{6,7},{7,6},{8,9},{9,8},{10,11... | collective-permute-start | bytes 3145736 | tf_op jit(solution)/shard_map/ppermute | solution.py:431
  281.6 25.0 %collective-permute-start.15 = (bf16[2,512,512]{2,1,0:T(8,128)(2,1)S(1)}, bf16[2,512,512]{2,1,0:T(8,128)(2,1)S(1)}, u32[]{:S(2)}, u32[]{:S(2)}) collective-permute-start(bf16[2,512,512]{2,1,0:T(8,128)(2,1)S(1)} %stack.68), channel_id=1, source_target_pairs={{0,2},{1,3},{2,0},{3,1},{4,6},{5,7},{6,4},{7,5},{8,10},{9,11},{10,... | collective-permute-start | bytes 3145736 | tf_op jit(solution)/shard_map/ppermute | solution.py:431
  307.0 13.0 %collective-permute-start.16 = (bf16[1,512,512]{2,1,0:T(8,128)(2,1)S(1)}, bf16[1,512,512]{2,1,0:T(8,128)(2,1)S(1)}, u32[]{:S(2)}, u32[]{:S(2)}) collective-permute-start(bf16[1,512,512]{2,1,0:T(8,128)(2,1)S(1)} %get-tuple-element.141), channel_id=1, source_target_pairs={{0,2},{1,3},{2,0},{3,1},{4,6},{5,7},{6,4},{7,5},{8,10},{9,11},{10,... | collective-permute-start | bytes 1572872 | tf_op jit(solution)/shard_map/ppermute | solution.py:431
  308.5 12.7 %collective-permute-start.17 = (bf16[1,512,512]{2,1,0:T(8,128)(2,1)S(1)}, bf16[1,512,512]{2,1,0:T(8,128)(2,1)S(1)}, u32[]{:S(2)}, u32[]{:S(2)}) collective-permute-start(bf16[1,512,512]{2,1,0:T(8,128)(2,1)S(1)} %get-tuple-element.140), channel_id=1, source_target_pairs={{0,1},{1,0},{2,3},{3,2},{4,5},{5,4},{6,7},{7,6},{8,9},{9,8},{10,11... | collective-permute-start | bytes 1572872 | tf_op jit(solution)/shard_map/ppermute | solution.py:431
  323.6 23.1 %collective-permute-start.18 = (bf16[1024,512]{1,0:T(8,128)(2,1)S(1)}, bf16[1024,512]{1,0:T(8,128)(2,1)S(1)}, u32[]{:S(2)}, u32[]{:S(2)}) collective-permute-start(bf16[1024,512]{1,0:T(8,128)(2,1)S(1)} %fusion.refs_0_), channel_id=1, source_target_pairs={{0,1},{1,0},{2,3},{3,2},{4,5},{5,4},{6,7},{7,6},{8,9},{9,8},{10,11... | collective-permute-start | bytes 3145736 | tf_op jit(solution)/shard_map/ppermute | solution.py:431
  324.3 23.9 %collective-permute-start.19 = (bf16[1024,512]{1,0:T(8,128)(2,1)S(1)}, bf16[1024,512]{1,0:T(8,128)(2,1)S(1)}, u32[]{:S(2)}, u32[]{:S(2)}) collective-permute-start(bf16[1024,512]{1,0:T(8,128)(2,1)S(1)} %fusion.refs_0_), channel_id=1, source_target_pairs={{0,2},{1,3},{2,0},{3,1},{4,6},{5,7},{6,4},{7,5},{8,10},{9,11},{10,... | collective-permute-start | bytes 3145736 | tf_op jit(solution)/shard_map/ppermute | solution.py:431
  347.6 11.1 %collective-permute-start.20 = (bf16[512,512]{1,0:T(8,128)(2,1)}, bf16[512,512]{1,0:T(8,128)(2,1)}, u32[]{:S(2)}, u32[]{:S(2)}) collective-permute-start(bf16[512,512]{1,0:T(8,128)(2,1)} %slice.348), channel_id=1, source_target_pairs={{0,2},{1,3},{2,0},{3,1},{4,6},{5,7},{6,4},{7,5},{8,10},{9,11},{10,... | collective-permute-start | bytes 1572872 | tf_op jit(solution)/shard_map/ppermute | solution.py:431
  349.0 10.9 %collective-permute-start.21 = (bf16[512,512]{1,0:T(8,128)(2,1)}, bf16[512,512]{1,0:T(8,128)(2,1)}, u32[]{:S(2)}, u32[]{:S(2)}) collective-permute-start(bf16[512,512]{1,0:T(8,128)(2,1)} %slice.349), channel_id=1, source_target_pairs={{0,1},{1,0},{2,3},{3,2},{4,5},{5,4},{6,7},{7,6},{8,9},{9,8},{10,11... | collective-permute-start | bytes 1572872 | tf_op jit(solution)/shard_map/ppermute | solution.py:431
  389.1 289.3 %reduce-scatter.3.cloned.1.call-start = ((), (), s32[]{:S(2)}) async-start(), calls=%async_computation.5 | async-start | bytes 16515072 | tf_op jit(solution)/shard_map/reduce_scatter | solution.py:918
  390.0 5.7 collective-permute-start.22
  395.7 5.7 collective-permute-start.30
  434.5 23.4 %collective-permute-start.29 = (f32[40,40]{1,0:T(8,128)S(1)}, f32[40,40]{1,0:T(8,128)S(1)}, u32[]{:S(2)}, u32[]{:S(2)}) collective-permute-start(f32[40,40]{1,0:T(8,128)S(1)} %copy-done.27), channel_id=1, source_target_pairs={{0,4},{4,0},{8,12},{12,8},{16,20},{20,16},{24,28},{28,24},{1,5},{5... | collective-permute-start | bytes 19208 | tf_op jit(solution)/shard_map/ppermute | solution.py:431
  436.0 37.0 %collective-permute-start.23 = (bf16[2,1,512,512]{3,2,1,0:T(8,128)(2,1)S(1)}, bf16[2,1,512,512]{3,2,1,0:T(8,128)(2,1)S(1)}, u32[]{:S(2)}, u32[]{:S(2)}) collective-permute-start(bf16[2,1,512,512]{3,2,1,0:T(8,128)(2,1)S(1)} %pad_maximum_fusion.5), channel_id=1, source_target_pairs={{0,1},{1,0},{2,3},{3,2},{4,5},{5,4},{6,7},{7,6},{8,9},{9,8},{10,11... | collective-permute-start | bytes 3145736 | tf_op jit(solution)/shard_map/ppermute | solution.py:431
  436.8 36.2 %collective-permute-start.25 = (bf16[2,1,512,512]{3,2,1,0:T(8,128)(2,1)S(1)}, bf16[2,1,512,512]{3,2,1,0:T(8,128)(2,1)S(1)}, u32[]{:S(2)}, u32[]{:S(2)}) collective-permute-start(bf16[2,1,512,512]{3,2,1,0:T(8,128)(2,1)S(1)} %stack.69), channel_id=1, source_target_pairs={{0,2},{1,3},{2,0},{3,1},{4,6},{5,7},{6,4},{7,5},{8,10},{9,11},{10,... | collective-permute-start | bytes 3145736 | tf_op jit(solution)/shard_map/ppermute | solution.py:431
  456.2 73.6 %collective-permute-start.27 = (bf16[2,2,512,512]{3,2,1,0:T(8,128)(2,1)}, bf16[2,2,512,512]{3,2,1,0:T(8,128)(2,1)S(1)}, u32[]{:S(2)}, u32[]{:S(2)}) collective-permute-start(bf16[2,2,512,512]{3,2,1,0:T(8,128)(2,1)} %pad_maximum_fusion), channel_id=1, source_target_pairs={{0,1},{1,0},{2,3},{3,2},{4,5},{5,4},{6,7},{7,6},{8,9},{9,8},{10,11... | collective-permute-start | bytes 6291464 | tf_op jit(solution)/shard_map/ppermute | solution.py:431
  457.5 72.4 %collective-permute-start.28 = (bf16[2,2,512,512]{3,2,1,0:T(8,128)(2,1)}, bf16[2,2,512,512]{3,2,1,0:T(8,128)(2,1)}, u32[]{:S(2)}, u32[]{:S(2)}) collective-permute-start(bf16[2,2,512,512]{3,2,1,0:T(8,128)(2,1)} %stack.70), channel_id=1, source_target_pairs={{0,2},{1,3},{2,0},{3,1},{4,6},{5,7},{6,4},{7,5},{8,10},{9,11},{10,... | collective-permute-start | bytes 6291464 | tf_op jit(solution)/shard_map/ppermute | solution.py:431
  491.6 38.2 %collective-permute-start.31 = (bf16[2,512,512]{2,1,0:T(8,128)(2,1)}, bf16[2,512,512]{2,1,0:T(8,128)(2,1)}, u32[]{:S(2)}, u32[]{:S(2)}) collective-permute-start(bf16[2,512,512]{2,1,0:T(8,128)(2,1)} %pad_maximum_fusion.6), channel_id=1, source_target_pairs={{0,1},{1,0},{2,3},{3,2},{4,5},{5,4},{6,7},{7,6},{8,9},{9,8},{10,11... | collective-permute-start | bytes 3145736 | tf_op jit(solution)/shard_map/ppermute | solution.py:431
  492.5 37.4 %collective-permute-start.32 = (bf16[2,512,512]{2,1,0:T(8,128)(2,1)}, bf16[2,512,512]{2,1,0:T(8,128)(2,1)}, u32[]{:S(2)}, u32[]{:S(2)}) collective-permute-start(bf16[2,512,512]{2,1,0:T(8,128)(2,1)} %stack.71), channel_id=1, source_target_pairs={{0,2},{1,3},{2,0},{3,1},{4,6},{5,7},{6,4},{7,5},{8,10},{9,11},{10,... | collective-permute-start | bytes 3145736 | tf_op jit(solution)/shard_map/ppermute | solution.py:431
  531.5 17.1 %collective-permute-start.24 = (bf16[1,1,512,512]{3,2,1,0:T(8,128)(2,1)S(1)}, bf16[1,1,512,512]{3,2,1,0:T(8,128)(2,1)S(1)}, u32[]{:S(2)}, u32[]{:S(2)}) collective-permute-start(bf16[1,1,512,512]{3,2,1,0:T(8,128)(2,1)S(1)} %get-tuple-element.135), channel_id=1, source_target_pairs={{0,2},{1,3},{2,0},{3,1},{4,6},{5,7},{6,4},{7,5},{8,10},{9,11},{10,... | collective-permute-start | bytes 1572872 | tf_op jit(solution)/shard_map/ppermute | solution.py:431
  536.3 46.2 %collective-permute-start.33 = (bf16[1,2,512,512]{3,2,1,0:T(8,128)(2,1)S(1)}, bf16[1,2,512,512]{3,2,1,0:T(8,128)(2,1)S(1)}, u32[]{:S(2)}, u32[]{:S(2)}) collective-permute-start(bf16[1,2,512,512]{3,2,1,0:T(8,128)(2,1)S(1)} %get-tuple-element.123), channel_id=1, source_target_pairs={{0,2},{1,3},{2,0},{3,1},{4,6},{5,7},{6,4},{7,5},{8,10},{9,11},{10,... | collective-permute-start | bytes 3145736 | tf_op jit(solution)/shard_map/ppermute | solution.py:431
  536.8 45.6 %collective-permute-start.34 = (bf16[1,2,512,512]{3,2,1,0:T(8,128)(2,1)S(1)}, bf16[1,2,512,512]{3,2,1,0:T(8,128)(2,1)S(1)}, u32[]{:S(2)}, u32[]{:S(2)}) collective-permute-start(bf16[1,2,512,512]{3,2,1,0:T(8,128)(2,1)S(1)} %get-tuple-element.122), channel_id=1, source_target_pairs={{0,1},{1,0},{2,3},{3,2},{4,5},{5,4},{6,7},{7,6},{8,9},{9,8},{10,11... | collective-permute-start | bytes 3145736 | tf_op jit(solution)/shard_map/ppermute | solution.py:431
  537.9 4.2 collective-permute-start.37
  542.1 5.3 collective-permute-start.38
  542.7 31.4 %collective-permute-start.26 = (bf16[1,1,512,512]{3,2,1,0:T(8,128)(2,1)S(1)}, bf16[1,1,512,512]{3,2,1,0:T(8,128)(2,1)S(1)}, u32[]{:S(2)}, u32[]{:S(2)}) collective-permute-start(bf16[1,1,512,512]{3,2,1,0:T(8,128)(2,1)S(1)} %get-tuple-element.134), channel_id=1, source_target_pairs={{0,1},{1,0},{2,3},{3,2},{4,5},{5,4},{6,7},{7,6},{8,9},{9,8},{10,11... | collective-permute-start | bytes 1572872 | tf_op jit(solution)/shard_map/ppermute | solution.py:431
  547.5 30.8 %collective-permute-start.35 = (bf16[1,512,512]{2,1,0:T(8,128)(2,1)S(1)}, bf16[1,512,512]{2,1,0:T(8,128)(2,1)S(1)}, u32[]{:S(2)}, u32[]{:S(2)}) collective-permute-start(bf16[1,512,512]{2,1,0:T(8,128)(2,1)S(1)} %get-tuple-element.131), channel_id=1, source_target_pairs={{0,2},{1,3},{2,0},{3,1},{4,6},{5,7},{6,4},{7,5},{8,10},{9,11},{10,... | collective-permute-start | bytes 1572872 | tf_op jit(solution)/shard_map/ppermute | solution.py:431
  548.7 33.7 %collective-permute-start.36 = (bf16[1,512,512]{2,1,0:T(8,128)(2,1)S(1)}, bf16[1,512,512]{2,1,0:T(8,128)(2,1)S(1)}, u32[]{:S(2)}, u32[]{:S(2)}) collective-permute-start(bf16[1,512,512]{2,1,0:T(8,128)(2,1)S(1)} %get-tuple-element.130), channel_id=1, source_target_pairs={{0,1},{1,0},{2,3},{3,2},{4,5},{5,4},{6,7},{7,6},{8,9},{9,8},{10,11... | collective-permute-start | bytes 1572872 | tf_op jit(solution)/shard_map/ppermute | solution.py:431
  611.2 5.9 collective-permute-start.39
  618.0 5.7 collective-permute-start.41
  619.4 4.3 collective-permute-start.42
  623.8 5.4 collective-permute-start.43
  629.2 4.3 collective-permute-start.44
  633.5 21.9 %collective-permute-start.45 = (f32[8,2048]{1,0:T(8,128)S(1)}, f32[8,2048]{1,0:T(8,128)S(1)}, u32[]{:S(2)}, u32[]{:S(2)}) collective-permute-start(f32[8,2048]{1,0:T(8,128)S(1)} %add_dynamic-update-slice_fusion), channel_id=1, source_target_pairs={{0,2},{1,3},{2,0},{3,1},{4,6},{5,7},{6,4},{7,5},{8,10},{9,11},{10,... | collective-permute-start | bytes 196616 | tf_op jit(solution)/shard_map/ppermute | solution.py:431
  (35 other events, 523.5 us)
Sparse Core Ops, SparseCore 0:
  9.6 68.2 all-gather.5
  79.5 80.6 all-gather.3
  162.4 98.3 all-gather.7
  389.2 108.6 reduce-scatter.4
  530.0 148.3 reduce-scatter.2

commit v4 on v3

--- a/solution.py
+++ b/solution.py
@@ -575,8 +575,9 @@
         smalls[:, : 2 * STREAMS].astype(F32), tensor_place * width, width, 0
     ).T
     gain_own, bias_own = norm_own[:STREAMS], norm_own[STREAMS:]
-    qkv_full = lax.all_gather(qkv_weight, "dp", axis=1, tiled=True)
-    up_full = lax.all_gather(up_weight, "dp", axis=0, tiled=True)
+    wide_full = lax.all_gather(
+        jnp.concatenate([up_weight, *qkv_weight], 1), "dp", axis=0, tiled=True
+    )
     both_full = lax.all_gather(
         jnp.concatenate([down_weight, out_weight], 0), "dp", axis=1, tiled=True
     )
@@ -625,8 +626,9 @@
     first_own, first_arrived = gather_start(normed_first)
     first_arrived = [after(arrived, fixed_part) for arrived in first_arrived]
     first_pieces = gather_finish((first_own, first_arrived))
-    last_pieces = gather_pieces(normed_last)
-    first_pieces = after(first_pieces, cot_pieces)
+    last_own, last_arrived = gather_start(
+        after(normed_last, *[part for parts in first_pieces[1:] for part in parts])
+    )
 
     places = (jnp.arange(tokens, dtype=jnp.int32) % LENGTH).astype(F32)
     freqs = jnp.power(10000.0, -jnp.arange(0, ROT, 2).astype(F32) / ROT)
@@ -650,7 +652,7 @@
             for part in parts
         ]
         + [
-            (qkv_full, (None, width, heads_width), lambda c, p, r=r: (c, p[0] ^ r, 0))
+            (wide_full, (width, heads_width), lambda c, p, r=r: (p[0] ^ r, hidden_steps + c))
             for r in range(count)
         ]
         + table_ins,
@@ -669,12 +671,14 @@
         name="attend",
         flops=4 * tokens * tokens * heads_width,
     )
+    last_pieces = gather_finish((last_own, [after(arrived, qkv) for arrived in last_arrived]))
+    last_pieces[0] = [after(part, attended) for part in last_pieces[0]]
     step = min(512, hidden_width)
     hidden, slope = call(
         functools.partial(up_kernel, [len(parts) for parts in last_pieces]),
         (hidden_width // step,),
         ins=[(part, part.shape, const(0, 0)) for parts in last_pieces for part in parts]
-        + [(up_full, (width, step), lambda j, p, r=r: (p[0] ^ r, j)) for r in range(count)],
+        + [(wide_full, (width, step), lambda j, p, r=r: (p[0] ^ r, j)) for r in range(count)],
         outs=[((tokens, hidden_width), BF16, (tokens, step), lambda j, p: (0, j))] * 2,
         name="up",
         flops=2 * tokens * width_all * hidden_width,
@@ -684,7 +688,7 @@
     seed = (mix_cotangent * jnp.repeat(seq_scale, LENGTH)[None, :]).T.astype(BF16)
     factor = jnp.repeat(seq_scale, LENGTH)[:, None]
     seed, factor, mix_full = lax.optimization_barrier((seed, factor, mix_full))
-    hidden = after(hidden, seed, factor, mix_full)
+    hidden = after(hidden, seed, factor, mix_full, cot_pieces)
     chunks = 1
     rows = tokens // chunks
     block_owns, block_states, held = [], [], hidden
@@ -774,10 +778,6 @@
     branch_grad = after(branch_grad, both_part)
     branch_in = (branch_grad, (tokens, width_all), const(0, 0))
     tensor_bits = axis_bits("tensor")
-    fixed_sums = after(fixed_part, branch_pieces)
-    fixed_sums = fixed_sums + swap(fixed_sums, "tensor", tensor_bits[0])
-    branch_grad = after(branch_grad, fixed_sums)
-    branch_in = (branch_grad, (tokens, width_all), const(0, 0))
     (attended_grad,) = call(
         back_kernel,
         (tokens // ROWS,),
@@ -789,10 +789,6 @@
         name="attended_grad",
         flops=2 * tokens * width_all * heads_width,
     )
-    for bit in tensor_bits[1:]:
-        fixed_sums = fixed_sums + swap(fixed_sums, "tensor", bit)
-    next_bits = axis_bits("dp")
-    next_sum = next_part + swap(next_part, "dp", next_bits[0])
     lin_grads = pl.pallas_call(
         attend_back_kernel,
         out_shape=jax.ShapeDtypeStruct((3, tokens, heads_width), BF16),
@@ -819,7 +815,11 @@
             (end - begin, count),
             ins=[
                 (grads, (None, tokens, heads_width), lambda c, r, p: (c + begin, 0, 0)),
-                (qkv_full, (None, width, heads_width), lambda c, r, p: (c + begin, p[0] ^ r, 0)),
+                (
+                    wide_full,
+                    (width, heads_width),
+                    lambda c, r, p: (p[0] ^ r, hidden_steps + c + begin),
+                ),
             ],
             outs=[
                 (
@@ -838,7 +838,7 @@
     lin_grads = after(lin_grads, grads_a)
     grads_b = qkv_back(lin_grads, 1, 3)
     states_b = scatter_start(grads_b)
-    branch_grad = after(branch_grad, grads_b, next_sum, fixed_sums)
+    branch_grad = after(branch_grad, grads_b)
     branch_in = (branch_grad, (tokens, width_all), const(0, 0))
     (hidden_grad,) = call(
         hidden_grad_kernel,
@@ -858,16 +858,17 @@
         (count,),
         ins=[
             (hidden_grad, (tokens, hidden_width), const(0, 0)),
-            (up_full, (width, hidden_width), lambda r, p: (p[0] ^ r, 0)),
+            (wide_full, (width, hidden_width), lambda r, p: (p[0] ^ r, 0)),
         ],
         outs=[((count, tokens, width), BF16, (None, tokens, width), lambda r, p: (r, 0, 0))],
         name="up_back",
         flops=2 * tokens * width_all * hidden_width,
     )
     last_states = scatter_start(last_grads)
+    next_bits = axis_bits("dp")
+    fixed_got = swap(after(fixed_part, hidden_grad), "tensor", tensor_bits[0])
+    next_got = swap(after(next_part, hidden_grad), "dp", next_bits[0])
     hidden_grad = after(hidden_grad, last_grads)
-    for bit in next_bits[1:]:
-        next_sum = next_sum + swap(next_sum, "dp", bit)
     all_steps = hidden_steps + 3
     lin_step = lambda j: jnp.maximum(j - hidden_steps, 0)
     (wide_part,) = call(
@@ -903,12 +904,19 @@
     )
     wide_part = after(
         wide_part,
+        fixed_got,
+        next_got,
         *scatter_arrived(states_b),
         *scatter_arrived(last_states),
     )
+    fixed_sums = fixed_part + fixed_got
+    for bit in tensor_bits[1:]:
+        fixed_sums = fixed_sums + swap(fixed_sums, "tensor", bit)
+    next_sum = next_part + next_got
+    next_sum = next_sum + swap(next_sum, "dp", next_bits[1])
     together(states_b + last_states)
     later = [scatter_second(states) for states in (states_a, states_b, last_states)]
-    together([state for states in later for state in states])
+    together([state for states in later for state in states] + [[None, None, next_sum]])
     first_grad = jnp.concatenate([scatter_end(later[0]), scatter_end(later[1])], 0)
     last_grad = scatter_end(later[2])
     both_grad = lax.psum_scatter(both_part, "dp", scatter_dimension=1, tiled=True).astype(F32)
@@ -931,7 +939,6 @@
         stats_in,
         gain_in,
     ]
-    grad_ins[0] = (after(first_grad, next_sum), *grad_ins[0][1:])
     block_grad_in = (block_grad, (LANES, width), lambda i, p: (i, 0))
     sums, norm_part = call(
         functools.partial(sums_kernel, width_all),
@@ -946,7 +953,9 @@
     dp_bits = axis_bits("dp")
     sums = sums + swap(sums, "tensor", tensor_bits[0])
     norm_part = norm_part + swap(norm_part, "dp", dp_bits[0])
-    sums, norm_part = lax.optimization_barrier((sums, norm_part))
+    for bit in next_bits[2:]:
+        next_sum = next_sum + swap(next_sum, "dp", bit)
+    sums, norm_part, next_sum = lax.optimization_barrier((sums, norm_part, next_sum))
     for bit in tensor_bits[1:]:
         sums = sums + swap(sums, "tensor", bit)
     norm_part = norm_part + swap(norm_part, "dp", dp_bits[1])

time: 702 us -> 679 us (0.967)
  waiting for transfers between devices: 264 us -> 237 us
    ppermute x46, waiting for transfers between devices: 244 us -> 220 us  [swap(): return lax.ppermute(values, axis, [(i, i ^ bit) for i in range(count)])]
    reduce_scatter x1, waiting for transfers between devices: 17.7 us -> 9.65 us  [per_device(): lax.psum_scatter(wide_part, 'dp', scatter_dimension=0, tiled=True)]
  transfers between devices with their start and end apart: 51 -> 50, of which waited for: 29 -> 27; matrix products, arithmetic and copies ran while one was open for 9% -> 9% of each run, Pallas kernels for 34% -> 35%
where the time goes in v4:
time: 679 us; the launch traced here: 667 us
  Pallas kernels  277 us (41%)
  waiting for transfers between devices  237 us (35%)
  starting transfers between devices  42.9 us (6%)
  other arithmetic  41.5 us (6%)
  local copies, waits for them, and re-layouts  38.1 us (6%)
  between operations  15.2 us (2%)
  blocking collectives  14.8 us (2%)
    pallas_call x17, Pallas kernels, kernel_call(): return call(place, *[a for a, _, _ in ins])  260 us
    ppermute x46, waiting for transfers between devices, swap(): return lax.ppermute(values, axis, [(i, i ^ bit) for i in range(count)])  220 us
    ppermute x46, starting transfers between devices, swap(): return lax.ppermute(values, axis, [(i, i ^ bit) for i in range(count)])  42.8 us
    pallas_call x1, Pallas kernels, per_device(): pl.pallas_call(attend_back_kernel, out_shape=jax.ShapeDtypeStruct((3, tok...  17.5 us
    all_gather x1, blocking collectives, per_device(): smalls = lax.all_gather(smalls, 'dp', axis=0, tiled=True)  14.8 us
  transfers between devices with their start and end apart: 50, of which 27 were waited for; matrix products, arithmetic and copies ran while one was open for 9% of the time, Pallas kernels for 35%

profile of v4, /device:TPU:0, one launch (start us, length us, event | category | flops | bytes accessed | tf_op | source)
XLA Modules:
  0.0 666.9 jit_solution(1301592203349375037)
XLA Ops:
  11.8 3.0 collective-permute-start.1
  16.3 14.8 %all_gather.9 = bf16[2048,48]{0,1:T(8,128)(2,1)S(1)} all-gather(bf16[256,48]{0,1:T(8,128)(2,1)S(1)} %pad_maximum_fusion.8), channel_id=1, replica_groups=mesh['dp'=8,'tensor'=4] {'dp'}, dimensions={0}, use_global_device_ids=true | all-gather | bytes 221184 | tf_op jit(solution)/shard_map/all_gather | solution.py:572
  33.7 14.3 %mix.1 = (f32[4,1024,512]{2,1,0:T(8,128)}, f32[8,1024]{1,0:T(8,128)}) custom-call(s32[2]{0:T(128)} %pad_add_fusion.place, bf16[9,1024,512]{2,1,0:T(8,128)(2,1)} %hist.5, f32[1024,36]{1,0:T(8,128)} %bitcast.43), custom_call_target="tpu_custom_call" | custom-call | flops 37748736 | bytes 18006016 | tf_op jit(solution)/shard_map/mix/pallas_call | solution.py:58
  48.6 3.7 collective-permute-done.2
  54.1 2.9 collective-permute-done.3
  57.6 9.6 %norm.1 = (bf16[3,1024,512]{2,1,0:T(8,128)(2,1)}, bf16[1024,512]{1,0:T(8,128)(2,1)}) custom-call(s32[2]{0:T(128)} %pad_add_fusion.place, f32[4,1024,512]{2,1,0:T(8,128)} %get-tuple-element.69.streams, f32[8,1024]{1,0:T(8,128)} %add.235.stats, f32[4,512]{1,0:T(4,128)} %get-tuple-element.153.gain, f32[4,512]{1,0:T(4,128)} %get-tuple-element.152.bias), custom_call_target="tpu_custom_call" | custom-call | bytes 12632064 | tf_op jit(solution)/shard_map/norm/pallas_call | solution.py:58
  68.0 14.8 %spread.1 = f32[48,1024]{1,0:T(8,128)} custom-call(s32[2]{0:T(128)} %pad_add_fusion.place, f32[4,1024,512]{2,1,0:T(8,128)} %get-tuple-element.69.streams, f32[8,1024]{1,0:T(8,128)} %add.235.stats, bf16[9,1024,512]{2,1,0:T(8,128)(2,1)} %hist.5), custom_call_target="tpu_custom_call" | custom-call | bytes 18055168 | tf_op jit(solution)/shard_map/spread/pallas_call | solution.py:58
  82.8 53.7 %collective-permute-done.5.refs_2_.refs_7_ = bf16[3,1024,512]{2,1,0:T(8,128)(2,1)S(1)} collective-permute-done((bf16[3,1024,512]{2,1,0:T(8,128)(2,1)}, bf16[3,1024,512]{2,1,0:T(8,128)(2,1)S(1)}, u32[]{:S(2)}, u32[]{:S(2)}) %collective-permute-start.5) | collective-permute-done | bytes 3145760 | tf_op jit(solution)/shard_map/ppermute | solution.py:431
  143.4 29.3 %collective-permute-done.7.refs_4_.refs_9_ = bf16[3,512,512]{2,1,0:T(8,128)(2,1)} collective-permute-done((bf16[3,512,512]{2,1,0:T(8,128)(2,1)}, bf16[3,512,512]{2,1,0:T(8,128)(2,1)}, u32[]{:S(2)}, u32[]{:S(2)}) %collective-permute-start.7) | collective-permute-done | bytes 1572896 | tf_op jit(solution)/shard_map/ppermute | solution.py:431
  178.4 15.4 %qkv.1.q.k.v = bf16[3,1024,512]{2,1,0:T(8,128)(2,1)} custom-call(s32[2]{0:T(128)} %pad_add_fusion.place, bf16[3,1024,512]{2,1,0:T(8,128)(2,1)} %get-tuple-element.68.refs_0_.refs_5_, bf16[3,1024,512]{2,1,0:T(8,128)(2,1)} %copy-done.3, bf16[3,1024,512]{2,1,0:T(8,128)(2,1)} %copy-done.2, bf16[3,512,512]{2,1,0:T(8,128)(2,1)} %collective-permute-done.6.refs_3_.refs_8_, ...), custom_call_target="tpu_custom_call" | custom-call | flops 6442450944 | bytes 76021760 | tf_op jit(solution)/shard_map/qkv/pallas_call | solution.py:58
  193.9 2.5 collective-permute-done.9.refs_2_
  199.1 2.1 collective-permute-start.10
  205.3 11.5 %attend.1.attended = bf16[1024,512]{1,0:T(8,128)(2,1)} custom-call(s32[2]{0:T(128)} %pad_add_fusion.place, bf16[3,1024,512]{2,1,0:T(8,128)(2,1)} %qkv.1.q.k.v, bf16[3,1024,512]{2,1,0:T(8,128)(2,1)} %qkv.1.q.k.v, bf16[3,1024,512]{2,1,0:T(8,128)(2,1)} %qkv.1.q.k.v), custom_call_target="tpu_custom_call" | custom-call | flops 2147483648 | bytes 10485760 | tf_op jit(solution)/shard_map/attend/pallas_call | solution.py:58
  218.4 21.2 %up.1 = (bf16[1024,2048]{1,0:T(8,128)(2,1)}, bf16[1024,2048]{1,0:T(8,128)(2,1)}) custom-call(s32[2]{0:T(128)} %pad_add_fusion.place, bf16[1024,512]{1,0:T(8,128)(2,1)} %get-tuple-element.73.refs_0_, bf16[1024,512]{1,0:T(8,128)(2,1)} %copy-done.8, bf16[1024,512]{1,0:T(8,128)(2,1)} %copy-done.7, bf16[512,512]{1,0:T(8,128)(2,1)} %copy-done.24, ...), custom_call_target="tpu_custom_call" | custom-call | flops 8589934592 | bytes 71303168 | tf_op jit(solution)/shard_map/up/pallas_call | solution.py:58
  239.6 7.4 %all-gather.5.cloned.1.call-done.down.out.weight = bf16[2560,2048]{1,0:T(8,128)(2,1)} async-done(((bf16[2560,256]{1,0:T(8,128)(2,1)}), bf16[2560,2048]{1,0:T(8,128)(2,1)}) %all-gather.5.cloned.1.call-update) | async-done | bytes 10485776 | tf_op jit(solution)/shard_map/all_gather | solution.py:581
  247.0 16.5 %down.1 = bf16[4,1024,512]{2,1,0:T(8,128)(2,1)} custom-call(s32[2]{0:T(128)} %pad_add_fusion.place, bf16[1024,2048]{1,0:T(8,128)(2,1)} %get-tuple-element.80.hidden, bf16[1024,512]{1,0:T(8,128)(2,1)} %attend.1.attended, bf16[2560,2048]{1,0:T(8,128)(2,1)} %all-gather.5.cloned.1.call-done.down.out.weight, ...), custom_call_target="tpu_custom_call" | custom-call | flops 10737418240 | bytes 30408704 | tf_op jit(solution)/shard_map/down/pallas_call | solution.py:58
  269.4 22.3 %collective-permute-done.14 = bf16[2,512,512]{2,1,0:T(8,128)(2,1)S(1)} collective-permute-done((bf16[2,512,512]{2,1,0:T(8,128)(2,1)S(1)}, bf16[2,512,512]{2,1,0:T(8,128)(2,1)S(1)}, u32[]{:S(2)}, u32[]{:S(2)}) %collective-permute-start.14) | collective-permute-done | bytes 1048608 | tf_op jit(solution)/shard_map/ppermute | solution.py:431
  295.3 10.9 %collective-permute-done.17 = bf16[1,512,512]{2,1,0:T(8,128)(2,1)S(1)} collective-permute-done((bf16[1,512,512]{2,1,0:T(8,128)(2,1)S(1)}, bf16[1,512,512]{2,1,0:T(8,128)(2,1)S(1)}, u32[]{:S(2)}, u32[]{:S(2)}) %collective-permute-start.17) | collective-permute-done | bytes 524320 | tf_op jit(solution)/shard_map/ppermute | solution.py:431
  312.0 20.0 %collective-permute-done.19.refs_2_ = bf16[1024,512]{1,0:T(8,128)(2,1)S(1)} collective-permute-done((bf16[1024,512]{1,0:T(8,128)(2,1)S(1)}, bf16[1024,512]{1,0:T(8,128)(2,1)S(1)}, u32[]{:S(2)}, u32[]{:S(2)}) %collective-permute-start.19) | collective-permute-done | bytes 1048608 | tf_op jit(solution)/shard_map/ppermute | solution.py:431
  337.8 6.9 %collective-permute-done.21.refs_4_ = bf16[512,512]{1,0:T(8,128)(2,1)} collective-permute-done((bf16[512,512]{1,0:T(8,128)(2,1)}, bf16[512,512]{1,0:T(8,128)(2,1)}, u32[]{:S(2)}, u32[]{:S(2)}) %collective-permute-start.21) | collective-permute-done | bytes 524320 | tf_op jit(solution)/shard_map/ppermute | solution.py:431
  346.1 11.4 %middle.1 = (bf16[1024,2048]{1,0:T(8,128)(2,1)}, f32[1024,512]{1,0:T(8,128)}, f32[40,1024]{1,0:T(8,128)}, f32[40,40]{1,0:T(8,128)}, f32[40,2048]{1,0:T(8,128)}) custom-call(s32[2]{0:T(128)} %pad_add_fusion.place, bf16[1024,512]{1,0:T(8,128)(2,1)} %copy-done.6, bf16[1024,512]{1,0:T(8,128)(2,1)} %copy-done.14, bf16[1024,512]{1,0:T(8,128)(2,1)} %copy-done.13, ...), custom_call_target="tpu_custom_call" | custom-call | flops 503316480 | bytes 15922560 | tf_op jit(solution)/shard_map/middle/pallas_call | solution.py:58
  358.5 16.9 %down_grad.1 = bf16[2608,2048]{1,0:T(8,128)(2,1)} custom-call(s32[2]{0:T(128)} %pad_add_fusion.place, bf16[1024,2048]{1,0:T(8,128)(2,1)} %get-tuple-element.80.hidden, bf16[1024,512]{1,0:T(8,128)(2,1)} %attend.1.attended, bf16[1024,2048]{1,0:T(8,128)(2,1)} %get-tuple-element.90.branch_grad.grad), custom_call_target="tpu_custom_call" | custom-call | flops 10737418240 | bytes 20119552 | tf_op jit(solution)/shard_map/down_grad/pallas_call | solution.py:58
  376.1 7.4 %attended_grad.1.grad = bf16[1024,512]{1,0:T(8,128)(2,1)} custom-call(s32[2]{0:T(128)} %pad_add_fusion.place, bf16[1024,2048]{1,0:T(8,128)(2,1)} %get-tuple-element.90.branch_grad.grad, bf16[2560,2048]{1,0:T(8,128)(2,1)} %all-gather.5.cloned.1.call-done.down.out.weight), custom_call_target="tpu_custom_call" | custom-call | flops 2147483648 | bytes 15728640 | tf_op jit(solution)/shard_map/attended_grad/pallas_call | solution.py:58
  383.6 17.5 %attend_back.1.grad.refs_11_ = bf16[3,1024,512]{2,1,0:T(8,128)(2,1)} custom-call(s32[2]{0:T(128)} %pad_add_fusion.place, bf16[3,1024,512]{2,1,0:T(8,128)(2,1)} %qkv.1.q.k.v, bf16[3,1024,512]{2,1,0:T(8,128)(2,1)} %qkv.1.q.k.v, bf16[3,1024,512]{2,1,0:T(8,128)(2,1)} %qkv.1.q.k.v, bf16[1024,512]{1,0:T(8,128)(2,1)} %attended_grad.1.grad, ...), custom_call_target="tpu_custom_call" | custom-call | flops 5368709120 | bytes 8388608 | tf_op jit(solution)/shard_map/attend_back/pallas_call | solution.py:792
  401.1 6.9 %qkv_back.2 = bf16[4,1,1024,512]{3,2,1,0:T(8,128)(2,1)} custom-call(s32[2]{0:T(128)} %pad_add_fusion.place, bf16[3,1024,512]{2,1,0:T(8,128)(2,1)} %attend_back.1.grad.refs_11_, bf16[2048,3584]{1,0:T(8,128)(2,1)} %all-gather.3.cloned.1.call-done.refs_5_.refs_6_.refs_7_.refs_8_.weight), custom_call_target="tpu_custom_call" | custom-call | flops 2147483648 | bytes 22020096 | tf_op jit(solution)/shard_map/qkv_back/pallas_call | solution.py:58
  413.2 11.5 %qkv_back.3 = bf16[4,2,1024,512]{3,2,1,0:T(8,128)(2,1)} custom-call(s32[2]{0:T(128)} %pad_add_fusion.place, bf16[3,1024,512]{2,1,0:T(8,128)(2,1)} %attend_back.1.grad.refs_11_, bf16[2048,3584]{1,0:T(8,128)(2,1)} %all-gather.3.cloned.1.call-done.refs_5_.refs_6_.refs_7_.refs_8_.weight), custom_call_target="tpu_custom_call" | custom-call | flops 4294967296 | bytes 26214400 | tf_op jit(solution)/shard_map/qkv_back/pallas_call | solution.py:58
  426.4 3.1 stack.70
  432.8 15.1 %hidden_grad.1.grad.refs_10_ = bf16[1024,2048]{1,0:T(8,128)(2,1)} custom-call(s32[2]{0:T(128)} %pad_add_fusion.place, bf16[1024,2048]{1,0:T(8,128)(2,1)} %get-tuple-element.90.branch_grad.grad, bf16[2560,2048]{1,0:T(8,128)(2,1)} %all-gather.5.cloned.1.call-done.down.out.weight, bf16[1024,2048]{1,0:T(8,128)(2,1)} %get-tuple-element.91.slope), custom_call_target="tpu_custom_call" | custom-call | flops 8589934592 | bytes 23068672 | tf_op jit(solution)/shard_map/hidden_grad/pallas_call | solution.py:58
  447.9 14.1 %up_back.1 = bf16[4,1024,512]{2,1,0:T(8,128)(2,1)} custom-call(s32[2]{0:T(128)} %pad_add_fusion.place, bf16[1024,2048]{1,0:T(8,128)(2,1)} %hidden_grad.1.grad.refs_10_, bf16[2048,3584]{1,0:T(8,128)(2,1)} %all-gather.3.cloned.1.call-done.refs_5_.refs_6_.refs_7_.refs_8_.weight), custom_call_target="tpu_custom_call" | custom-call | flops 8589934592 | bytes 23068672 | tf_op jit(solution)/shard_map/up_back/pallas_call | solution.py:58
  462.0 2.3 stack.71
  470.8 35.8 %weight_grad.1 = bf16[2048,3584]{1,0:T(8,128)(2,1)} custom-call(s32[2]{0:T(128)} %pad_add_fusion.place, bf16[1024,512]{1,0:T(8,128)(2,1)} %get-tuple-element.73.refs_0_, bf16[1024,512]{1,0:T(8,128)(2,1)} %copy-done.8, bf16[1024,512]{1,0:T(8,128)(2,1)} %copy-done.7, bf16[512,512]{1,0:T(8,128)(2,1)} %copy-done.24, bf16[512,512]{1,0:T(8,128)(2,1)} %copy-done.23, ...), custom_call_target="tpu_custom_call" | custom-call | flops 15032385536 | bytes 38797312 | tf_op jit(solution)/shard_map/weight_grad/pallas_call | solution.py:58
  509.4 4.0 add_convert_fusion
  514.0 2.0 collective-permute-start.23
  517.6 2.9 collective-permute-done.35
  523.9 27.5 %collective-permute-done.23 = bf16[1,1,512,512]{3,2,1,0:T(8,128)(2,1)S(1)} collective-permute-done((bf16[1,1,512,512]{3,2,1,0:T(8,128)(2,1)S(1)}, bf16[1,1,512,512]{3,2,1,0:T(8,128)(2,1)S(1)}, u32[]{:S(2)}, u32[]{:S(2)}) %collective-permute-start.23) | collective-permute-done | bytes 524320 | tf_op jit(solution)/shard_map/ppermute | solution.py:431
  551.3 4.2 collective-permute-done.33
  555.5 4.8 collective-permute-done.32
  565.0 2.7 add_bitcast_fusion.1
  567.8 3.2 maximum_maximum_fusion.first
  570.9 17.9 %sums.1 = (f32[48,1024]{1,0:T(8,128)}, f32[8,512]{1,0:T(8,128)}) custom-call(s32[2]{0:T(128)} %pad_add_fusion.place, f32[3,1024,512]{2,1,0:T(8,128)} %maximum_maximum_fusion.first, f32[1024,512]{1,0:T(8,128)} %pad_maximum_fusion.1.last, f32[4,1024,512]{2,1,0:T(8,128)} %get-tuple-element.69.streams, f32[8,1024]{1,0:T(8,128)} %add.235.stats, ...), custom_call_target="tpu_custom_call" | custom-call | bytes 28565504 | tf_op jit(solution)/shard_map/sums/pallas_call | solution.py:58
  590.6 5.6 collective-permute-done.38
  600.7 4.0 collective-permute-done.42
  605.1 2.7 collective-permute-done.39
  608.0 5.3 collective-permute-done.43
  613.8 3.9 collective-permute-done.44
  619.2 19.6 %history.1 = f32[9,1024,512]{2,1,0:T(8,128)} custom-call(s32[2]{0:T(128)} %pad_add_fusion.place, f32[3,1024,512]{2,1,0:T(8,128)} %maximum_maximum_fusion.first, f32[1024,512]{1,0:T(8,128)} %pad_maximum_fusion.1.last, f32[4,1024,512]{2,1,0:T(8,128)} %get-tuple-element.69.streams, f32[8,1024]{1,0:T(8,128)} %add.235.stats, f32[4,512]{1,0:T(4,128)} %get-tuple-element.153.gain, ...), custom_call_target="tpu_custom_call" | custom-call | bytes 37969920 | tf_op jit(solution)/shard_map/history/pallas_call | solution.py:58
  641.2 2.8 slice.379
  644.8 9.7 %reduce-scatter.3.cloned.1.call-done = bf16[256,3584]{1,0:T(8,128)(2,1)} async-done(((bf16[2048,3584]{1,0:T(8,128)(2,1)}), bf16[256,3584]{1,0:T(8,128)(2,1)}) %reduce-scatter.3.cloned.1.call-update) | async-done | bytes 1835024 | tf_op jit(solution)/shard_map/reduce_scatter | solution.py:926
  (236 shorter events, 104.2 us)
Async XLA Ops:
  7.2 171.2 %all-gather.3.cloned.1.call-start = ((), (), s32[]{:S(2)}) async-start(), calls=%async_computation.2 | async-start | bytes 16515072 | tf_op jit(solution)/shard_map/all_gather | solution.py:578
  10.1 236.9 %all-gather.5.cloned.1.call-start = ((), (), s32[]{:S(2)}) async-start(), calls=%async_computation.3 | async-start | bytes 11796480 | tf_op jit(solution)/shard_map/all_gather | solution.py:581
  11.7 627.7 %reduce-scatter.5.cloned.1.call-start = ((), (), s32[]{:S(2)}) async-start(), calls=%async_computation.5 | async-start | bytes 12017664 | tf_op jit(solution)/shard_map/reduce_scatter | solution.py:922
  11.8 36.3 %collective-permute-start.1 = (bf16[1024,512]{1,0:T(8,128)(2,1)S(1)}, bf16[1024,512]{1,0:T(8,128)(2,1)S(1)}, u32[]{:S(2)}, u32[]{:S(2)}) collective-permute-start(bf16[1024,512]{1,0:T(8,128)(2,1)S(1)} %copy-done.20), channel_id=1, source_target_pairs={{0,2},{1,3},{2,0},{3,1},{4,6},{5,7},{6,4},{7,5},{8,10},{9,11},{10,... | collective-permute-start | bytes 3145736 | tf_op jit(solution)/shard_map/ppermute | solution.py:431
  14.8 33.3 %collective-permute-start = (bf16[1024,512]{1,0:T(8,128)(2,1)S(1)}, bf16[1024,512]{1,0:T(8,128)(2,1)S(1)}, u32[]{:S(2)}, u32[]{:S(2)}) collective-permute-start(bf16[1024,512]{1,0:T(8,128)(2,1)S(1)} %copy-done.20), channel_id=1, source_target_pairs={{0,1},{1,0},{2,3},{3,2},{4,5},{5,4},{6,7},{7,6},{8,9},{9,8},{10,11... | collective-permute-start | bytes 3145736 | tf_op jit(solution)/shard_map/ppermute | solution.py:431
  67.2 69.3 %collective-permute-start.5 = (bf16[3,1024,512]{2,1,0:T(8,128)(2,1)}, bf16[3,1024,512]{2,1,0:T(8,128)(2,1)S(1)}, u32[]{:S(2)}, u32[]{:S(2)}) collective-permute-start(bf16[3,1024,512]{2,1,0:T(8,128)(2,1)} %get-tuple-element.68.refs_0_.refs_5_), channel_id=1, source_target_pairs={{0,2},{1,3},{2,0},{3,1},{4,6},{5,7},{6,4},{7,5},{8,10},{9,11},{10,... | collective-permute-start | bytes 9437192 | tf_op jit(solution)/shard_map/ppermute | solution.py:431
  67.8 70.4 %collective-permute-start.4 = (bf16[3,1024,512]{2,1,0:T(8,128)(2,1)}, bf16[3,1024,512]{2,1,0:T(8,128)(2,1)S(1)}, u32[]{:S(2)}, u32[]{:S(2)}) collective-permute-start(bf16[3,1024,512]{2,1,0:T(8,128)(2,1)} %get-tuple-element.68.refs_0_.refs_5_), channel_id=1, source_target_pairs={{0,1},{1,0},{2,3},{3,2},{4,5},{5,4},{6,7},{7,6},{8,9},{9,8},{10,11... | collective-permute-start | bytes 9437192 | tf_op jit(solution)/shard_map/ppermute | solution.py:431
  137.8 34.8 %collective-permute-start.7 = (bf16[3,512,512]{2,1,0:T(8,128)(2,1)}, bf16[3,512,512]{2,1,0:T(8,128)(2,1)}, u32[]{:S(2)}, u32[]{:S(2)}) collective-permute-start(bf16[3,512,512]{2,1,0:T(8,128)(2,1)} %slice.269), channel_id=1, source_target_pairs={{0,1},{1,0},{2,3},{3,2},{4,5},{5,4},{6,7},{7,6},{8,9},{9,8},{10,11... | collective-permute-start | bytes 4718600 | tf_op jit(solution)/shard_map/ppermute | solution.py:431
  139.5 34.6 %collective-permute-start.6 = (bf16[3,512,512]{2,1,0:T(8,128)(2,1)}, bf16[3,512,512]{2,1,0:T(8,128)(2,1)}, u32[]{:S(2)}, u32[]{:S(2)}) collective-permute-start(bf16[3,512,512]{2,1,0:T(8,128)(2,1)} %slice.268), channel_id=1, source_target_pairs={{0,2},{1,3},{2,0},{3,1},{4,6},{5,7},{6,4},{7,5},{8,10},{9,11},{10,... | collective-permute-start | bytes 4718600 | tf_op jit(solution)/shard_map/ppermute | solution.py:431
  174.1 22.3 %collective-permute-start.9 = (bf16[1024,512]{1,0:T(8,128)(2,1)}, bf16[1024,512]{1,0:T(8,128)(2,1)S(1)}, u32[]{:S(2)}, u32[]{:S(2)}) collective-permute-start(bf16[1024,512]{1,0:T(8,128)(2,1)} %get-tuple-element.73.refs_0_), channel_id=1, source_target_pairs={{0,2},{1,3},{2,0},{3,1},{4,6},{5,7},{6,4},{7,5},{8,10},{9,11},{10,... | collective-permute-start | bytes 3145736 | tf_op jit(solution)/shard_map/ppermute | solution.py:431
  174.4 22.8 %collective-permute-start.8 = (bf16[1024,512]{1,0:T(8,128)(2,1)}, bf16[1024,512]{1,0:T(8,128)(2,1)S(1)}, u32[]{:S(2)}, u32[]{:S(2)}) collective-permute-start(bf16[1024,512]{1,0:T(8,128)(2,1)} %get-tuple-element.73.refs_0_), channel_id=1, source_target_pairs={{0,1},{1,0},{2,3},{3,2},{4,5},{5,4},{6,7},{7,6},{8,9},{9,8},{10,11... | collective-permute-start | bytes 3145736 | tf_op jit(solution)/shard_map/ppermute | solution.py:431
  197.3 19.5 %collective-permute-start.11 = (bf16[512,512]{1,0:T(8,128)(2,1)S(1)}, bf16[512,512]{1,0:T(8,128)(2,1)S(1)}, u32[]{:S(2)}, u32[]{:S(2)}) collective-permute-start(bf16[512,512]{1,0:T(8,128)(2,1)S(1)} %slice.271), channel_id=1, source_target_pairs={{0,1},{1,0},{2,3},{3,2},{4,5},{5,4},{6,7},{7,6},{8,9},{9,8},{10,11... | collective-permute-start | bytes 1572872 | tf_op jit(solution)/shard_map/ppermute | solution.py:431
  199.1 17.7 %collective-permute-start.10 = (bf16[512,512]{1,0:T(8,128)(2,1)S(1)}, bf16[512,512]{1,0:T(8,128)(2,1)S(1)}, u32[]{:S(2)}, u32[]{:S(2)}) collective-permute-start(bf16[512,512]{1,0:T(8,128)(2,1)S(1)} %slice.270), channel_id=1, source_target_pairs={{0,2},{1,3},{2,0},{3,1},{4,6},{5,7},{6,4},{7,5},{8,10},{9,11},{10,... | collective-permute-start | bytes 1572872 | tf_op jit(solution)/shard_map/ppermute | solution.py:431
  204.8 34.8 %collective-permute-start.13 = (bf16[512,512]{1,0:T(8,128)(2,1)S(1)}, bf16[512,512]{1,0:T(8,128)(2,1)}, u32[]{:S(2)}, u32[]{:S(2)}) collective-permute-start(bf16[512,512]{1,0:T(8,128)(2,1)S(1)} %slice.339), channel_id=1, source_target_pairs={{0,1},{1,0},{2,3},{3,2},{4,5},{5,4},{6,7},{7,6},{8,9},{9,8},{10,11... | collective-permute-start | bytes 1572872 | tf_op jit(solution)/shard_map/ppermute | solution.py:431
  205.2 34.3 %collective-permute-start.12 = (bf16[512,512]{1,0:T(8,128)(2,1)S(1)}, bf16[512,512]{1,0:T(8,128)(2,1)}, u32[]{:S(2)}, u32[]{:S(2)}) collective-permute-start(bf16[512,512]{1,0:T(8,128)(2,1)S(1)} %slice.338), channel_id=1, source_target_pairs={{0,2},{1,3},{2,0},{3,1},{4,6},{5,7},{6,4},{7,5},{8,10},{9,11},{10,... | collective-permute-start | bytes 1572872 | tf_op jit(solution)/shard_map/ppermute | solution.py:431
  266.3 25.4 %collective-permute-start.14 = (bf16[2,512,512]{2,1,0:T(8,128)(2,1)S(1)}, bf16[2,512,512]{2,1,0:T(8,128)(2,1)S(1)}, u32[]{:S(2)}, u32[]{:S(2)}) collective-permute-start(bf16[2,512,512]{2,1,0:T(8,128)(2,1)S(1)} %pad_maximum_fusion.5), channel_id=1, source_target_pairs={{0,1},{1,0},{2,3},{3,2},{4,5},{5,4},{6,7},{7,6},{8,9},{9,8},{10,11... | collective-permute-start | bytes 3145736 | tf_op jit(solution)/shard_map/ppermute | solution.py:431
  267.8 25.0 %collective-permute-start.15 = (bf16[2,512,512]{2,1,0:T(8,128)(2,1)S(1)}, bf16[2,512,512]{2,1,0:T(8,128)(2,1)S(1)}, u32[]{:S(2)}, u32[]{:S(2)}) collective-permute-start(bf16[2,512,512]{2,1,0:T(8,128)(2,1)S(1)} %stack.68), channel_id=1, source_target_pairs={{0,2},{1,3},{2,0},{3,1},{4,6},{5,7},{6,4},{7,5},{8,10},{9,11},{10,... | collective-permute-start | bytes 3145736 | tf_op jit(solution)/shard_map/ppermute | solution.py:431
  293.2 13.0 %collective-permute-start.17 = (bf16[1,512,512]{2,1,0:T(8,128)(2,1)S(1)}, bf16[1,512,512]{2,1,0:T(8,128)(2,1)S(1)}, u32[]{:S(2)}, u32[]{:S(2)}) collective-permute-start(bf16[1,512,512]{2,1,0:T(8,128)(2,1)S(1)} %get-tuple-element.138), channel_id=1, source_target_pairs={{0,1},{1,0},{2,3},{3,2},{4,5},{5,4},{6,7},{7,6},{8,9},{9,8},{10,11... | collective-permute-start | bytes 1572872 | tf_op jit(solution)/shard_map/ppermute | solution.py:431
  293.8 12.7 %collective-permute-start.16 = (bf16[1,512,512]{2,1,0:T(8,128)(2,1)S(1)}, bf16[1,512,512]{2,1,0:T(8,128)(2,1)S(1)}, u32[]{:S(2)}, u32[]{:S(2)}) collective-permute-start(bf16[1,512,512]{2,1,0:T(8,128)(2,1)S(1)} %get-tuple-element.139), channel_id=1, source_target_pairs={{0,2},{1,3},{2,0},{3,1},{4,6},{5,7},{6,4},{7,5},{8,10},{9,11},{10,... | collective-permute-start | bytes 1572872 | tf_op jit(solution)/shard_map/ppermute | solution.py:431
  308.9 23.1 %collective-permute-start.19 = (bf16[1024,512]{1,0:T(8,128)(2,1)S(1)}, bf16[1024,512]{1,0:T(8,128)(2,1)S(1)}, u32[]{:S(2)}, u32[]{:S(2)}) collective-permute-start(bf16[1024,512]{1,0:T(8,128)(2,1)S(1)} %fusion.refs_0_), channel_id=1, source_target_pairs={{0,2},{1,3},{2,0},{3,1},{4,6},{5,7},{6,4},{7,5},{8,10},{9,11},{10,... | collective-permute-start | bytes 3145736 | tf_op jit(solution)/shard_map/ppermute | solution.py:431
  310.6 23.7 %collective-permute-start.18 = (bf16[1024,512]{1,0:T(8,128)(2,1)S(1)}, bf16[1024,512]{1,0:T(8,128)(2,1)S(1)}, u32[]{:S(2)}, u32[]{:S(2)}) collective-permute-start(bf16[1024,512]{1,0:T(8,128)(2,1)S(1)} %fusion.refs_0_), channel_id=1, source_target_pairs={{0,1},{1,0},{2,3},{3,2},{4,5},{5,4},{6,7},{7,6},{8,9},{9,8},{10,11... | collective-permute-start | bytes 3145736 | tf_op jit(solution)/shard_map/ppermute | solution.py:431
  332.9 11.8 %collective-permute-start.21 = (bf16[512,512]{1,0:T(8,128)(2,1)}, bf16[512,512]{1,0:T(8,128)(2,1)}, u32[]{:S(2)}, u32[]{:S(2)}) collective-permute-start(bf16[512,512]{1,0:T(8,128)(2,1)} %slice.347), channel_id=1, source_target_pairs={{0,1},{1,0},{2,3},{3,2},{4,5},{5,4},{6,7},{7,6},{8,9},{9,8},{10,11... | collective-permute-start | bytes 1572872 | tf_op jit(solution)/shard_map/ppermute | solution.py:431
  335.2 10.9 %collective-permute-start.20 = (bf16[512,512]{1,0:T(8,128)(2,1)}, bf16[512,512]{1,0:T(8,128)(2,1)}, u32[]{:S(2)}, u32[]{:S(2)}) collective-permute-start(bf16[512,512]{1,0:T(8,128)(2,1)} %slice.346), channel_id=1, source_target_pairs={{0,2},{1,3},{2,0},{3,1},{4,6},{5,7},{6,4},{7,5},{8,10},{9,11},{10,... | collective-permute-start | bytes 1572872 | tf_op jit(solution)/shard_map/ppermute | solution.py:431
  376.1 278.4 %reduce-scatter.3.cloned.1.call-start = ((), (), s32[]{:S(2)}) async-start(), calls=%async_computation.4 | async-start | bytes 16515072 | tf_op jit(solution)/shard_map/reduce_scatter | solution.py:926
  410.7 37.2 %collective-permute-start.22 = (bf16[2,1,512,512]{3,2,1,0:T(8,128)(2,1)S(1)}, bf16[2,1,512,512]{3,2,1,0:T(8,128)(2,1)S(1)}, u32[]{:S(2)}, u32[]{:S(2)}) collective-permute-start(bf16[2,1,512,512]{3,2,1,0:T(8,128)(2,1)S(1)} %pad_maximum_fusion.6), channel_id=1, source_target_pairs={{0,1},{1,0},{2,3},{3,2},{4,5},{5,4},{6,7},{7,6},{8,9},{9,8},{10,11... | collective-permute-start | bytes 3145736 | tf_op jit(solution)/shard_map/ppermute | solution.py:431
  411.5 36.3 %collective-permute-start.24 = (bf16[2,1,512,512]{3,2,1,0:T(8,128)(2,1)S(1)}, bf16[2,1,512,512]{3,2,1,0:T(8,128)(2,1)S(1)}, u32[]{:S(2)}, u32[]{:S(2)}) collective-permute-start(bf16[2,1,512,512]{3,2,1,0:T(8,128)(2,1)S(1)} %stack.69), channel_id=1, source_target_pairs={{0,2},{1,3},{2,0},{3,1},{4,6},{5,7},{6,4},{7,5},{8,10},{9,11},{10,... | collective-permute-start | bytes 3145736 | tf_op jit(solution)/shard_map/ppermute | solution.py:431
  431.0 75.6 %collective-permute-start.26 = (bf16[2,2,512,512]{3,2,1,0:T(8,128)(2,1)}, bf16[2,2,512,512]{3,2,1,0:T(8,128)(2,1)S(1)}, u32[]{:S(2)}, u32[]{:S(2)}) collective-permute-start(bf16[2,2,512,512]{3,2,1,0:T(8,128)(2,1)} %pad_maximum_fusion), channel_id=1, source_target_pairs={{0,1},{1,0},{2,3},{3,2},{4,5},{5,4},{6,7},{7,6},{8,9},{9,8},{10,11... | collective-permute-start | bytes 6291464 | tf_op jit(solution)/shard_map/ppermute | solution.py:431
  432.1 74.5 %collective-permute-start.27 = (bf16[2,2,512,512]{3,2,1,0:T(8,128)(2,1)}, bf16[2,2,512,512]{3,2,1,0:T(8,128)(2,1)}, u32[]{:S(2)}, u32[]{:S(2)}) collective-permute-start(bf16[2,2,512,512]{3,2,1,0:T(8,128)(2,1)} %stack.70), channel_id=1, source_target_pairs={{0,2},{1,3},{2,0},{3,1},{4,6},{5,7},{6,4},{7,5},{8,10},{9,11},{10,... | collective-permute-start | bytes 6291464 | tf_op jit(solution)/shard_map/ppermute | solution.py:431
  464.3 4.5 collective-permute-start.34
  464.3 42.3 %collective-permute-start.41 = (f32[48,1024]{1,0:T(8,128)S(1)}, f32[48,1024]{1,0:T(8,128)S(1)}, u32[]{:S(2)}, u32[]{:S(2)}) collective-permute-start(f32[48,1024]{1,0:T(8,128)S(1)} %copy-done.22), channel_id=1, source_target_pairs={{0,1},{1,0},{2,3},{3,2},{4,5},{5,4},{6,7},{7,6},{8,9},{9,8},{10,11... | collective-permute-start | bytes 589832 | tf_op jit(solution)/shard_map/ppermute | solution.py:431
  467.6 39.0 %collective-permute-start.28 = (bf16[2,512,512]{2,1,0:T(8,128)(2,1)}, bf16[2,512,512]{2,1,0:T(8,128)(2,1)}, u32[]{:S(2)}, u32[]{:S(2)}) collective-permute-start(bf16[2,512,512]{2,1,0:T(8,128)(2,1)} %pad_maximum_fusion.7), channel_id=1, source_target_pairs={{0,1},{1,0},{2,3},{3,2},{4,5},{5,4},{6,7},{7,6},{8,9},{9,8},{10,11... | collective-permute-start | bytes 3145736 | tf_op jit(solution)/shard_map/ppermute | solution.py:431
  469.4 37.2 %collective-permute-start.29 = (bf16[2,512,512]{2,1,0:T(8,128)(2,1)}, bf16[2,512,512]{2,1,0:T(8,128)(2,1)}, u32[]{:S(2)}, u32[]{:S(2)}) collective-permute-start(bf16[2,512,512]{2,1,0:T(8,128)(2,1)} %stack.71), channel_id=1, source_target_pairs={{0,2},{1,3},{2,0},{3,1},{4,6},{5,7},{6,4},{7,5},{8,10},{9,11},{10,... | collective-permute-start | bytes 3145736 | tf_op jit(solution)/shard_map/ppermute | solution.py:431
  508.4 14.9 %collective-permute-start.25 = (bf16[1,1,512,512]{3,2,1,0:T(8,128)(2,1)S(1)}, bf16[1,1,512,512]{3,2,1,0:T(8,128)(2,1)S(1)}, u32[]{:S(2)}, u32[]{:S(2)}) collective-permute-start(bf16[1,1,512,512]{3,2,1,0:T(8,128)(2,1)S(1)} %get-tuple-element.132), channel_id=1, source_target_pairs={{0,1},{1,0},{2,3},{3,2},{4,5},{5,4},{6,7},{7,6},{8,9},{9,8},{10,11... | collective-permute-start | bytes 1572872 | tf_op jit(solution)/shard_map/ppermute | solution.py:431
  513.4 46.9 %collective-permute-start.31 = (bf16[1,2,512,512]{3,2,1,0:T(8,128)(2,1)S(1)}, bf16[1,2,512,512]{3,2,1,0:T(8,128)(2,1)S(1)}, u32[]{:S(2)}, u32[]{:S(2)}) collective-permute-start(bf16[1,2,512,512]{3,2,1,0:T(8,128)(2,1)S(1)} %get-tuple-element.120), channel_id=1, source_target_pairs={{0,1},{1,0},{2,3},{3,2},{4,5},{5,4},{6,7},{7,6},{8,9},{9,8},{10,11... | collective-permute-start | bytes 3145736 | tf_op jit(solution)/shard_map/ppermute | solution.py:431
  514.0 46.3 %collective-permute-start.30 = (bf16[1,2,512,512]{3,2,1,0:T(8,128)(2,1)S(1)}, bf16[1,2,512,512]{3,2,1,0:T(8,128)(2,1)S(1)}, u32[]{:S(2)}, u32[]{:S(2)}) collective-permute-start(bf16[1,2,512,512]{3,2,1,0:T(8,128)(2,1)S(1)} %get-tuple-element.121), channel_id=1, source_target_pairs={{0,2},{1,3},{2,0},{3,1},{4,6},{5,7},{6,4},{7,5},{8,10},{9,11},{10,... | collective-permute-start | bytes 3145736 | tf_op jit(solution)/shard_map/ppermute | solution.py:431
  514.0 37.3 %collective-permute-start.23 = (bf16[1,1,512,512]{3,2,1,0:T(8,128)(2,1)S(1)}, bf16[1,1,512,512]{3,2,1,0:T(8,128)(2,1)S(1)}, u32[]{:S(2)}, u32[]{:S(2)}) collective-permute-start(bf16[1,1,512,512]{3,2,1,0:T(8,128)(2,1)S(1)} %get-tuple-element.133), channel_id=1, source_target_pairs={{0,2},{1,3},{2,0},{3,1},{4,6},{5,7},{6,4},{7,5},{8,10},{9,11},{10,... | collective-permute-start | bytes 1572872 | tf_op jit(solution)/shard_map/ppermute | solution.py:431
  516.0 4.5 collective-permute-start.35
  520.5 35.0 %collective-permute-start.33 = (bf16[1,512,512]{2,1,0:T(8,128)(2,1)S(1)}, bf16[1,512,512]{2,1,0:T(8,128)(2,1)S(1)}, u32[]{:S(2)}, u32[]{:S(2)}) collective-permute-start(bf16[1,512,512]{2,1,0:T(8,128)(2,1)S(1)} %get-tuple-element.128), channel_id=1, source_target_pairs={{0,1},{1,0},{2,3},{3,2},{4,5},{5,4},{6,7},{7,6},{8,9},{9,8},{10,11... | collective-permute-start | bytes 1572872 | tf_op jit(solution)/shard_map/ppermute | solution.py:431
  523.3 37.0 %collective-permute-start.32 = (bf16[1,512,512]{2,1,0:T(8,128)(2,1)S(1)}, bf16[1,512,512]{2,1,0:T(8,128)(2,1)S(1)}, u32[]{:S(2)}, u32[]{:S(2)}) collective-permute-start(bf16[1,512,512]{2,1,0:T(8,128)(2,1)S(1)} %get-tuple-element.129), channel_id=1, source_target_pairs={{0,2},{1,3},{2,0},{3,1},{4,6},{5,7},{6,4},{7,5},{8,10},{9,11},{10,... | collective-permute-start | bytes 1572872 | tf_op jit(solution)/shard_map/ppermute | solution.py:431
  588.8 9.1 %collective-permute-start.36 = (f32[48,1024]{1,0:T(8,128)}, f32[48,1024]{1,0:T(8,128)S(1)}, u32[]{:S(2)}, u32[]{:S(2)}) collective-permute-start(f32[48,1024]{1,0:T(8,128)} %get-tuple-element.106), channel_id=1, source_target_pairs={{0,1},{1,0},{2,3},{3,2},{4,5},{5,4},{6,7},{7,6},{8,9},{9,8},{10,11... | collective-permute-start | bytes 589832 | tf_op jit(solution)/shard_map/ppermute | solution.py:431
  590.6 6.6 collective-permute-start.37
  590.6 5.6 collective-permute-start.38
  596.8 7.8 %collective-permute-start.42 = (f32[48,1024]{1,0:T(8,128)S(1)}, f32[48,1024]{1,0:T(8,128)S(1)}, u32[]{:S(2)}, u32[]{:S(2)}) collective-permute-start(f32[48,1024]{1,0:T(8,128)S(1)} %add.281), channel_id=1, source_target_pairs={{0,2},{1,3},{2,0},{3,1},{4,6},{5,7},{6,4},{7,5},{8,10},{9,11},{10,... | collective-permute-start | bytes 589832 | tf_op jit(solution)/shard_map/ppermute | solution.py:431
  598.8 9.0 %collective-permute-start.39 = (f32[48,1024]{1,0:T(8,128)S(1)}, f32[48,1024]{1,0:T(8,128)S(1)}, u32[]{:S(2)}, u32[]{:S(2)}) collective-permute-start(f32[48,1024]{1,0:T(8,128)S(1)} %add.274), channel_id=1, source_target_pairs={{0,2},{1,3},{2,0},{3,1},{4,6},{5,7},{6,4},{7,5},{8,10},{9,11},{10,... | collective-permute-start | bytes 589832 | tf_op jit(solution)/shard_map/ppermute | solution.py:431
  600.7 4.4 collective-permute-start.40
  607.9 5.4 collective-permute-start.43
  613.3 4.3 collective-permute-start.44
  617.6 21.2 %collective-permute-start.45 = (f32[8,2048]{1,0:T(8,128)S(1)}, f32[8,2048]{1,0:T(8,128)S(1)}, u32[]{:S(2)}, u32[]{:S(2)}) collective-permute-start(f32[8,2048]{1,0:T(8,128)S(1)} %add_dynamic-update-slice_fusion), channel_id=1, source_target_pairs={{0,2},{1,3},{2,0},{3,1},{4,6},{5,7},{6,4},{7,5},{8,10},{9,11},{10,... | collective-permute-start | bytes 196616 | tf_op jit(solution)/shard_map/ppermute | solution.py:431
  (38 other events, 423.2 us)
Sparse Core Ops, SparseCore 0:
  10.2 137.1 all-gather.2
  149.0 97.9 all-gather.4
  376.2 108.8 reduce-scatter.4
  506.8 147.6 reduce-scatter.2

commit v5 on v4

--- a/solution.py
+++ b/solution.py
@@ -361,20 +361,27 @@
     last, refs = group_parts(refs, shape)
     first, refs = group_parts(refs, shape)
     hidden_grad, lin_grad, out, turned = refs
-    j, r = pl.program_id(0), pl.program_id(1)
-    for k in range(len(shape)):
-
-        @pl.when((j == 0) & (r == k))
-        def _():
+    j = pl.program_id(0)
+    width = turned.shape[1]
+
+    def store(k, total):
+        offset = pl.multiple_of((place[0] ^ k) * width, width)
+        out[pl.ds(offset, width), :] = total.astype(BF16)
+
+    @pl.when(j == 0)
+    def _():
+        for k in range(len(shape)):
             turned[k] = joined(last[k]).T
-
-        @pl.when((j >= hidden_steps) & (r == k))
-        def _():
-            out[...] = mul(joined(first[k]), lin_grad[...], TN).astype(BF16)
 
     @pl.when(j < hidden_steps)
     def _():
-        out[...] = mul(turned[r], hidden_grad[...]).astype(BF16)
+        for k in range(len(shape)):
+            store(k, mul(turned[k], hidden_grad[...]))
+
+    @pl.when(j >= hidden_steps)
+    def _():
+        for k in range(len(shape)):
+            store(k, mul(joined(first[k]), lin_grad[...], TN))
 
 
 def sums_kernel(
@@ -875,10 +882,10 @@
         functools.partial(
             weight_grad_kernel, [len(parts) for parts in last_pieces], hidden_steps
         ),
-        (all_steps, count),
+        (all_steps,),
         ins=[(part, part.shape, const(0, 0)) for parts in last_pieces for part in parts]
         + [
-            (part, (None, *part.shape[1:]), lambda j, r, p: (lin_step(j), 0, 0))
+            (part, (None, *part.shape[1:]), lambda j, p: (lin_step(j), 0, 0))
             for parts in first_pieces
             for part in parts
         ]
@@ -886,16 +893,16 @@
             (
                 hidden_grad,
                 (tokens, heads_width),
-                lambda j, r, p: (0, jnp.minimum(j, hidden_steps - 1)),
+                lambda j, p: (0, jnp.minimum(j, hidden_steps - 1)),
             ),
-            (lin_grads, (None, tokens, heads_width), lambda j, r, p: (lin_step(j), 0, 0)),
+            (lin_grads, (None, tokens, heads_width), lambda j, p: (lin_step(j), 0, 0)),
         ],
         outs=[
             (
                 (width_all, all_steps * heads_width),
                 BF16,
-                (width, heads_width),
-                lambda j, r, p: (p[0] ^ r, j),
+                (width_all, heads_width),
+                lambda j, p: (0, j),
             )
         ],
         name="weight_grad",

time: 679 us -> 676 us (level)
  Pallas kernels: 277 us -> 267 us
    pallas_call x17, Pallas kernels: 260 us -> 250 us  [kernel_call(): return call(place, *[a for a, _, _ in ins])]
  transfers between devices with their start and end apart: 50 -> 50, of which waited for: 27 -> 28; matrix products, arithmetic and copies ran while one was open for 9% -> 9% of each run, Pallas kernels for 35% -> 33%
where the time goes in v5:
time: 676 us; the launch traced here: 665 us
  Pallas kernels  267 us (39%)
  waiting for transfers between devices  243 us (36%)
  starting transfers between devices  45.2 us (7%)
  other arithmetic  40.9 us (6%)
  local copies, waits for them, and re-layouts  38.1 us (6%)
  between operations  15.5 us (2%)
  blocking collectives  14.8 us (2%)
    pallas_call x17, Pallas kernels, kernel_call(): return call(place, *[a for a, _, _ in ins])  250 us
    ppermute x46, waiting for transfers between devices, swap(): return lax.ppermute(values, axis, [(i, i ^ bit) for i in range(count)])  223 us
    ppermute x46, starting transfers between devices, swap(): return lax.ppermute(values, axis, [(i, i ^ bit) for i in range(count)])  45 us
    pallas_call x1, Pallas kernels, per_device(): pl.pallas_call(attend_back_kernel, out_shape=jax.ShapeDtypeStruct((3, tok...  17.5 us
    all_gather x1, blocking collectives, per_device(): smalls = lax.all_gather(smalls, 'dp', axis=0, tiled=True)  14.8 us
  transfers between devices with their start and end apart: 50, of which 28 were waited for; matrix products, arithmetic and copies ran while one was open for 9% of the time, Pallas kernels for 33%

profile of v5, /device:TPU:0, one launch (start us, length us, event | category | flops | bytes accessed | tf_op | source)
XLA Modules:
  0.0 664.6 jit_solution(6735998148946422417)
XLA Ops:
  11.8 3.0 collective-permute-start.1
  16.3 14.8 %all_gather.9 = bf16[2048,48]{0,1:T(8,128)(2,1)S(1)} all-gather(bf16[256,48]{0,1:T(8,128)(2,1)S(1)} %pad_maximum_fusion.8), channel_id=1, replica_groups=mesh['dp'=8,'tensor'=4] {'dp'}, dimensions={0}, use_global_device_ids=true | all-gather | bytes 221184 | tf_op jit(solution)/shard_map/all_gather | solution.py:579
  33.7 14.3 %mix.1 = (f32[4,1024,512]{2,1,0:T(8,128)}, f32[8,1024]{1,0:T(8,128)}) custom-call(s32[2]{0:T(128)} %pad_add_fusion.place, bf16[9,1024,512]{2,1,0:T(8,128)(2,1)} %hist.5, f32[1024,36]{1,0:T(8,128)} %bitcast.43), custom_call_target="tpu_custom_call" | custom-call | flops 37748736 | bytes 18006016 | tf_op jit(solution)/shard_map/mix/pallas_call | solution.py:58
  48.6 3.7 collective-permute-done.2
  54.1 2.9 collective-permute-done.3
  57.6 9.6 %norm.1 = (bf16[3,1024,512]{2,1,0:T(8,128)(2,1)}, bf16[1024,512]{1,0:T(8,128)(2,1)}) custom-call(s32[2]{0:T(128)} %pad_add_fusion.place, f32[4,1024,512]{2,1,0:T(8,128)} %get-tuple-element.69.streams, f32[8,1024]{1,0:T(8,128)} %add.235.stats, f32[4,512]{1,0:T(4,128)} %get-tuple-element.153.gain, f32[4,512]{1,0:T(4,128)} %get-tuple-element.152.bias), custom_call_target="tpu_custom_call" | custom-call | bytes 12632064 | tf_op jit(solution)/shard_map/norm/pallas_call | solution.py:58
  68.0 14.8 %spread.1 = f32[48,1024]{1,0:T(8,128)} custom-call(s32[2]{0:T(128)} %pad_add_fusion.place, f32[4,1024,512]{2,1,0:T(8,128)} %get-tuple-element.69.streams, f32[8,1024]{1,0:T(8,128)} %add.235.stats, bf16[9,1024,512]{2,1,0:T(8,128)(2,1)} %hist.5), custom_call_target="tpu_custom_call" | custom-call | bytes 18055168 | tf_op jit(solution)/shard_map/spread/pallas_call | solution.py:58
  82.8 53.7 %collective-permute-done.5.refs_2_.refs_7_ = bf16[3,1024,512]{2,1,0:T(8,128)(2,1)S(1)} collective-permute-done((bf16[3,1024,512]{2,1,0:T(8,128)(2,1)}, bf16[3,1024,512]{2,1,0:T(8,128)(2,1)S(1)}, u32[]{:S(2)}, u32[]{:S(2)}) %collective-permute-start.5) | collective-permute-done | bytes 3145760 | tf_op jit(solution)/shard_map/ppermute | solution.py:438
  143.4 29.3 %collective-permute-done.7.refs_4_.refs_9_ = bf16[3,512,512]{2,1,0:T(8,128)(2,1)} collective-permute-done((bf16[3,512,512]{2,1,0:T(8,128)(2,1)}, bf16[3,512,512]{2,1,0:T(8,128)(2,1)}, u32[]{:S(2)}, u32[]{:S(2)}) %collective-permute-start.7) | collective-permute-done | bytes 1572896 | tf_op jit(solution)/shard_map/ppermute | solution.py:438
  178.4 15.4 %qkv.1.q.k.v = bf16[3,1024,512]{2,1,0:T(8,128)(2,1)} custom-call(s32[2]{0:T(128)} %pad_add_fusion.place, bf16[3,1024,512]{2,1,0:T(8,128)(2,1)} %get-tuple-element.68.refs_0_.refs_5_, bf16[3,1024,512]{2,1,0:T(8,128)(2,1)} %copy-done.3, bf16[3,1024,512]{2,1,0:T(8,128)(2,1)} %copy-done.2, bf16[3,512,512]{2,1,0:T(8,128)(2,1)} %collective-permute-done.6.refs_3_.refs_8_, ...), custom_call_target="tpu_custom_call" | custom-call | flops 6442450944 | bytes 76021760 | tf_op jit(solution)/shard_map/qkv/pallas_call | solution.py:58
  193.9 2.5 collective-permute-done.9.refs_2_
  199.1 2.1 collective-permute-start.10
  205.3 11.5 %attend.1.attended = bf16[1024,512]{1,0:T(8,128)(2,1)} custom-call(s32[2]{0:T(128)} %pad_add_fusion.place, bf16[3,1024,512]{2,1,0:T(8,128)(2,1)} %qkv.1.q.k.v, bf16[3,1024,512]{2,1,0:T(8,128)(2,1)} %qkv.1.q.k.v, bf16[3,1024,512]{2,1,0:T(8,128)(2,1)} %qkv.1.q.k.v), custom_call_target="tpu_custom_call" | custom-call | flops 2147483648 | bytes 10485760 | tf_op jit(solution)/shard_map/attend/pallas_call | solution.py:58
  218.4 21.4 %up.1 = (bf16[1024,2048]{1,0:T(8,128)(2,1)}, bf16[1024,2048]{1,0:T(8,128)(2,1)}) custom-call(s32[2]{0:T(128)} %pad_add_fusion.place, bf16[1024,512]{1,0:T(8,128)(2,1)} %get-tuple-element.73.refs_0_, bf16[1024,512]{1,0:T(8,128)(2,1)} %copy-done.8, bf16[1024,512]{1,0:T(8,128)(2,1)} %copy-done.7, bf16[512,512]{1,0:T(8,128)(2,1)} %copy-done.24, ...), custom_call_target="tpu_custom_call" | custom-call | flops 8589934592 | bytes 71303168 | tf_op jit(solution)/shard_map/up/pallas_call | solution.py:58
  239.8 7.2 %all-gather.5.cloned.1.call-done.down.out.weight = bf16[2560,2048]{1,0:T(8,128)(2,1)} async-done(((bf16[2560,256]{1,0:T(8,128)(2,1)}), bf16[2560,2048]{1,0:T(8,128)(2,1)}) %all-gather.5.cloned.1.call-update) | async-done | bytes 10485776 | tf_op jit(solution)/shard_map/all_gather | solution.py:588
  247.0 16.5 %down.1 = bf16[4,1024,512]{2,1,0:T(8,128)(2,1)} custom-call(s32[2]{0:T(128)} %pad_add_fusion.place, bf16[1024,2048]{1,0:T(8,128)(2,1)} %get-tuple-element.80.hidden, bf16[1024,512]{1,0:T(8,128)(2,1)} %attend.1.attended, bf16[2560,2048]{1,0:T(8,128)(2,1)} %all-gather.5.cloned.1.call-done.down.out.weight, ...), custom_call_target="tpu_custom_call" | custom-call | flops 10737418240 | bytes 30408704 | tf_op jit(solution)/shard_map/down/pallas_call | solution.py:58
  269.4 22.3 %collective-permute-done.14 = bf16[2,512,512]{2,1,0:T(8,128)(2,1)S(1)} collective-permute-done((bf16[2,512,512]{2,1,0:T(8,128)(2,1)S(1)}, bf16[2,512,512]{2,1,0:T(8,128)(2,1)S(1)}, u32[]{:S(2)}, u32[]{:S(2)}) %collective-permute-start.14) | collective-permute-done | bytes 1048608 | tf_op jit(solution)/shard_map/ppermute | solution.py:438
  295.3 10.9 %collective-permute-done.17 = bf16[1,512,512]{2,1,0:T(8,128)(2,1)S(1)} collective-permute-done((bf16[1,512,512]{2,1,0:T(8,128)(2,1)S(1)}, bf16[1,512,512]{2,1,0:T(8,128)(2,1)S(1)}, u32[]{:S(2)}, u32[]{:S(2)}) %collective-permute-start.17) | collective-permute-done | bytes 524320 | tf_op jit(solution)/shard_map/ppermute | solution.py:438
  312.0 20.0 %collective-permute-done.19.refs_2_ = bf16[1024,512]{1,0:T(8,128)(2,1)S(1)} collective-permute-done((bf16[1024,512]{1,0:T(8,128)(2,1)S(1)}, bf16[1024,512]{1,0:T(8,128)(2,1)S(1)}, u32[]{:S(2)}, u32[]{:S(2)}) %collective-permute-start.19) | collective-permute-done | bytes 1048608 | tf_op jit(solution)/shard_map/ppermute | solution.py:438
  337.8 6.9 %collective-permute-done.21.refs_4_ = bf16[512,512]{1,0:T(8,128)(2,1)} collective-permute-done((bf16[512,512]{1,0:T(8,128)(2,1)}, bf16[512,512]{1,0:T(8,128)(2,1)}, u32[]{:S(2)}, u32[]{:S(2)}) %collective-permute-start.21) | collective-permute-done | bytes 524320 | tf_op jit(solution)/shard_map/ppermute | solution.py:438
  346.1 11.4 %middle.1 = (bf16[1024,2048]{1,0:T(8,128)(2,1)}, f32[1024,512]{1,0:T(8,128)}, f32[40,1024]{1,0:T(8,128)}, f32[40,40]{1,0:T(8,128)}, f32[40,2048]{1,0:T(8,128)}) custom-call(s32[2]{0:T(128)} %pad_add_fusion.place, bf16[1024,512]{1,0:T(8,128)(2,1)} %copy-done.6, bf16[1024,512]{1,0:T(8,128)(2,1)} %copy-done.14, bf16[1024,512]{1,0:T(8,128)(2,1)} %copy-done.13, ...), custom_call_target="tpu_custom_call" | custom-call | flops 503316480 | bytes 15922560 | tf_op jit(solution)/shard_map/middle/pallas_call | solution.py:58
  358.5 16.9 %down_grad.1 = bf16[2608,2048]{1,0:T(8,128)(2,1)} custom-call(s32[2]{0:T(128)} %pad_add_fusion.place, bf16[1024,2048]{1,0:T(8,128)(2,1)} %get-tuple-element.80.hidden, bf16[1024,512]{1,0:T(8,128)(2,1)} %attend.1.attended, bf16[1024,2048]{1,0:T(8,128)(2,1)} %get-tuple-element.90.branch_grad.grad), custom_call_target="tpu_custom_call" | custom-call | flops 10737418240 | bytes 20119552 | tf_op jit(solution)/shard_map/down_grad/pallas_call | solution.py:58
  376.1 7.2 %attended_grad.1.grad = bf16[1024,512]{1,0:T(8,128)(2,1)} custom-call(s32[2]{0:T(128)} %pad_add_fusion.place, bf16[1024,2048]{1,0:T(8,128)(2,1)} %get-tuple-element.90.branch_grad.grad, bf16[2560,2048]{1,0:T(8,128)(2,1)} %all-gather.5.cloned.1.call-done.down.out.weight), custom_call_target="tpu_custom_call" | custom-call | flops 2147483648 | bytes 15728640 | tf_op jit(solution)/shard_map/attended_grad/pallas_call | solution.py:58
  383.3 17.5 %attend_back.1.grad.refs_11_ = bf16[3,1024,512]{2,1,0:T(8,128)(2,1)} custom-call(s32[2]{0:T(128)} %pad_add_fusion.place, bf16[3,1024,512]{2,1,0:T(8,128)(2,1)} %qkv.1.q.k.v, bf16[3,1024,512]{2,1,0:T(8,128)(2,1)} %qkv.1.q.k.v, bf16[3,1024,512]{2,1,0:T(8,128)(2,1)} %qkv.1.q.k.v, bf16[1024,512]{1,0:T(8,128)(2,1)} %attended_grad.1.grad, ...), custom_call_target="tpu_custom_call" | custom-call | flops 5368709120 | bytes 8388608 | tf_op jit(solution)/shard_map/attend_back/pallas_call | solution.py:799
  400.9 6.8 %qkv_back.2 = bf16[4,1,1024,512]{3,2,1,0:T(8,128)(2,1)} custom-call(s32[2]{0:T(128)} %pad_add_fusion.place, bf16[3,1024,512]{2,1,0:T(8,128)(2,1)} %attend_back.1.grad.refs_11_, bf16[2048,3584]{1,0:T(8,128)(2,1)} %all-gather.3.cloned.1.call-done.refs_5_.refs_6_.refs_7_.refs_8_.weight), custom_call_target="tpu_custom_call" | custom-call | flops 2147483648 | bytes 22020096 | tf_op jit(solution)/shard_map/qkv_back/pallas_call | solution.py:58
  413.0 11.5 %qkv_back.3 = bf16[4,2,1024,512]{3,2,1,0:T(8,128)(2,1)} custom-call(s32[2]{0:T(128)} %pad_add_fusion.place, bf16[3,1024,512]{2,1,0:T(8,128)(2,1)} %attend_back.1.grad.refs_11_, bf16[2048,3584]{1,0:T(8,128)(2,1)} %all-gather.3.cloned.1.call-done.refs_5_.refs_6_.refs_7_.refs_8_.weight), custom_call_target="tpu_custom_call" | custom-call | flops 4294967296 | bytes 26214400 | tf_op jit(solution)/shard_map/qkv_back/pallas_call | solution.py:58
  426.1 3.1 stack.70
  432.5 15.1 %hidden_grad.1.grad.refs_10_ = bf16[1024,2048]{1,0:T(8,128)(2,1)} custom-call(s32[2]{0:T(128)} %pad_add_fusion.place, bf16[1024,2048]{1,0:T(8,128)(2,1)} %get-tuple-element.90.branch_grad.grad, bf16[2560,2048]{1,0:T(8,128)(2,1)} %all-gather.5.cloned.1.call-done.down.out.weight, bf16[1024,2048]{1,0:T(8,128)(2,1)} %get-tuple-element.91.slope), custom_call_target="tpu_custom_call" | custom-call | flops 8589934592 | bytes 23068672 | tf_op jit(solution)/shard_map/hidden_grad/pallas_call | solution.py:58
  447.7 14.1 %up_back.1 = bf16[4,1024,512]{2,1,0:T(8,128)(2,1)} custom-call(s32[2]{0:T(128)} %pad_add_fusion.place, bf16[1024,2048]{1,0:T(8,128)(2,1)} %hidden_grad.1.grad.refs_10_, bf16[2048,3584]{1,0:T(8,128)(2,1)} %all-gather.3.cloned.1.call-done.refs_5_.refs_6_.refs_7_.refs_8_.weight), custom_call_target="tpu_custom_call" | custom-call | flops 8589934592 | bytes 23068672 | tf_op jit(solution)/shard_map/up_back/pallas_call | solution.py:58
  461.8 2.3 stack.71
  470.6 25.8 %weight_grad.1 = bf16[2048,3584]{1,0:T(8,128)(2,1)} custom-call(s32[2]{0:T(128)} %pad_add_fusion.place, bf16[1024,512]{1,0:T(8,128)(2,1)} %get-tuple-element.73.refs_0_, bf16[1024,512]{1,0:T(8,128)(2,1)} %copy-done.8, bf16[1024,512]{1,0:T(8,128)(2,1)} %copy-done.7, bf16[512,512]{1,0:T(8,128)(2,1)} %copy-done.24, bf16[512,512]{1,0:T(8,128)(2,1)} %copy-done.23, ...), custom_call_target="tpu_custom_call" | custom-call | flops 15032385536 | bytes 38797312 | tf_op jit(solution)/shard_map/weight_grad/pallas_call | solution.py:58
  496.4 7.1 %collective-permute-done.28 = bf16[2,512,512]{2,1,0:T(8,128)(2,1)} collective-permute-done((bf16[2,512,512]{2,1,0:T(8,128)(2,1)}, bf16[2,512,512]{2,1,0:T(8,128)(2,1)}, u32[]{:S(2)}, u32[]{:S(2)}) %collective-permute-start.28) | collective-permute-done | bytes 1048608 | tf_op jit(solution)/shard_map/ppermute | solution.py:438
  506.3 3.5 add_convert_fusion
  513.8 2.9 collective-permute-done.35
  521.8 25.7 %collective-permute-done.23 = bf16[1,1,512,512]{3,2,1,0:T(8,128)(2,1)S(1)} collective-permute-done((bf16[1,1,512,512]{3,2,1,0:T(8,128)(2,1)S(1)}, bf16[1,1,512,512]{3,2,1,0:T(8,128)(2,1)S(1)}, u32[]{:S(2)}, u32[]{:S(2)}) %collective-permute-start.23) | collective-permute-done | bytes 524320 | tf_op jit(solution)/shard_map/ppermute | solution.py:438
  547.5 2.6 collective-permute-done.33
  550.1 4.3 collective-permute-done.32
  559.2 2.7 add_bitcast_fusion.1
  561.9 3.1 maximum_maximum_fusion.first
  565.0 17.8 %sums.1 = (f32[48,1024]{1,0:T(8,128)}, f32[8,512]{1,0:T(8,128)}) custom-call(s32[2]{0:T(128)} %pad_add_fusion.place, f32[3,1024,512]{2,1,0:T(8,128)} %maximum_maximum_fusion.first, f32[1024,512]{1,0:T(8,128)} %pad_maximum_fusion.1.last, f32[4,1024,512]{2,1,0:T(8,128)} %get-tuple-element.69.streams, f32[8,1024]{1,0:T(8,128)} %add.235.stats, ...), custom_call_target="tpu_custom_call" | custom-call | bytes 28565504 | tf_op jit(solution)/shard_map/sums/pallas_call | solution.py:58
  583.8 5.6 collective-permute-done.38
  593.9 4.0 collective-permute-done.42
  598.3 2.7 collective-permute-done.39
  601.2 5.3 collective-permute-done.43
  607.8 3.0 collective-permute-done.44
  613.5 19.6 %history.1 = f32[9,1024,512]{2,1,0:T(8,128)} custom-call(s32[2]{0:T(128)} %pad_add_fusion.place, f32[3,1024,512]{2,1,0:T(8,128)} %maximum_maximum_fusion.first, f32[1024,512]{1,0:T(8,128)} %pad_maximum_fusion.1.last, f32[4,1024,512]{2,1,0:T(8,128)} %get-tuple-element.69.streams, f32[8,1024]{1,0:T(8,128)} %add.235.stats, f32[4,512]{1,0:T(4,128)} %get-tuple-element.153.gain, ...), custom_call_target="tpu_custom_call" | custom-call | bytes 37969920 | tf_op jit(solution)/shard_map/history/pallas_call | solution.py:58
  635.5 2.8 slice.379
  639.2 12.8 %reduce-scatter.3.cloned.1.call-done = bf16[256,3584]{1,0:T(8,128)(2,1)} async-done(((bf16[2048,3584]{1,0:T(8,128)(2,1)}), bf16[256,3584]{1,0:T(8,128)(2,1)}) %reduce-scatter.3.cloned.1.call-update) | async-done | bytes 1835024 | tf_op jit(solution)/shard_map/reduce_scatter | solution.py:933
  (236 shorter events, 108.9 us)
Async XLA Ops:
  7.2 171.2 %all-gather.3.cloned.1.call-start = ((), (), s32[]{:S(2)}) async-start(), calls=%async_computation.2 | async-start | bytes 16515072 | tf_op jit(solution)/shard_map/all_gather | solution.py:585
  10.1 236.9 %all-gather.5.cloned.1.call-start = ((), (), s32[]{:S(2)}) async-start(), calls=%async_computation.3 | async-start | bytes 11796480 | tf_op jit(solution)/shard_map/all_gather | solution.py:588
  11.7 622.0 %reduce-scatter.5.cloned.1.call-start = ((), (), s32[]{:S(2)}) async-start(), calls=%async_computation.5 | async-start | bytes 12017664 | tf_op jit(solution)/shard_map/reduce_scatter | solution.py:929
  11.8 36.3 %collective-permute-start.1 = (bf16[1024,512]{1,0:T(8,128)(2,1)S(1)}, bf16[1024,512]{1,0:T(8,128)(2,1)S(1)}, u32[]{:S(2)}, u32[]{:S(2)}) collective-permute-start(bf16[1024,512]{1,0:T(8,128)(2,1)S(1)} %copy-done.20), channel_id=1, source_target_pairs={{0,2},{1,3},{2,0},{3,1},{4,6},{5,7},{6,4},{7,5},{8,10},{9,11},{10,... | collective-permute-start | bytes 3145736 | tf_op jit(solution)/shard_map/ppermute | solution.py:438
  14.8 33.3 %collective-permute-start = (bf16[1024,512]{1,0:T(8,128)(2,1)S(1)}, bf16[1024,512]{1,0:T(8,128)(2,1)S(1)}, u32[]{:S(2)}, u32[]{:S(2)}) collective-permute-start(bf16[1024,512]{1,0:T(8,128)(2,1)S(1)} %copy-done.20), channel_id=1, source_target_pairs={{0,1},{1,0},{2,3},{3,2},{4,5},{5,4},{6,7},{7,6},{8,9},{9,8},{10,11... | collective-permute-start | bytes 3145736 | tf_op jit(solution)/shard_map/ppermute | solution.py:438
  67.2 69.3 %collective-permute-start.5 = (bf16[3,1024,512]{2,1,0:T(8,128)(2,1)}, bf16[3,1024,512]{2,1,0:T(8,128)(2,1)S(1)}, u32[]{:S(2)}, u32[]{:S(2)}) collective-permute-start(bf16[3,1024,512]{2,1,0:T(8,128)(2,1)} %get-tuple-element.68.refs_0_.refs_5_), channel_id=1, source_target_pairs={{0,2},{1,3},{2,0},{3,1},{4,6},{5,7},{6,4},{7,5},{8,10},{9,11},{10,... | collective-permute-start | bytes 9437192 | tf_op jit(solution)/shard_map/ppermute | solution.py:438
  67.8 70.4 %collective-permute-start.4 = (bf16[3,1024,512]{2,1,0:T(8,128)(2,1)}, bf16[3,1024,512]{2,1,0:T(8,128)(2,1)S(1)}, u32[]{:S(2)}, u32[]{:S(2)}) collective-permute-start(bf16[3,1024,512]{2,1,0:T(8,128)(2,1)} %get-tuple-element.68.refs_0_.refs_5_), channel_id=1, source_target_pairs={{0,1},{1,0},{2,3},{3,2},{4,5},{5,4},{6,7},{7,6},{8,9},{9,8},{10,11... | collective-permute-start | bytes 9437192 | tf_op jit(solution)/shard_map/ppermute | solution.py:438
  137.8 34.8 %collective-permute-start.7 = (bf16[3,512,512]{2,1,0:T(8,128)(2,1)}, bf16[3,512,512]{2,1,0:T(8,128)(2,1)}, u32[]{:S(2)}, u32[]{:S(2)}) collective-permute-start(bf16[3,512,512]{2,1,0:T(8,128)(2,1)} %slice.269), channel_id=1, source_target_pairs={{0,1},{1,0},{2,3},{3,2},{4,5},{5,4},{6,7},{7,6},{8,9},{9,8},{10,11... | collective-permute-start | bytes 4718600 | tf_op jit(solution)/shard_map/ppermute | solution.py:438
  139.5 34.6 %collective-permute-start.6 = (bf16[3,512,512]{2,1,0:T(8,128)(2,1)}, bf16[3,512,512]{2,1,0:T(8,128)(2,1)}, u32[]{:S(2)}, u32[]{:S(2)}) collective-permute-start(bf16[3,512,512]{2,1,0:T(8,128)(2,1)} %slice.268), channel_id=1, source_target_pairs={{0,2},{1,3},{2,0},{3,1},{4,6},{5,7},{6,4},{7,5},{8,10},{9,11},{10,... | collective-permute-start | bytes 4718600 | tf_op jit(solution)/shard_map/ppermute | solution.py:438
  174.1 22.3 %collective-permute-start.9 = (bf16[1024,512]{1,0:T(8,128)(2,1)}, bf16[1024,512]{1,0:T(8,128)(2,1)S(1)}, u32[]{:S(2)}, u32[]{:S(2)}) collective-permute-start(bf16[1024,512]{1,0:T(8,128)(2,1)} %get-tuple-element.73.refs_0_), channel_id=1, source_target_pairs={{0,2},{1,3},{2,0},{3,1},{4,6},{5,7},{6,4},{7,5},{8,10},{9,11},{10,... | collective-permute-start | bytes 3145736 | tf_op jit(solution)/shard_map/ppermute | solution.py:438
  174.4 22.8 %collective-permute-start.8 = (bf16[1024,512]{1,0:T(8,128)(2,1)}, bf16[1024,512]{1,0:T(8,128)(2,1)S(1)}, u32[]{:S(2)}, u32[]{:S(2)}) collective-permute-start(bf16[1024,512]{1,0:T(8,128)(2,1)} %get-tuple-element.73.refs_0_), channel_id=1, source_target_pairs={{0,1},{1,0},{2,3},{3,2},{4,5},{5,4},{6,7},{7,6},{8,9},{9,8},{10,11... | collective-permute-start | bytes 3145736 | tf_op jit(solution)/shard_map/ppermute | solution.py:438
  197.3 19.5 %collective-permute-start.11 = (bf16[512,512]{1,0:T(8,128)(2,1)S(1)}, bf16[512,512]{1,0:T(8,128)(2,1)S(1)}, u32[]{:S(2)}, u32[]{:S(2)}) collective-permute-start(bf16[512,512]{1,0:T(8,128)(2,1)S(1)} %slice.271), channel_id=1, source_target_pairs={{0,1},{1,0},{2,3},{3,2},{4,5},{5,4},{6,7},{7,6},{8,9},{9,8},{10,11... | collective-permute-start | bytes 1572872 | tf_op jit(solution)/shard_map/ppermute | solution.py:438
  199.1 17.7 %collective-permute-start.10 = (bf16[512,512]{1,0:T(8,128)(2,1)S(1)}, bf16[512,512]{1,0:T(8,128)(2,1)S(1)}, u32[]{:S(2)}, u32[]{:S(2)}) collective-permute-start(bf16[512,512]{1,0:T(8,128)(2,1)S(1)} %slice.270), channel_id=1, source_target_pairs={{0,2},{1,3},{2,0},{3,1},{4,6},{5,7},{6,4},{7,5},{8,10},{9,11},{10,... | collective-permute-start | bytes 1572872 | tf_op jit(solution)/shard_map/ppermute | solution.py:438
  204.8 35.0 %collective-permute-start.13 = (bf16[512,512]{1,0:T(8,128)(2,1)S(1)}, bf16[512,512]{1,0:T(8,128)(2,1)}, u32[]{:S(2)}, u32[]{:S(2)}) collective-permute-start(bf16[512,512]{1,0:T(8,128)(2,1)S(1)} %slice.339), channel_id=1, source_target_pairs={{0,1},{1,0},{2,3},{3,2},{4,5},{5,4},{6,7},{7,6},{8,9},{9,8},{10,11... | collective-permute-start | bytes 1572872 | tf_op jit(solution)/shard_map/ppermute | solution.py:438
  205.2 34.5 %collective-permute-start.12 = (bf16[512,512]{1,0:T(8,128)(2,1)S(1)}, bf16[512,512]{1,0:T(8,128)(2,1)}, u32[]{:S(2)}, u32[]{:S(2)}) collective-permute-start(bf16[512,512]{1,0:T(8,128)(2,1)S(1)} %slice.338), channel_id=1, source_target_pairs={{0,2},{1,3},{2,0},{3,1},{4,6},{5,7},{6,4},{7,5},{8,10},{9,11},{10,... | collective-permute-start | bytes 1572872 | tf_op jit(solution)/shard_map/ppermute | solution.py:438
  266.3 25.4 %collective-permute-start.14 = (bf16[2,512,512]{2,1,0:T(8,128)(2,1)S(1)}, bf16[2,512,512]{2,1,0:T(8,128)(2,1)S(1)}, u32[]{:S(2)}, u32[]{:S(2)}) collective-permute-start(bf16[2,512,512]{2,1,0:T(8,128)(2,1)S(1)} %pad_maximum_fusion.5), channel_id=1, source_target_pairs={{0,1},{1,0},{2,3},{3,2},{4,5},{5,4},{6,7},{7,6},{8,9},{9,8},{10,11... | collective-permute-start | bytes 3145736 | tf_op jit(solution)/shard_map/ppermute | solution.py:438
  267.8 25.0 %collective-permute-start.15 = (bf16[2,512,512]{2,1,0:T(8,128)(2,1)S(1)}, bf16[2,512,512]{2,1,0:T(8,128)(2,1)S(1)}, u32[]{:S(2)}, u32[]{:S(2)}) collective-permute-start(bf16[2,512,512]{2,1,0:T(8,128)(2,1)S(1)} %stack.68), channel_id=1, source_target_pairs={{0,2},{1,3},{2,0},{3,1},{4,6},{5,7},{6,4},{7,5},{8,10},{9,11},{10,... | collective-permute-start | bytes 3145736 | tf_op jit(solution)/shard_map/ppermute | solution.py:438
  293.2 13.0 %collective-permute-start.17 = (bf16[1,512,512]{2,1,0:T(8,128)(2,1)S(1)}, bf16[1,512,512]{2,1,0:T(8,128)(2,1)S(1)}, u32[]{:S(2)}, u32[]{:S(2)}) collective-permute-start(bf16[1,512,512]{2,1,0:T(8,128)(2,1)S(1)} %get-tuple-element.138), channel_id=1, source_target_pairs={{0,1},{1,0},{2,3},{3,2},{4,5},{5,4},{6,7},{7,6},{8,9},{9,8},{10,11... | collective-permute-start | bytes 1572872 | tf_op jit(solution)/shard_map/ppermute | solution.py:438
  293.8 12.7 %collective-permute-start.16 = (bf16[1,512,512]{2,1,0:T(8,128)(2,1)S(1)}, bf16[1,512,512]{2,1,0:T(8,128)(2,1)S(1)}, u32[]{:S(2)}, u32[]{:S(2)}) collective-permute-start(bf16[1,512,512]{2,1,0:T(8,128)(2,1)S(1)} %get-tuple-element.139), channel_id=1, source_target_pairs={{0,2},{1,3},{2,0},{3,1},{4,6},{5,7},{6,4},{7,5},{8,10},{9,11},{10,... | collective-permute-start | bytes 1572872 | tf_op jit(solution)/shard_map/ppermute | solution.py:438
  308.9 23.1 %collective-permute-start.19 = (bf16[1024,512]{1,0:T(8,128)(2,1)S(1)}, bf16[1024,512]{1,0:T(8,128)(2,1)S(1)}, u32[]{:S(2)}, u32[]{:S(2)}) collective-permute-start(bf16[1024,512]{1,0:T(8,128)(2,1)S(1)} %fusion.refs_0_), channel_id=1, source_target_pairs={{0,2},{1,3},{2,0},{3,1},{4,6},{5,7},{6,4},{7,5},{8,10},{9,11},{10,... | collective-permute-start | bytes 3145736 | tf_op jit(solution)/shard_map/ppermute | solution.py:438
  310.6 23.7 %collective-permute-start.18 = (bf16[1024,512]{1,0:T(8,128)(2,1)S(1)}, bf16[1024,512]{1,0:T(8,128)(2,1)S(1)}, u32[]{:S(2)}, u32[]{:S(2)}) collective-permute-start(bf16[1024,512]{1,0:T(8,128)(2,1)S(1)} %fusion.refs_0_), channel_id=1, source_target_pairs={{0,1},{1,0},{2,3},{3,2},{4,5},{5,4},{6,7},{7,6},{8,9},{9,8},{10,11... | collective-permute-start | bytes 3145736 | tf_op jit(solution)/shard_map/ppermute | solution.py:438
  332.9 11.8 %collective-permute-start.21 = (bf16[512,512]{1,0:T(8,128)(2,1)}, bf16[512,512]{1,0:T(8,128)(2,1)}, u32[]{:S(2)}, u32[]{:S(2)}) collective-permute-start(bf16[512,512]{1,0:T(8,128)(2,1)} %slice.347), channel_id=1, source_target_pairs={{0,1},{1,0},{2,3},{3,2},{4,5},{5,4},{6,7},{7,6},{8,9},{9,8},{10,11... | collective-permute-start | bytes 1572872 | tf_op jit(solution)/shard_map/ppermute | solution.py:438
  335.2 10.9 %collective-permute-start.20 = (bf16[512,512]{1,0:T(8,128)(2,1)}, bf16[512,512]{1,0:T(8,128)(2,1)}, u32[]{:S(2)}, u32[]{:S(2)}) collective-permute-start(bf16[512,512]{1,0:T(8,128)(2,1)} %slice.346), channel_id=1, source_target_pairs={{0,2},{1,3},{2,0},{3,1},{4,6},{5,7},{6,4},{7,5},{8,10},{9,11},{10,... | collective-permute-start | bytes 1572872 | tf_op jit(solution)/shard_map/ppermute | solution.py:438
  376.1 275.9 %reduce-scatter.3.cloned.1.call-start = ((), (), s32[]{:S(2)}) async-start(), calls=%async_computation.4 | async-start | bytes 16515072 | tf_op jit(solution)/shard_map/reduce_scatter | solution.py:933
  410.4 37.2 %collective-permute-start.22 = (bf16[2,1,512,512]{3,2,1,0:T(8,128)(2,1)S(1)}, bf16[2,1,512,512]{3,2,1,0:T(8,128)(2,1)S(1)}, u32[]{:S(2)}, u32[]{:S(2)}) collective-permute-start(bf16[2,1,512,512]{3,2,1,0:T(8,128)(2,1)S(1)} %pad_maximum_fusion.6), channel_id=1, source_target_pairs={{0,1},{1,0},{2,3},{3,2},{4,5},{5,4},{6,7},{7,6},{8,9},{9,8},{10,11... | collective-permute-start | bytes 3145736 | tf_op jit(solution)/shard_map/ppermute | solution.py:438
  411.3 36.3 %collective-permute-start.24 = (bf16[2,1,512,512]{3,2,1,0:T(8,128)(2,1)S(1)}, bf16[2,1,512,512]{3,2,1,0:T(8,128)(2,1)S(1)}, u32[]{:S(2)}, u32[]{:S(2)}) collective-permute-start(bf16[2,1,512,512]{3,2,1,0:T(8,128)(2,1)S(1)} %stack.69), channel_id=1, source_target_pairs={{0,2},{1,3},{2,0},{3,1},{4,6},{5,7},{6,4},{7,5},{8,10},{9,11},{10,... | collective-permute-start | bytes 3145736 | tf_op jit(solution)/shard_map/ppermute | solution.py:438
  430.7 72.8 %collective-permute-start.26 = (bf16[2,2,512,512]{3,2,1,0:T(8,128)(2,1)}, bf16[2,2,512,512]{3,2,1,0:T(8,128)(2,1)S(1)}, u32[]{:S(2)}, u32[]{:S(2)}) collective-permute-start(bf16[2,2,512,512]{3,2,1,0:T(8,128)(2,1)} %pad_maximum_fusion), channel_id=1, source_target_pairs={{0,1},{1,0},{2,3},{3,2},{4,5},{5,4},{6,7},{7,6},{8,9},{9,8},{10,11... | collective-permute-start | bytes 6291464 | tf_op jit(solution)/shard_map/ppermute | solution.py:438
  431.9 71.6 %collective-permute-start.27 = (bf16[2,2,512,512]{3,2,1,0:T(8,128)(2,1)}, bf16[2,2,512,512]{3,2,1,0:T(8,128)(2,1)}, u32[]{:S(2)}, u32[]{:S(2)}) collective-permute-start(bf16[2,2,512,512]{3,2,1,0:T(8,128)(2,1)} %stack.70), channel_id=1, source_target_pairs={{0,2},{1,3},{2,0},{3,1},{4,6},{5,7},{6,4},{7,5},{8,10},{9,11},{10,... | collective-permute-start | bytes 6291464 | tf_op jit(solution)/shard_map/ppermute | solution.py:438
  464.1 4.5 collective-permute-start.34
  464.1 32.3 %collective-permute-start.41 = (f32[48,1024]{1,0:T(8,128)S(1)}, f32[48,1024]{1,0:T(8,128)S(1)}, u32[]{:S(2)}, u32[]{:S(2)}) collective-permute-start(f32[48,1024]{1,0:T(8,128)S(1)} %copy-done.22), channel_id=1, source_target_pairs={{0,1},{1,0},{2,3},{3,2},{4,5},{5,4},{6,7},{7,6},{8,9},{9,8},{10,11... | collective-permute-start | bytes 589832 | tf_op jit(solution)/shard_map/ppermute | solution.py:438
  467.4 36.1 %collective-permute-start.28 = (bf16[2,512,512]{2,1,0:T(8,128)(2,1)}, bf16[2,512,512]{2,1,0:T(8,128)(2,1)}, u32[]{:S(2)}, u32[]{:S(2)}) collective-permute-start(bf16[2,512,512]{2,1,0:T(8,128)(2,1)} %pad_maximum_fusion.7), channel_id=1, source_target_pairs={{0,1},{1,0},{2,3},{3,2},{4,5},{5,4},{6,7},{7,6},{8,9},{9,8},{10,11... | collective-permute-start | bytes 3145736 | tf_op jit(solution)/shard_map/ppermute | solution.py:438
  469.2 34.3 %collective-permute-start.29 = (bf16[2,512,512]{2,1,0:T(8,128)(2,1)}, bf16[2,512,512]{2,1,0:T(8,128)(2,1)}, u32[]{:S(2)}, u32[]{:S(2)}) collective-permute-start(bf16[2,512,512]{2,1,0:T(8,128)(2,1)} %stack.71), channel_id=1, source_target_pairs={{0,2},{1,3},{2,0},{3,1},{4,6},{5,7},{6,4},{7,5},{8,10},{9,11},{10,... | collective-permute-start | bytes 3145736 | tf_op jit(solution)/shard_map/ppermute | solution.py:438
  505.2 14.9 %collective-permute-start.25 = (bf16[1,1,512,512]{3,2,1,0:T(8,128)(2,1)S(1)}, bf16[1,1,512,512]{3,2,1,0:T(8,128)(2,1)S(1)}, u32[]{:S(2)}, u32[]{:S(2)}) collective-permute-start(bf16[1,1,512,512]{3,2,1,0:T(8,128)(2,1)S(1)} %get-tuple-element.132), channel_id=1, source_target_pairs={{0,1},{1,0},{2,3},{3,2},{4,5},{5,4},{6,7},{7,6},{8,9},{9,8},{10,11... | collective-permute-start | bytes 1572872 | tf_op jit(solution)/shard_map/ppermute | solution.py:438
  509.8 44.6 %collective-permute-start.31 = (bf16[1,2,512,512]{3,2,1,0:T(8,128)(2,1)S(1)}, bf16[1,2,512,512]{3,2,1,0:T(8,128)(2,1)S(1)}, u32[]{:S(2)}, u32[]{:S(2)}) collective-permute-start(bf16[1,2,512,512]{3,2,1,0:T(8,128)(2,1)S(1)} %get-tuple-element.120), channel_id=1, source_target_pairs={{0,1},{1,0},{2,3},{3,2},{4,5},{5,4},{6,7},{7,6},{8,9},{9,8},{10,11... | collective-permute-start | bytes 3145736 | tf_op jit(solution)/shard_map/ppermute | solution.py:438
  510.2 44.3 %collective-permute-start.30 = (bf16[1,2,512,512]{3,2,1,0:T(8,128)(2,1)S(1)}, bf16[1,2,512,512]{3,2,1,0:T(8,128)(2,1)S(1)}, u32[]{:S(2)}, u32[]{:S(2)}) collective-permute-start(bf16[1,2,512,512]{3,2,1,0:T(8,128)(2,1)S(1)} %get-tuple-element.121), channel_id=1, source_target_pairs={{0,2},{1,3},{2,0},{3,1},{4,6},{5,7},{6,4},{7,5},{8,10},{9,11},{10,... | collective-permute-start | bytes 3145736 | tf_op jit(solution)/shard_map/ppermute | solution.py:438
  512.0 35.5 %collective-permute-start.23 = (bf16[1,1,512,512]{3,2,1,0:T(8,128)(2,1)S(1)}, bf16[1,1,512,512]{3,2,1,0:T(8,128)(2,1)S(1)}, u32[]{:S(2)}, u32[]{:S(2)}) collective-permute-start(bf16[1,1,512,512]{3,2,1,0:T(8,128)(2,1)S(1)} %get-tuple-element.133), channel_id=1, source_target_pairs={{0,2},{1,3},{2,0},{3,1},{4,6},{5,7},{6,4},{7,5},{8,10},{9,11},{10,... | collective-permute-start | bytes 1572872 | tf_op jit(solution)/shard_map/ppermute | solution.py:438
  512.2 4.5 collective-permute-start.35
  516.7 33.4 %collective-permute-start.33 = (bf16[1,512,512]{2,1,0:T(8,128)(2,1)S(1)}, bf16[1,512,512]{2,1,0:T(8,128)(2,1)S(1)}, u32[]{:S(2)}, u32[]{:S(2)}) collective-permute-start(bf16[1,512,512]{2,1,0:T(8,128)(2,1)S(1)} %get-tuple-element.128), channel_id=1, source_target_pairs={{0,1},{1,0},{2,3},{3,2},{4,5},{5,4},{6,7},{7,6},{8,9},{9,8},{10,11... | collective-permute-start | bytes 1572872 | tf_op jit(solution)/shard_map/ppermute | solution.py:438
  520.1 34.3 %collective-permute-start.32 = (bf16[1,512,512]{2,1,0:T(8,128)(2,1)S(1)}, bf16[1,512,512]{2,1,0:T(8,128)(2,1)S(1)}, u32[]{:S(2)}, u32[]{:S(2)}) collective-permute-start(bf16[1,512,512]{2,1,0:T(8,128)(2,1)S(1)} %get-tuple-element.129), channel_id=1, source_target_pairs={{0,2},{1,3},{2,0},{3,1},{4,6},{5,7},{6,4},{7,5},{8,10},{9,11},{10,... | collective-permute-start | bytes 1572872 | tf_op jit(solution)/shard_map/ppermute | solution.py:438
  582.8 9.4 %collective-permute-start.36 = (f32[48,1024]{1,0:T(8,128)}, f32[48,1024]{1,0:T(8,128)S(1)}, u32[]{:S(2)}, u32[]{:S(2)}) collective-permute-start(f32[48,1024]{1,0:T(8,128)} %get-tuple-element.106), channel_id=1, source_target_pairs={{0,1},{1,0},{2,3},{3,2},{4,5},{5,4},{6,7},{7,6},{8,9},{9,8},{10,11... | collective-permute-start | bytes 589832 | tf_op jit(solution)/shard_map/ppermute | solution.py:438
  583.8 7.7 %collective-permute-start.37 = (f32[8,512]{1,0:T(8,128)}, f32[8,512]{1,0:T(8,128)S(1)}, u32[]{:S(2)}, u32[]{:S(2)}) collective-permute-start(f32[8,512]{1,0:T(8,128)} %get-tuple-element.107), channel_id=1, source_target_pairs={{0,4},{4,0},{8,12},{12,8},{16,20},{20,16},{24,28},{28,24},{1,5},{5... | collective-permute-start | bytes 49160 | tf_op jit(solution)/shard_map/ppermute | solution.py:438
  583.8 5.6 collective-permute-start.38
  590.0 7.8 %collective-permute-start.42 = (f32[48,1024]{1,0:T(8,128)S(1)}, f32[48,1024]{1,0:T(8,128)S(1)}, u32[]{:S(2)}, u32[]{:S(2)}) collective-permute-start(f32[48,1024]{1,0:T(8,128)S(1)} %add.281), channel_id=1, source_target_pairs={{0,2},{1,3},{2,0},{3,1},{4,6},{5,7},{6,4},{7,5},{8,10},{9,11},{10,... | collective-permute-start | bytes 589832 | tf_op jit(solution)/shard_map/ppermute | solution.py:438
  593.1 7.9 %collective-permute-start.39 = (f32[48,1024]{1,0:T(8,128)S(1)}, f32[48,1024]{1,0:T(8,128)S(1)}, u32[]{:S(2)}, u32[]{:S(2)}) collective-permute-start(f32[48,1024]{1,0:T(8,128)S(1)} %add.274), channel_id=1, source_target_pairs={{0,2},{1,3},{2,0},{3,1},{4,6},{5,7},{6,4},{7,5},{8,10},{9,11},{10,... | collective-permute-start | bytes 589832 | tf_op jit(solution)/shard_map/ppermute | solution.py:438
  593.9 4.4 collective-permute-start.40
  601.1 5.4 collective-permute-start.43
  606.5 4.3 collective-permute-start.44
  610.8 22.3 %collective-permute-start.45 = (f32[8,2048]{1,0:T(8,128)S(1)}, f32[8,2048]{1,0:T(8,128)S(1)}, u32[]{:S(2)}, u32[]{:S(2)}) collective-permute-start(f32[8,2048]{1,0:T(8,128)S(1)} %add_dynamic-update-slice_fusion), channel_id=1, source_target_pairs={{0,2},{1,3},{2,0},{3,1},{4,6},{5,7},{6,4},{7,5},{8,10},{9,11},{10,... | collective-permute-start | bytes 196616 | tf_op jit(solution)/shard_map/ppermute | solution.py:438
  (38 other events, 420.4 us)
Sparse Core Ops, SparseCore 0:
  10.2 137.1 all-gather.2
  149.0 97.9 all-gather.4
  376.2 108.8 reduce-scatter.4
  503.6 148.2 reduce-scatter.2

commit v6 on v5

--- a/solution.py
+++ b/solution.py
@@ -911,8 +911,6 @@
     )
     wide_part = after(
         wide_part,
-        fixed_got,
-        next_got,
         *scatter_arrived(states_b),
         *scatter_arrived(last_states),
     )

time: 676 us -> 672 us (level)
  transfers between devices with their start and end apart: 50 -> 50, of which waited for: 28 -> 30; matrix products, arithmetic and copies ran while one was open for 9% -> 9% of each run, Pallas kernels for 33% -> 34%
where the time goes in v6:
time: 672 us; the launch traced here: 661 us
  Pallas kernels  267 us (40%)
  waiting for transfers between devices  241 us (36%)
  starting transfers between devices  43.7 us (7%)
  other arithmetic  41.6 us (6%)
  local copies, waits for them, and re-layouts  37.4 us (6%)
  between operations  15.4 us (2%)
  blocking collectives  14.8 us (2%)
    pallas_call x17, Pallas kernels, kernel_call(): return call(place, *[a for a, _, _ in ins])  250 us
    ppermute x46, waiting for transfers between devices, swap(): return lax.ppermute(values, axis, [(i, i ^ bit) for i in range(count)])  221 us
    ppermute x46, starting transfers between devices, swap(): return lax.ppermute(values, axis, [(i, i ^ bit) for i in range(count)])  43.5 us
    pallas_call x1, Pallas kernels, per_device(): pl.pallas_call(attend_back_kernel, out_shape=jax.ShapeDtypeStruct((3, tok...  17.5 us
    all_gather x1, blocking collectives, per_device(): smalls = lax.all_gather(smalls, 'dp', axis=0, tiled=True)  14.8 us
  transfers between devices with their start and end apart: 50, of which 30 were waited for; matrix products, arithmetic and copies ran while one was open for 9% of the time, Pallas kernels for 34%

profile of v6, /device:TPU:0, one launch (start us, length us, event | category | flops | bytes accessed | tf_op | source)
XLA Modules:
  0.0 661.1 jit_solution(2252748477202273523)
XLA Ops:
  11.8 3.0 collective-permute-start.1
  16.3 14.8 %all_gather.9 = bf16[2048,48]{0,1:T(8,128)(2,1)S(1)} all-gather(bf16[256,48]{0,1:T(8,128)(2,1)S(1)} %pad_maximum_fusion.8), channel_id=1, replica_groups=mesh['dp'=8,'tensor'=4] {'dp'}, dimensions={0}, use_global_device_ids=true | all-gather | bytes 221184 | tf_op jit(solution)/shard_map/all_gather | solution.py:579
  31.2 2.0 copy.38
  33.8 14.4 %mix.1 = (f32[4,1024,512]{2,1,0:T(8,128)}, f32[8,1024]{1,0:T(8,128)}) custom-call(s32[2]{0:T(128)} %pad_add_fusion.place, bf16[9,1024,512]{2,1,0:T(8,128)(2,1)} %hist.5, f32[1024,36]{1,0:T(8,128)} %bitcast.43), custom_call_target="tpu_custom_call" | custom-call | flops 37748736 | bytes 18006016 | tf_op jit(solution)/shard_map/mix/pallas_call | solution.py:58
  48.7 3.7 collective-permute-done.2
  54.1 2.9 collective-permute-done.3
  57.7 9.6 %norm.1 = (bf16[3,1024,512]{2,1,0:T(8,128)(2,1)}, bf16[1024,512]{1,0:T(8,128)(2,1)}) custom-call(s32[2]{0:T(128)} %pad_add_fusion.place, f32[4,1024,512]{2,1,0:T(8,128)} %get-tuple-element.69.streams, f32[8,1024]{1,0:T(8,128)} %add.235.stats, f32[4,512]{1,0:T(4,128)} %get-tuple-element.153.gain, f32[4,512]{1,0:T(4,128)} %get-tuple-element.152.bias), custom_call_target="tpu_custom_call" | custom-call | bytes 12632064 | tf_op jit(solution)/shard_map/norm/pallas_call | solution.py:58
  68.1 14.8 %spread.1 = f32[48,1024]{1,0:T(8,128)} custom-call(s32[2]{0:T(128)} %pad_add_fusion.place, f32[4,1024,512]{2,1,0:T(8,128)} %get-tuple-element.69.streams, f32[8,1024]{1,0:T(8,128)} %add.235.stats, bf16[9,1024,512]{2,1,0:T(8,128)(2,1)} %hist.5), custom_call_target="tpu_custom_call" | custom-call | bytes 18055168 | tf_op jit(solution)/shard_map/spread/pallas_call | solution.py:58
  82.9 53.6 %collective-permute-done.5.refs_2_.refs_7_ = bf16[3,1024,512]{2,1,0:T(8,128)(2,1)S(1)} collective-permute-done((bf16[3,1024,512]{2,1,0:T(8,128)(2,1)}, bf16[3,1024,512]{2,1,0:T(8,128)(2,1)S(1)}, u32[]{:S(2)}, u32[]{:S(2)}) %collective-permute-start.5) | collective-permute-done | bytes 3145760 | tf_op jit(solution)/shard_map/ppermute | solution.py:438
  143.5 29.2 %collective-permute-done.7.refs_4_.refs_9_ = bf16[3,512,512]{2,1,0:T(8,128)(2,1)} collective-permute-done((bf16[3,512,512]{2,1,0:T(8,128)(2,1)}, bf16[3,512,512]{2,1,0:T(8,128)(2,1)}, u32[]{:S(2)}, u32[]{:S(2)}) %collective-permute-start.7) | collective-permute-done | bytes 1572896 | tf_op jit(solution)/shard_map/ppermute | solution.py:438
  178.4 15.4 %qkv.1.q.k.v = bf16[3,1024,512]{2,1,0:T(8,128)(2,1)} custom-call(s32[2]{0:T(128)} %pad_add_fusion.place, bf16[3,1024,512]{2,1,0:T(8,128)(2,1)} %get-tuple-element.68.refs_0_.refs_5_, bf16[3,1024,512]{2,1,0:T(8,128)(2,1)} %copy-done.3, bf16[3,1024,512]{2,1,0:T(8,128)(2,1)} %copy-done.2, bf16[3,512,512]{2,1,0:T(8,128)(2,1)} %collective-permute-done.6.refs_3_.refs_8_, ...), custom_call_target="tpu_custom_call" | custom-call | flops 6442450944 | bytes 76021760 | tf_op jit(solution)/shard_map/qkv/pallas_call | solution.py:58
  193.9 2.5 collective-permute-done.9.refs_2_
  199.1 2.1 collective-permute-start.10
  205.3 11.5 %attend.1.attended = bf16[1024,512]{1,0:T(8,128)(2,1)} custom-call(s32[2]{0:T(128)} %pad_add_fusion.place, bf16[3,1024,512]{2,1,0:T(8,128)(2,1)} %qkv.1.q.k.v, bf16[3,1024,512]{2,1,0:T(8,128)(2,1)} %qkv.1.q.k.v, bf16[3,1024,512]{2,1,0:T(8,128)(2,1)} %qkv.1.q.k.v), custom_call_target="tpu_custom_call" | custom-call | flops 2147483648 | bytes 10485760 | tf_op jit(solution)/shard_map/attend/pallas_call | solution.py:58
  218.4 21.4 %up.1 = (bf16[1024,2048]{1,0:T(8,128)(2,1)}, bf16[1024,2048]{1,0:T(8,128)(2,1)}) custom-call(s32[2]{0:T(128)} %pad_add_fusion.place, bf16[1024,512]{1,0:T(8,128)(2,1)} %get-tuple-element.73.refs_0_, bf16[1024,512]{1,0:T(8,128)(2,1)} %copy-done.8, bf16[1024,512]{1,0:T(8,128)(2,1)} %copy-done.7, bf16[512,512]{1,0:T(8,128)(2,1)} %copy-done.24, ...), custom_call_target="tpu_custom_call" | custom-call | flops 8589934592 | bytes 71303168 | tf_op jit(solution)/shard_map/up/pallas_call | solution.py:58
  239.9 7.1 %all-gather.5.cloned.1.call-done.down.out.weight = bf16[2560,2048]{1,0:T(8,128)(2,1)} async-done(((bf16[2560,256]{1,0:T(8,128)(2,1)}), bf16[2560,2048]{1,0:T(8,128)(2,1)}) %all-gather.5.cloned.1.call-update) | async-done | bytes 10485776 | tf_op jit(solution)/shard_map/all_gather | solution.py:588
  247.0 16.5 %down.1 = bf16[4,1024,512]{2,1,0:T(8,128)(2,1)} custom-call(s32[2]{0:T(128)} %pad_add_fusion.place, bf16[1024,2048]{1,0:T(8,128)(2,1)} %get-tuple-element.80.hidden, bf16[1024,512]{1,0:T(8,128)(2,1)} %attend.1.attended, bf16[2560,2048]{1,0:T(8,128)(2,1)} %all-gather.5.cloned.1.call-done.down.out.weight, ...), custom_call_target="tpu_custom_call" | custom-call | flops 10737418240 | bytes 30408704 | tf_op jit(solution)/shard_map/down/pallas_call | solution.py:58
  269.3 22.4 %collective-permute-done.14 = bf16[2,512,512]{2,1,0:T(8,128)(2,1)S(1)} collective-permute-done((bf16[2,512,512]{2,1,0:T(8,128)(2,1)S(1)}, bf16[2,512,512]{2,1,0:T(8,128)(2,1)S(1)}, u32[]{:S(2)}, u32[]{:S(2)}) %collective-permute-start.14) | collective-permute-done | bytes 1048608 | tf_op jit(solution)/shard_map/ppermute | solution.py:438
  295.3 11.0 %collective-permute-done.17 = bf16[1,512,512]{2,1,0:T(8,128)(2,1)S(1)} collective-permute-done((bf16[1,512,512]{2,1,0:T(8,128)(2,1)S(1)}, bf16[1,512,512]{2,1,0:T(8,128)(2,1)S(1)}, u32[]{:S(2)}, u32[]{:S(2)}) %collective-permute-start.17) | collective-permute-done | bytes 524320 | tf_op jit(solution)/shard_map/ppermute | solution.py:438
  311.9 20.3 %collective-permute-done.19.refs_2_ = bf16[1024,512]{1,0:T(8,128)(2,1)S(1)} collective-permute-done((bf16[1024,512]{1,0:T(8,128)(2,1)S(1)}, bf16[1024,512]{1,0:T(8,128)(2,1)S(1)}, u32[]{:S(2)}, u32[]{:S(2)}) %collective-permute-start.19) | collective-permute-done | bytes 1048608 | tf_op jit(solution)/shard_map/ppermute | solution.py:438
  337.7 6.9 %collective-permute-done.21.refs_4_ = bf16[512,512]{1,0:T(8,128)(2,1)} collective-permute-done((bf16[512,512]{1,0:T(8,128)(2,1)}, bf16[512,512]{1,0:T(8,128)(2,1)}, u32[]{:S(2)}, u32[]{:S(2)}) %collective-permute-start.21) | collective-permute-done | bytes 524320 | tf_op jit(solution)/shard_map/ppermute | solution.py:438
  346.2 11.4 %middle.1 = (bf16[1024,2048]{1,0:T(8,128)(2,1)}, f32[1024,512]{1,0:T(8,128)}, f32[40,1024]{1,0:T(8,128)}, f32[40,40]{1,0:T(8,128)}, f32[40,2048]{1,0:T(8,128)}) custom-call(s32[2]{0:T(128)} %pad_add_fusion.place, bf16[1024,512]{1,0:T(8,128)(2,1)} %copy-done.6, bf16[1024,512]{1,0:T(8,128)(2,1)} %copy-done.14, bf16[1024,512]{1,0:T(8,128)(2,1)} %copy-done.13, ...), custom_call_target="tpu_custom_call" | custom-call | flops 503316480 | bytes 15922560 | tf_op jit(solution)/shard_map/middle/pallas_call | solution.py:58
  358.6 16.9 %down_grad.1 = bf16[2608,2048]{1,0:T(8,128)(2,1)} custom-call(s32[2]{0:T(128)} %pad_add_fusion.place, bf16[1024,2048]{1,0:T(8,128)(2,1)} %get-tuple-element.80.hidden, bf16[1024,512]{1,0:T(8,128)(2,1)} %attend.1.attended, bf16[1024,2048]{1,0:T(8,128)(2,1)} %get-tuple-element.90.branch_grad.grad), custom_call_target="tpu_custom_call" | custom-call | flops 10737418240 | bytes 20119552 | tf_op jit(solution)/shard_map/down_grad/pallas_call | solution.py:58
  376.2 7.2 %attended_grad.1.grad = bf16[1024,512]{1,0:T(8,128)(2,1)} custom-call(s32[2]{0:T(128)} %pad_add_fusion.place, bf16[1024,2048]{1,0:T(8,128)(2,1)} %get-tuple-element.90.branch_grad.grad, bf16[2560,2048]{1,0:T(8,128)(2,1)} %all-gather.5.cloned.1.call-done.down.out.weight), custom_call_target="tpu_custom_call" | custom-call | flops 2147483648 | bytes 15728640 | tf_op jit(solution)/shard_map/attended_grad/pallas_call | solution.py:58
  383.4 17.5 %attend_back.1.grad.refs_11_ = bf16[3,1024,512]{2,1,0:T(8,128)(2,1)} custom-call(s32[2]{0:T(128)} %pad_add_fusion.place, bf16[3,1024,512]{2,1,0:T(8,128)(2,1)} %qkv.1.q.k.v, bf16[3,1024,512]{2,1,0:T(8,128)(2,1)} %qkv.1.q.k.v, bf16[3,1024,512]{2,1,0:T(8,128)(2,1)} %qkv.1.q.k.v, bf16[1024,512]{1,0:T(8,128)(2,1)} %attended_grad.1.grad, ...), custom_call_target="tpu_custom_call" | custom-call | flops 5368709120 | bytes 8388608 | tf_op jit(solution)/shard_map/attend_back/pallas_call | solution.py:799
  400.9 6.9 %qkv_back.2 = bf16[4,1,1024,512]{3,2,1,0:T(8,128)(2,1)} custom-call(s32[2]{0:T(128)} %pad_add_fusion.place, bf16[3,1024,512]{2,1,0:T(8,128)(2,1)} %attend_back.1.grad.refs_11_, bf16[2048,3584]{1,0:T(8,128)(2,1)} %all-gather.3.cloned.1.call-done.refs_5_.refs_6_.refs_7_.refs_8_.weight), custom_call_target="tpu_custom_call" | custom-call | flops 2147483648 | bytes 22020096 | tf_op jit(solution)/shard_map/qkv_back/pallas_call | solution.py:58
  412.8 11.5 %qkv_back.3 = bf16[4,2,1024,512]{3,2,1,0:T(8,128)(2,1)} custom-call(s32[2]{0:T(128)} %pad_add_fusion.place, bf16[3,1024,512]{2,1,0:T(8,128)(2,1)} %attend_back.1.grad.refs_11_, bf16[2048,3584]{1,0:T(8,128)(2,1)} %all-gather.3.cloned.1.call-done.refs_5_.refs_6_.refs_7_.refs_8_.weight), custom_call_target="tpu_custom_call" | custom-call | flops 4294967296 | bytes 26214400 | tf_op jit(solution)/shard_map/qkv_back/pallas_call | solution.py:58
  425.9 3.1 stack.70
  432.6 15.1 %hidden_grad.1.grad.refs_10_ = bf16[1024,2048]{1,0:T(8,128)(2,1)} custom-call(s32[2]{0:T(128)} %pad_add_fusion.place, bf16[1024,2048]{1,0:T(8,128)(2,1)} %get-tuple-element.90.branch_grad.grad, bf16[2560,2048]{1,0:T(8,128)(2,1)} %all-gather.5.cloned.1.call-done.down.out.weight, bf16[1024,2048]{1,0:T(8,128)(2,1)} %get-tuple-element.91.slope), custom_call_target="tpu_custom_call" | custom-call | flops 8589934592 | bytes 23068672 | tf_op jit(solution)/shard_map/hidden_grad/pallas_call | solution.py:58
  447.7 14.1 %up_back.1 = bf16[4,1024,512]{2,1,0:T(8,128)(2,1)} custom-call(s32[2]{0:T(128)} %pad_add_fusion.place, bf16[1024,2048]{1,0:T(8,128)(2,1)} %hidden_grad.1.grad.refs_10_, bf16[2048,3584]{1,0:T(8,128)(2,1)} %all-gather.3.cloned.1.call-done.refs_5_.refs_6_.refs_7_.refs_8_.weight), custom_call_target="tpu_custom_call" | custom-call | flops 8589934592 | bytes 23068672 | tf_op jit(solution)/shard_map/up_back/pallas_call | solution.py:58
  461.8 2.3 stack.71
  468.5 25.6 %weight_grad.1 = bf16[2048,3584]{1,0:T(8,128)(2,1)} custom-call(s32[2]{0:T(128)} %pad_add_fusion.place, bf16[1024,512]{1,0:T(8,128)(2,1)} %get-tuple-element.73.refs_0_, bf16[1024,512]{1,0:T(8,128)(2,1)} %copy-done.8, bf16[1024,512]{1,0:T(8,128)(2,1)} %copy-done.7, bf16[512,512]{1,0:T(8,128)(2,1)} %copy-done.24, bf16[512,512]{1,0:T(8,128)(2,1)} %copy-done.23, ...), custom_call_target="tpu_custom_call" | custom-call | flops 15032385536 | bytes 38797312 | tf_op jit(solution)/shard_map/weight_grad/pallas_call | solution.py:58
  494.1 5.2 collective-permute-done.28
  502.8 4.1 add_convert_fusion
  511.0 2.9 collective-permute-done.35
  518.1 26.4 %collective-permute-done.23 = bf16[1,1,512,512]{3,2,1,0:T(8,128)(2,1)S(1)} collective-permute-done((bf16[1,1,512,512]{3,2,1,0:T(8,128)(2,1)S(1)}, bf16[1,1,512,512]{3,2,1,0:T(8,128)(2,1)S(1)}, u32[]{:S(2)}, u32[]{:S(2)}) %collective-permute-start.23) | collective-permute-done | bytes 524320 | tf_op jit(solution)/shard_map/ppermute | solution.py:438
  546.1 2.9 collective-permute-done.33
  552.6 2.7 add_bitcast_fusion.1
  555.3 3.0 maximum_maximum_fusion.first
  561.5 17.8 %sums.1 = (f32[48,1024]{1,0:T(8,128)}, f32[8,512]{1,0:T(8,128)}) custom-call(s32[2]{0:T(128)} %pad_add_fusion.place, f32[3,1024,512]{2,1,0:T(8,128)} %maximum_maximum_fusion.first, f32[1024,512]{1,0:T(8,128)} %pad_maximum_fusion.1.last, f32[4,1024,512]{2,1,0:T(8,128)} %get-tuple-element.69.streams, f32[8,1024]{1,0:T(8,128)} %add.235.stats, ...), custom_call_target="tpu_custom_call" | custom-call | bytes 28565504 | tf_op jit(solution)/shard_map/sums/pallas_call | solution.py:58
  580.1 5.6 collective-permute-done.38
  590.2 4.0 collective-permute-done.42
  594.6 2.7 collective-permute-done.39
  597.5 5.3 collective-permute-done.43
  604.3 2.8 collective-permute-done.44
  609.8 19.6 %history.1 = f32[9,1024,512]{2,1,0:T(8,128)} custom-call(s32[2]{0:T(128)} %pad_add_fusion.place, f32[3,1024,512]{2,1,0:T(8,128)} %maximum_maximum_fusion.first, f32[1024,512]{1,0:T(8,128)} %pad_maximum_fusion.1.last, f32[4,1024,512]{2,1,0:T(8,128)} %get-tuple-element.69.streams, f32[8,1024]{1,0:T(8,128)} %add.235.stats, f32[4,512]{1,0:T(4,128)} %get-tuple-element.153.gain, ...), custom_call_target="tpu_custom_call" | custom-call | bytes 37969920 | tf_op jit(solution)/shard_map/history/pallas_call | solution.py:58
  631.9 2.8 slice.379
  635.5 13.0 %reduce-scatter.3.cloned.1.call-done = bf16[256,3584]{1,0:T(8,128)(2,1)} async-done(((bf16[2048,3584]{1,0:T(8,128)(2,1)}), bf16[256,3584]{1,0:T(8,128)(2,1)}) %reduce-scatter.3.cloned.1.call-update) | async-done | bytes 1835024 | tf_op jit(solution)/shard_map/reduce_scatter | solution.py:931
  (230 shorter events, 108.2 us)
Async XLA Ops:
  7.2 171.3 %all-gather.3.cloned.1.call-start = ((), (), s32[]{:S(2)}) async-start(), calls=%async_computation.2 | async-start | bytes 16515072 | tf_op jit(solution)/shard_map/all_gather | solution.py:585
  10.1 236.9 %all-gather.5.cloned.1.call-start = ((), (), s32[]{:S(2)}) async-start(), calls=%async_computation.3 | async-start | bytes 11796480 | tf_op jit(solution)/shard_map/all_gather | solution.py:588
  11.7 618.3 %reduce-scatter.5.cloned.1.call-start = ((), (), s32[]{:S(2)}) async-start(), calls=%async_computation.5 | async-start | bytes 12017664 | tf_op jit(solution)/shard_map/reduce_scatter | solution.py:927
  11.8 36.3 %collective-permute-start.1 = (bf16[1024,512]{1,0:T(8,128)(2,1)S(1)}, bf16[1024,512]{1,0:T(8,128)(2,1)S(1)}, u32[]{:S(2)}, u32[]{:S(2)}) collective-permute-start(bf16[1024,512]{1,0:T(8,128)(2,1)S(1)} %copy-done.20), channel_id=1, source_target_pairs={{0,2},{1,3},{2,0},{3,1},{4,6},{5,7},{6,4},{7,5},{8,10},{9,11},{10,... | collective-permute-start | bytes 3145736 | tf_op jit(solution)/shard_map/ppermute | solution.py:438
  14.8 33.3 %collective-permute-start = (bf16[1024,512]{1,0:T(8,128)(2,1)S(1)}, bf16[1024,512]{1,0:T(8,128)(2,1)S(1)}, u32[]{:S(2)}, u32[]{:S(2)}) collective-permute-start(bf16[1024,512]{1,0:T(8,128)(2,1)S(1)} %copy-done.20), channel_id=1, source_target_pairs={{0,1},{1,0},{2,3},{3,2},{4,5},{5,4},{6,7},{7,6},{8,9},{9,8},{10,11... | collective-permute-start | bytes 3145736 | tf_op jit(solution)/shard_map/ppermute | solution.py:438
  48.2 4.2 collective-permute-start.2
  67.3 69.3 %collective-permute-start.5 = (bf16[3,1024,512]{2,1,0:T(8,128)(2,1)}, bf16[3,1024,512]{2,1,0:T(8,128)(2,1)S(1)}, u32[]{:S(2)}, u32[]{:S(2)}) collective-permute-start(bf16[3,1024,512]{2,1,0:T(8,128)(2,1)} %get-tuple-element.68.refs_0_.refs_5_), channel_id=1, source_target_pairs={{0,2},{1,3},{2,0},{3,1},{4,6},{5,7},{6,4},{7,5},{8,10},{9,11},{10,... | collective-permute-start | bytes 9437192 | tf_op jit(solution)/shard_map/ppermute | solution.py:438
  67.9 70.4 %collective-permute-start.4 = (bf16[3,1024,512]{2,1,0:T(8,128)(2,1)}, bf16[3,1024,512]{2,1,0:T(8,128)(2,1)S(1)}, u32[]{:S(2)}, u32[]{:S(2)}) collective-permute-start(bf16[3,1024,512]{2,1,0:T(8,128)(2,1)} %get-tuple-element.68.refs_0_.refs_5_), channel_id=1, source_target_pairs={{0,1},{1,0},{2,3},{3,2},{4,5},{5,4},{6,7},{7,6},{8,9},{9,8},{10,11... | collective-permute-start | bytes 9437192 | tf_op jit(solution)/shard_map/ppermute | solution.py:438
  137.9 34.8 %collective-permute-start.7 = (bf16[3,512,512]{2,1,0:T(8,128)(2,1)}, bf16[3,512,512]{2,1,0:T(8,128)(2,1)}, u32[]{:S(2)}, u32[]{:S(2)}) collective-permute-start(bf16[3,512,512]{2,1,0:T(8,128)(2,1)} %slice.269), channel_id=1, source_target_pairs={{0,1},{1,0},{2,3},{3,2},{4,5},{5,4},{6,7},{7,6},{8,9},{9,8},{10,11... | collective-permute-start | bytes 4718600 | tf_op jit(solution)/shard_map/ppermute | solution.py:438
  139.7 34.6 %collective-permute-start.6 = (bf16[3,512,512]{2,1,0:T(8,128)(2,1)}, bf16[3,512,512]{2,1,0:T(8,128)(2,1)}, u32[]{:S(2)}, u32[]{:S(2)}) collective-permute-start(bf16[3,512,512]{2,1,0:T(8,128)(2,1)} %slice.268), channel_id=1, source_target_pairs={{0,2},{1,3},{2,0},{3,1},{4,6},{5,7},{6,4},{7,5},{8,10},{9,11},{10,... | collective-permute-start | bytes 4718600 | tf_op jit(solution)/shard_map/ppermute | solution.py:438
  174.2 22.2 %collective-permute-start.9 = (bf16[1024,512]{1,0:T(8,128)(2,1)}, bf16[1024,512]{1,0:T(8,128)(2,1)S(1)}, u32[]{:S(2)}, u32[]{:S(2)}) collective-permute-start(bf16[1024,512]{1,0:T(8,128)(2,1)} %get-tuple-element.73.refs_0_), channel_id=1, source_target_pairs={{0,2},{1,3},{2,0},{3,1},{4,6},{5,7},{6,4},{7,5},{8,10},{9,11},{10,... | collective-permute-start | bytes 3145736 | tf_op jit(solution)/shard_map/ppermute | solution.py:438
  174.5 22.6 %collective-permute-start.8 = (bf16[1024,512]{1,0:T(8,128)(2,1)}, bf16[1024,512]{1,0:T(8,128)(2,1)S(1)}, u32[]{:S(2)}, u32[]{:S(2)}) collective-permute-start(bf16[1024,512]{1,0:T(8,128)(2,1)} %get-tuple-element.73.refs_0_), channel_id=1, source_target_pairs={{0,1},{1,0},{2,3},{3,2},{4,5},{5,4},{6,7},{7,6},{8,9},{9,8},{10,11... | collective-permute-start | bytes 3145736 | tf_op jit(solution)/shard_map/ppermute | solution.py:438
  197.2 19.6 %collective-permute-start.11 = (bf16[512,512]{1,0:T(8,128)(2,1)S(1)}, bf16[512,512]{1,0:T(8,128)(2,1)S(1)}, u32[]{:S(2)}, u32[]{:S(2)}) collective-permute-start(bf16[512,512]{1,0:T(8,128)(2,1)S(1)} %slice.271), channel_id=1, source_target_pairs={{0,1},{1,0},{2,3},{3,2},{4,5},{5,4},{6,7},{7,6},{8,9},{9,8},{10,11... | collective-permute-start | bytes 1572872 | tf_op jit(solution)/shard_map/ppermute | solution.py:438
  199.1 17.7 %collective-permute-start.10 = (bf16[512,512]{1,0:T(8,128)(2,1)S(1)}, bf16[512,512]{1,0:T(8,128)(2,1)S(1)}, u32[]{:S(2)}, u32[]{:S(2)}) collective-permute-start(bf16[512,512]{1,0:T(8,128)(2,1)S(1)} %slice.270), channel_id=1, source_target_pairs={{0,2},{1,3},{2,0},{3,1},{4,6},{5,7},{6,4},{7,5},{8,10},{9,11},{10,... | collective-permute-start | bytes 1572872 | tf_op jit(solution)/shard_map/ppermute | solution.py:438
  204.8 35.1 %collective-permute-start.13 = (bf16[512,512]{1,0:T(8,128)(2,1)S(1)}, bf16[512,512]{1,0:T(8,128)(2,1)}, u32[]{:S(2)}, u32[]{:S(2)}) collective-permute-start(bf16[512,512]{1,0:T(8,128)(2,1)S(1)} %slice.339), channel_id=1, source_target_pairs={{0,1},{1,0},{2,3},{3,2},{4,5},{5,4},{6,7},{7,6},{8,9},{9,8},{10,11... | collective-permute-start | bytes 1572872 | tf_op jit(solution)/shard_map/ppermute | solution.py:438
  205.2 34.6 %collective-permute-start.12 = (bf16[512,512]{1,0:T(8,128)(2,1)S(1)}, bf16[512,512]{1,0:T(8,128)(2,1)}, u32[]{:S(2)}, u32[]{:S(2)}) collective-permute-start(bf16[512,512]{1,0:T(8,128)(2,1)S(1)} %slice.338), channel_id=1, source_target_pairs={{0,2},{1,3},{2,0},{3,1},{4,6},{5,7},{6,4},{7,5},{8,10},{9,11},{10,... | collective-permute-start | bytes 1572872 | tf_op jit(solution)/shard_map/ppermute | solution.py:438
  266.3 25.4 %collective-permute-start.14 = (bf16[2,512,512]{2,1,0:T(8,128)(2,1)S(1)}, bf16[2,512,512]{2,1,0:T(8,128)(2,1)S(1)}, u32[]{:S(2)}, u32[]{:S(2)}) collective-permute-start(bf16[2,512,512]{2,1,0:T(8,128)(2,1)S(1)} %pad_maximum_fusion.5), channel_id=1, source_target_pairs={{0,1},{1,0},{2,3},{3,2},{4,5},{5,4},{6,7},{7,6},{8,9},{9,8},{10,11... | collective-permute-start | bytes 3145736 | tf_op jit(solution)/shard_map/ppermute | solution.py:438
  267.9 25.0 %collective-permute-start.15 = (bf16[2,512,512]{2,1,0:T(8,128)(2,1)S(1)}, bf16[2,512,512]{2,1,0:T(8,128)(2,1)S(1)}, u32[]{:S(2)}, u32[]{:S(2)}) collective-permute-start(bf16[2,512,512]{2,1,0:T(8,128)(2,1)S(1)} %stack.68), channel_id=1, source_target_pairs={{0,2},{1,3},{2,0},{3,1},{4,6},{5,7},{6,4},{7,5},{8,10},{9,11},{10,... | collective-permute-start | bytes 3145736 | tf_op jit(solution)/shard_map/ppermute | solution.py:438
  293.3 13.0 %collective-permute-start.17 = (bf16[1,512,512]{2,1,0:T(8,128)(2,1)S(1)}, bf16[1,512,512]{2,1,0:T(8,128)(2,1)S(1)}, u32[]{:S(2)}, u32[]{:S(2)}) collective-permute-start(bf16[1,512,512]{2,1,0:T(8,128)(2,1)S(1)} %get-tuple-element.138), channel_id=1, source_target_pairs={{0,1},{1,0},{2,3},{3,2},{4,5},{5,4},{6,7},{7,6},{8,9},{9,8},{10,11... | collective-permute-start | bytes 1572872 | tf_op jit(solution)/shard_map/ppermute | solution.py:438
  293.9 12.8 %collective-permute-start.16 = (bf16[1,512,512]{2,1,0:T(8,128)(2,1)S(1)}, bf16[1,512,512]{2,1,0:T(8,128)(2,1)S(1)}, u32[]{:S(2)}, u32[]{:S(2)}) collective-permute-start(bf16[1,512,512]{2,1,0:T(8,128)(2,1)S(1)} %get-tuple-element.139), channel_id=1, source_target_pairs={{0,2},{1,3},{2,0},{3,1},{4,6},{5,7},{6,4},{7,5},{8,10},{9,11},{10,... | collective-permute-start | bytes 1572872 | tf_op jit(solution)/shard_map/ppermute | solution.py:438
  309.0 23.1 %collective-permute-start.19 = (bf16[1024,512]{1,0:T(8,128)(2,1)S(1)}, bf16[1024,512]{1,0:T(8,128)(2,1)S(1)}, u32[]{:S(2)}, u32[]{:S(2)}) collective-permute-start(bf16[1024,512]{1,0:T(8,128)(2,1)S(1)} %fusion.refs_0_), channel_id=1, source_target_pairs={{0,2},{1,3},{2,0},{3,1},{4,6},{5,7},{6,4},{7,5},{8,10},{9,11},{10,... | collective-permute-start | bytes 3145736 | tf_op jit(solution)/shard_map/ppermute | solution.py:438
  310.5 23.9 %collective-permute-start.18 = (bf16[1024,512]{1,0:T(8,128)(2,1)S(1)}, bf16[1024,512]{1,0:T(8,128)(2,1)S(1)}, u32[]{:S(2)}, u32[]{:S(2)}) collective-permute-start(bf16[1024,512]{1,0:T(8,128)(2,1)S(1)} %fusion.refs_0_), channel_id=1, source_target_pairs={{0,1},{1,0},{2,3},{3,2},{4,5},{5,4},{6,7},{7,6},{8,9},{9,8},{10,11... | collective-permute-start | bytes 3145736 | tf_op jit(solution)/shard_map/ppermute | solution.py:438
  333.1 11.5 %collective-permute-start.21 = (bf16[512,512]{1,0:T(8,128)(2,1)}, bf16[512,512]{1,0:T(8,128)(2,1)}, u32[]{:S(2)}, u32[]{:S(2)}) collective-permute-start(bf16[512,512]{1,0:T(8,128)(2,1)} %slice.347), channel_id=1, source_target_pairs={{0,1},{1,0},{2,3},{3,2},{4,5},{5,4},{6,7},{7,6},{8,9},{9,8},{10,11... | collective-permute-start | bytes 1572872 | tf_op jit(solution)/shard_map/ppermute | solution.py:438
  335.3 10.9 %collective-permute-start.20 = (bf16[512,512]{1,0:T(8,128)(2,1)}, bf16[512,512]{1,0:T(8,128)(2,1)}, u32[]{:S(2)}, u32[]{:S(2)}) collective-permute-start(bf16[512,512]{1,0:T(8,128)(2,1)} %slice.346), channel_id=1, source_target_pairs={{0,2},{1,3},{2,0},{3,1},{4,6},{5,7},{6,4},{7,5},{8,10},{9,11},{10,... | collective-permute-start | bytes 1572872 | tf_op jit(solution)/shard_map/ppermute | solution.py:438
  376.2 272.3 %reduce-scatter.3.cloned.1.call-start = ((), (), s32[]{:S(2)}) async-start(), calls=%async_computation.4 | async-start | bytes 16515072 | tf_op jit(solution)/shard_map/reduce_scatter | solution.py:931
  410.5 37.2 %collective-permute-start.22 = (bf16[2,1,512,512]{3,2,1,0:T(8,128)(2,1)S(1)}, bf16[2,1,512,512]{3,2,1,0:T(8,128)(2,1)S(1)}, u32[]{:S(2)}, u32[]{:S(2)}) collective-permute-start(bf16[2,1,512,512]{3,2,1,0:T(8,128)(2,1)S(1)} %pad_maximum_fusion.6), channel_id=1, source_target_pairs={{0,1},{1,0},{2,3},{3,2},{4,5},{5,4},{6,7},{7,6},{8,9},{9,8},{10,11... | collective-permute-start | bytes 3145736 | tf_op jit(solution)/shard_map/ppermute | solution.py:438
  411.5 36.2 %collective-permute-start.24 = (bf16[2,1,512,512]{3,2,1,0:T(8,128)(2,1)S(1)}, bf16[2,1,512,512]{3,2,1,0:T(8,128)(2,1)S(1)}, u32[]{:S(2)}, u32[]{:S(2)}) collective-permute-start(bf16[2,1,512,512]{3,2,1,0:T(8,128)(2,1)S(1)} %stack.69), channel_id=1, source_target_pairs={{0,2},{1,3},{2,0},{3,1},{4,6},{5,7},{6,4},{7,5},{8,10},{9,11},{10,... | collective-permute-start | bytes 3145736 | tf_op jit(solution)/shard_map/ppermute | solution.py:438
  430.5 69.8 %collective-permute-start.26 = (bf16[2,2,512,512]{3,2,1,0:T(8,128)(2,1)}, bf16[2,2,512,512]{3,2,1,0:T(8,128)(2,1)S(1)}, u32[]{:S(2)}, u32[]{:S(2)}) collective-permute-start(bf16[2,2,512,512]{3,2,1,0:T(8,128)(2,1)} %pad_maximum_fusion), channel_id=1, source_target_pairs={{0,1},{1,0},{2,3},{3,2},{4,5},{5,4},{6,7},{7,6},{8,9},{9,8},{10,11... | collective-permute-start | bytes 6291464 | tf_op jit(solution)/shard_map/ppermute | solution.py:438
  431.7 68.6 %collective-permute-start.27 = (bf16[2,2,512,512]{3,2,1,0:T(8,128)(2,1)}, bf16[2,2,512,512]{3,2,1,0:T(8,128)(2,1)}, u32[]{:S(2)}, u32[]{:S(2)}) collective-permute-start(bf16[2,2,512,512]{3,2,1,0:T(8,128)(2,1)} %stack.70), channel_id=1, source_target_pairs={{0,2},{1,3},{2,0},{3,1},{4,6},{5,7},{6,4},{7,5},{8,10},{9,11},{10,... | collective-permute-start | bytes 6291464 | tf_op jit(solution)/shard_map/ppermute | solution.py:438
  466.5 32.8 %collective-permute-start.28 = (bf16[2,512,512]{2,1,0:T(8,128)(2,1)}, bf16[2,512,512]{2,1,0:T(8,128)(2,1)}, u32[]{:S(2)}, u32[]{:S(2)}) collective-permute-start(bf16[2,512,512]{2,1,0:T(8,128)(2,1)} %pad_maximum_fusion.7), channel_id=1, source_target_pairs={{0,1},{1,0},{2,3},{3,2},{4,5},{5,4},{6,7},{7,6},{8,9},{9,8},{10,11... | collective-permute-start | bytes 3145736 | tf_op jit(solution)/shard_map/ppermute | solution.py:438
  467.3 33.0 %collective-permute-start.29 = (bf16[2,512,512]{2,1,0:T(8,128)(2,1)}, bf16[2,512,512]{2,1,0:T(8,128)(2,1)}, u32[]{:S(2)}, u32[]{:S(2)}) collective-permute-start(bf16[2,512,512]{2,1,0:T(8,128)(2,1)} %stack.71), channel_id=1, source_target_pairs={{0,2},{1,3},{2,0},{3,1},{4,6},{5,7},{6,4},{7,5},{8,10},{9,11},{10,... | collective-permute-start | bytes 3145736 | tf_op jit(solution)/shard_map/ppermute | solution.py:438
  502.0 15.0 %collective-permute-start.25 = (bf16[1,1,512,512]{3,2,1,0:T(8,128)(2,1)S(1)}, bf16[1,1,512,512]{3,2,1,0:T(8,128)(2,1)S(1)}, u32[]{:S(2)}, u32[]{:S(2)}) collective-permute-start(bf16[1,1,512,512]{3,2,1,0:T(8,128)(2,1)S(1)} %get-tuple-element.132), channel_id=1, source_target_pairs={{0,1},{1,0},{2,3},{3,2},{4,5},{5,4},{6,7},{7,6},{8,9},{9,8},{10,11... | collective-permute-start | bytes 1572872 | tf_op jit(solution)/shard_map/ppermute | solution.py:438
  506.9 44.1 %collective-permute-start.31 = (bf16[1,2,512,512]{3,2,1,0:T(8,128)(2,1)S(1)}, bf16[1,2,512,512]{3,2,1,0:T(8,128)(2,1)S(1)}, u32[]{:S(2)}, u32[]{:S(2)}) collective-permute-start(bf16[1,2,512,512]{3,2,1,0:T(8,128)(2,1)S(1)} %get-tuple-element.120), channel_id=1, source_target_pairs={{0,1},{1,0},{2,3},{3,2},{4,5},{5,4},{6,7},{7,6},{8,9},{9,8},{10,11... | collective-permute-start | bytes 3145736 | tf_op jit(solution)/shard_map/ppermute | solution.py:438
  507.1 43.9 %collective-permute-start.30 = (bf16[1,2,512,512]{3,2,1,0:T(8,128)(2,1)S(1)}, bf16[1,2,512,512]{3,2,1,0:T(8,128)(2,1)S(1)}, u32[]{:S(2)}, u32[]{:S(2)}) collective-permute-start(bf16[1,2,512,512]{3,2,1,0:T(8,128)(2,1)S(1)} %get-tuple-element.121), channel_id=1, source_target_pairs={{0,2},{1,3},{2,0},{3,1},{4,6},{5,7},{6,4},{7,5},{8,10},{9,11},{10,... | collective-permute-start | bytes 3145736 | tf_op jit(solution)/shard_map/ppermute | solution.py:438
  508.3 36.2 %collective-permute-start.23 = (bf16[1,1,512,512]{3,2,1,0:T(8,128)(2,1)S(1)}, bf16[1,1,512,512]{3,2,1,0:T(8,128)(2,1)S(1)}, u32[]{:S(2)}, u32[]{:S(2)}) collective-permute-start(bf16[1,1,512,512]{3,2,1,0:T(8,128)(2,1)S(1)} %get-tuple-element.133), channel_id=1, source_target_pairs={{0,2},{1,3},{2,0},{3,1},{4,6},{5,7},{6,4},{7,5},{8,10},{9,11},{10,... | collective-permute-start | bytes 1572872 | tf_op jit(solution)/shard_map/ppermute | solution.py:438
  509.5 4.4 collective-permute-start.35
  513.9 35.1 %collective-permute-start.33 = (bf16[1,512,512]{2,1,0:T(8,128)(2,1)S(1)}, bf16[1,512,512]{2,1,0:T(8,128)(2,1)S(1)}, u32[]{:S(2)}, u32[]{:S(2)}) collective-permute-start(bf16[1,512,512]{2,1,0:T(8,128)(2,1)S(1)} %get-tuple-element.128), channel_id=1, source_target_pairs={{0,1},{1,0},{2,3},{3,2},{4,5},{5,4},{6,7},{7,6},{8,9},{9,8},{10,11... | collective-permute-start | bytes 1572872 | tf_op jit(solution)/shard_map/ppermute | solution.py:438
  517.0 34.0 %collective-permute-start.32 = (bf16[1,512,512]{2,1,0:T(8,128)(2,1)S(1)}, bf16[1,512,512]{2,1,0:T(8,128)(2,1)S(1)}, u32[]{:S(2)}, u32[]{:S(2)}) collective-permute-start(bf16[1,512,512]{2,1,0:T(8,128)(2,1)S(1)} %get-tuple-element.129), channel_id=1, source_target_pairs={{0,2},{1,3},{2,0},{3,1},{4,6},{5,7},{6,4},{7,5},{8,10},{9,11},{10,... | collective-permute-start | bytes 1572872 | tf_op jit(solution)/shard_map/ppermute | solution.py:438
  544.5 41.8 %collective-permute-start.41 = (f32[48,1024]{1,0:T(8,128)S(1)}, f32[48,1024]{1,0:T(8,128)S(1)}, u32[]{:S(2)}, u32[]{:S(2)}) collective-permute-start(f32[48,1024]{1,0:T(8,128)S(1)} %copy-done.22), channel_id=1, source_target_pairs={{0,1},{1,0},{2,3},{3,2},{4,5},{5,4},{6,7},{7,6},{8,9},{9,8},{10,11... | collective-permute-start | bytes 589832 | tf_op jit(solution)/shard_map/ppermute | solution.py:438
  579.4 9.1 %collective-permute-start.36 = (f32[48,1024]{1,0:T(8,128)}, f32[48,1024]{1,0:T(8,128)S(1)}, u32[]{:S(2)}, u32[]{:S(2)}) collective-permute-start(f32[48,1024]{1,0:T(8,128)} %get-tuple-element.106), channel_id=1, source_target_pairs={{0,1},{1,0},{2,3},{3,2},{4,5},{5,4},{6,7},{7,6},{8,9},{9,8},{10,11... | collective-permute-start | bytes 589832 | tf_op jit(solution)/shard_map/ppermute | solution.py:438
  580.0 7.7 %collective-permute-start.37 = (f32[8,512]{1,0:T(8,128)}, f32[8,512]{1,0:T(8,128)S(1)}, u32[]{:S(2)}, u32[]{:S(2)}) collective-permute-start(f32[8,512]{1,0:T(8,128)} %get-tuple-element.107), channel_id=1, source_target_pairs={{0,4},{4,0},{8,12},{12,8},{16,20},{20,16},{24,28},{28,24},{1,5},{5... | collective-permute-start | bytes 49160 | tf_op jit(solution)/shard_map/ppermute | solution.py:438
  580.1 5.6 collective-permute-start.38
  586.3 7.8 %collective-permute-start.42 = (f32[48,1024]{1,0:T(8,128)S(1)}, f32[48,1024]{1,0:T(8,128)S(1)}, u32[]{:S(2)}, u32[]{:S(2)}) collective-permute-start(f32[48,1024]{1,0:T(8,128)S(1)} %add.281), channel_id=1, source_target_pairs={{0,2},{1,3},{2,0},{3,1},{4,6},{5,7},{6,4},{7,5},{8,10},{9,11},{10,... | collective-permute-start | bytes 589832 | tf_op jit(solution)/shard_map/ppermute | solution.py:438
  589.5 7.9 %collective-permute-start.39 = (f32[48,1024]{1,0:T(8,128)S(1)}, f32[48,1024]{1,0:T(8,128)S(1)}, u32[]{:S(2)}, u32[]{:S(2)}) collective-permute-start(f32[48,1024]{1,0:T(8,128)S(1)} %add.274), channel_id=1, source_target_pairs={{0,2},{1,3},{2,0},{3,1},{4,6},{5,7},{6,4},{7,5},{8,10},{9,11},{10,... | collective-permute-start | bytes 589832 | tf_op jit(solution)/shard_map/ppermute | solution.py:438
  590.2 4.4 collective-permute-start.40
  597.4 5.4 collective-permute-start.43
  602.8 4.3 collective-permute-start.44
  607.1 22.3 %collective-permute-start.45 = (f32[8,2048]{1,0:T(8,128)S(1)}, f32[8,2048]{1,0:T(8,128)S(1)}, u32[]{:S(2)}, u32[]{:S(2)}) collective-permute-start(f32[8,2048]{1,0:T(8,128)S(1)} %add_dynamic-update-slice_fusion), channel_id=1, source_target_pairs={{0,2},{1,3},{2,0},{3,1},{4,6},{5,7},{6,4},{7,5},{8,10},{9,11},{10,... | collective-permute-start | bytes 196616 | tf_op jit(solution)/shard_map/ppermute | solution.py:438
  (35 other events, 485.0 us)
Sparse Core Ops, SparseCore 0:
  10.2 137.1 all-gather.2
  149.0 97.8 all-gather.4
  376.3 108.5 reduce-scatter.4
  500.5 147.9 reduce-scatter.2
